TPU v7x, 128 devices: a whole 4x4x4 slice. The times are simulated.
128 devices in a mesh: skyx: 16 (over x, z), skyy: 8 (over y, core).
Axes of the slice: x: 4, y: 4, z: 4, core: 2. Of those that a mesh axis runs over, the one named last changes fastest.
Arguments:
- patches: float32 [8, 256, 128, 256], P('skyy', 'skyx'), may hold values from -8 to 8
- dest: int32 [8, 256, 1], P('skyy', 'skyx'), may hold values from 0 to 15; in each aligned block of 16 rows (0 to 15, 16 to 31, ..., all dimensions but the last counted through in order) at most 2 rows name the same one
- row_offset: int32 [8, 256], P('skyy', 'skyx'), may hold values from -128 to 512
- col_offset: int32 [8, 256], P('skyy', 'skyx'), may hold values from -128 to 384
- live_rows: int32 [8, 256], P('skyy', 'skyx'), may hold values from 32 to 128
- weight: float32 [8, 256], P('skyy', 'skyx'), may hold values from 0.2 to 2
- coefficient: float32 [8, 256, 8], P('skyy', 'skyx'), may hold values from -3 to 3
- basis: float32 [2, 8, 41], replicated, may hold values from -0.9 to 0.9
Outputs:
- coadd: float32 [4096, 8192], P('skyy', 'skyx')
- depth: float32 [4096, 8192], P('skyy', 'skyx')
Inputs may be any that keep to these rules, and one draw needn't show every extreme that they name: `dest`: among the 16 patches of a band k = m * 16 to (m + 1) * 16 - 1, for each m, no tile column is named more than 2 times.
All inputs are finite; a program needn't handle non-finite values.
Results may differ from a plain program's by a relative error of at most 0.0003.
Values sent between devices are 32-bit elements; how exact they have to be, the bound alone decides.
No kernel may reach another device: no remote copies, remote signals or barrier semaphores. Data moves between devices by JAX's collectives and lax.ppermute only.
A program may use at most 192 MiB of HBM per device.

v0:
```python
import jax
import jax.numpy as jnp
from jax import lax
from jax.sharding import PartitionSpec as P

TILE = 512
MARGIN = 128
CAP = 2


prior_weight = 0.5
highest = lax.Precision.HIGHEST


def shifted_2(block, axis, distance):
    devices = range(lax.axis_size(axis))
    route = [(i - distance, i) for i in devices if i - distance in devices]
    return lax.ppermute(block, axis, route)


def band_matrix(taps, size):
    tap_count = taps.shape[-1]
    positions = jnp.arange(size)
    offset_table = positions[:, None] - positions[None, :] + tap_count // 2
    onehot = (offset_table[:, :, None] == jnp.arange(tap_count)[None, None, :]).astype(jnp.float32)
    return jnp.einsum("act,bt->bac", onehot, taps, precision=highest)


def match_psf(images, coeffs, live_count, scales, row_band, col_band):
    row_index = jnp.arange(images.shape[1])
    row_mask = (row_index[None, :] < live_count[:, None]).astype(jnp.float32)[:, :, None]
    masked = images * row_mask
    across = jnp.einsum("kpj,bij->kbpi", masked, col_band, precision=highest)
    downward = jnp.einsum("bqp,kbpi->kbqi", row_band, across, precision=highest)
    matched = jnp.einsum("kb,kbqi->kqi", coeffs, downward, precision=highest)
    return matched * row_mask * scales[:, None, None]


def spill_columns(canvas):
    side_width = MARGIN
    interior = TILE
    from_west = shifted_2(canvas[:, :, interior + side_width :], "skyx", 1)
    from_east = shifted_2(canvas[:, :, :side_width], "skyx", -1)
    canvas = canvas.at[:, :, side_width : 2 * side_width].add(from_west)
    return canvas.at[:, :, interior : interior + side_width].add(from_east)


def spill_rows(canvas):
    side_width = MARGIN
    interior = TILE
    from_north = shifted_2(canvas[:, interior + side_width :, :], "skyy", 1)
    from_south = shifted_2(canvas[:, :side_width, :], "skyy", -1)
    canvas = canvas.at[:, side_width : 2 * side_width, :].add(from_north)
    return canvas.at[:, interior : interior + side_width, :].add(from_south)


def per_device(patches, dest, row_offset, col_offset, live_rows, weight, coefficient, basis):
    images = patches[0]
    count = images.shape[0]
    patch_rows = images.shape[1]
    patch_cols = images.shape[2]
    num_columns = lax.axis_size("skyx")
    slots_total = num_columns * CAP
    row_band = band_matrix(basis[0], patch_rows)
    col_band = band_matrix(basis[1], patch_cols)
    targets = dest[0, :, 0]
    order_index = jnp.arange(count)
    earlier = (targets[:, None] == targets[None, :]) & (order_index[:, None] > order_index[None, :])
    rank_within = jnp.sum(earlier.astype(jnp.int32), axis=1)
    slot_of = targets * CAP + rank_within
    select_int = (slot_of[None, :] == jnp.arange(slots_total)[:, None]).astype(jnp.int32)
    select = select_int.astype(jnp.float32)
    int_meta = jnp.stack([row_offset[0], col_offset[0], live_rows[0]], axis=1)
    sent_ints = jnp.sum(select_int[:, :, None] * int_meta[None, :, :], axis=1).reshape(
        num_columns, CAP, 3
    )
    float_meta = jnp.concatenate([coefficient[0], weight[0][:, None]], axis=1)
    meta_width = float_meta.shape[1]
    sent_floats = jnp.dot(select, float_meta, precision=highest).reshape(
        num_columns, CAP, meta_width
    )
    routed = jnp.einsum("sp,pij->sij", select, images, precision=highest)
    slot_data = lax.all_to_all(
        routed.reshape(num_columns, CAP, patch_rows, patch_cols),
        "skyx",
        split_axis=0,
        concat_axis=0,
        tiled=True,
    )
    slot_floats = lax.all_to_all(sent_floats, "skyx", split_axis=0, concat_axis=0, tiled=True)
    slot_ints = lax.all_to_all(sent_ints, "skyx", split_axis=0, concat_axis=0, tiled=True)
    basis_count = slot_floats.shape[2] - 1
    flat_floats = slot_floats.reshape(-1, basis_count + 1)
    flat_images = slot_data.reshape(-1, patch_rows, patch_cols)
    matched = match_psf(
        flat_images,
        flat_floats[:, :basis_count],
        slot_ints.reshape(-1, 3)[:, 2],
        flat_floats[:, basis_count],
        row_band,
        col_band,
    )
    arrived = matched.reshape(slot_data.shape)
    arrived_weight = slot_floats[:, :, basis_count:]
    flat_data = arrived.reshape(slots_total, patch_rows, patch_cols)
    flat_weight = arrived_weight.reshape(slots_total)
    flat_ints = slot_ints.reshape(slots_total, 3)
    side_total = TILE + 2 * MARGIN
    canvas_index = jnp.arange(side_total)
    tops = flat_ints[:, 0] + MARGIN
    lefts = flat_ints[:, 1] + MARGIN
    lives = flat_ints[:, 2]
    col_place = (
        canvas_index[None, None, :] == jnp.arange(patch_cols)[None, :, None] + lefts[:, None, None]
    ).astype(jnp.float32)
    shifted = jnp.einsum("spj,sjc->spc", flat_data, col_place, precision=highest)
    row_place = (
        canvas_index[:, None, None] == jnp.arange(patch_rows)[None, None, :] + tops[None, :, None]
    ).astype(jnp.float32)
    summed_canvas = jnp.dot(
        row_place.reshape(side_total, slots_total * patch_rows),
        shifted.reshape(slots_total * patch_rows, side_total),
        precision=highest,
    )
    rel_rows = canvas_index[:, None] - tops[None, :]
    row_cover = ((rel_rows >= 0) & (rel_rows < lives[None, :])).astype(jnp.float32) * flat_weight[
        None, :
    ]
    rel_cols = canvas_index[None, :] - lefts[:, None]
    col_cover = ((rel_cols >= 0) & (rel_cols < patch_cols)).astype(jnp.float32)
    plane_canvas = jnp.dot(row_cover, col_cover, precision=highest)
    canvas = jnp.stack([summed_canvas, plane_canvas])
    canvas = spill_rows(spill_columns(canvas))
    core = canvas[:, MARGIN : MARGIN + TILE, MARGIN : MARGIN + TILE]
    depth = core[1]
    coadd = core[0] / (depth + prior_weight)
    return (coadd, depth)


def solution(mesh):
    in_specs = (
        P("skyy", "skyx", None, None),
        P("skyy", "skyx", None),
        P("skyy", "skyx"),
        P("skyy", "skyx"),
        P("skyy", "skyx"),
        P("skyy", "skyx"),
        P("skyy", "skyx", None),
        P(),
    )
    out_specs = (P("skyy", "skyx"), P("skyy", "skyx"))
    return jax.shard_map(
        per_device, mesh=mesh, in_specs=in_specs, out_specs=out_specs, check_vma=False
    )
```

profile of v0, /device:TPU:107, one launch (start us, length us, event | category | flops | bytes accessed | tf_op | source)
XLA Modules:
  0.0 347.7 jit_solution(10758795862064687796)
XLA Ops:
  0.6 0.9 convert_reduce_fusion
  1.5 0.7 multiply_add_fusion.1
  2.3 0.7 pad_add_fusion
  3.1 0.7 copy.44
  3.8 6.4 %all-to-all-start = ((s32[16,2,3]{2,1,0:T(2,128)}), s32[16,2,3]{2,1,0:T(2,128)S(1)}, u32[]{:S(2)}, u32[]{:S(2)}) async-start(s32[16,2,3]{2,1,0:T(2,128)} %bitcast.4), calls=%async_computation | async-start | bytes 32768 | tf_op jit(solution)/shard_map/all_to_all | solution.py:91
  10.2 1.6 fusion.59
  11.8 2.3 all-to-all-done
  14.0 6.0 %all-to-all-start.1 = ((f32[16,2,9]{2,1,0:T(2,128)}), f32[16,2,9]{2,1,0:T(2,128)S(1)}, u32[]{:S(2)}, u32[]{:S(2)}) async-start(f32[16,2,9]{2,1,0:T(2,128)} %bitcast.9), calls=%async_computation.1 | async-start | bytes 32768 | tf_op jit(solution)/shard_map/all_to_all | solution.py:90
  20.0 5.8 %fusion.17 = f32[16,2,128,256]{3,0,2,1:T(8,128)S(1)} fusion(f32[16,128,256]{2,1,0:T(8,128)} %bitcast.75, s32[16,2]{0,1:T(2,128)S(1)} %multiply_add_fusion, s32[16]{0:T(128)S(1)} %multiply_add_fusion.1), kind=kOutput, calls=%fused_computation.28 | convolution fusion | flops 201328128 | bytes 6291648 | tf_op jit(solution)/shard_map/sp,pij->sij/dot_general | solution.py:82
  25.8 4.4 %copy.34 = f32[16,2,128,256]{3,2,1,0:T(8,128)} copy(f32[16,2,128,256]{3,0,2,1:T(8,128)S(1)} %fusion.17) | data formatting | bytes 8388608 | tf_op jit(solution)/shard_map/sp,pij->sij/dot_general | solution.py:82
  30.2 7.5 %all-to-all-start.2 = ((f32[16,2,128,256]{3,2,1,0:T(8,128)}), f32[16,2,128,256]{3,2,1,0:T(8,128)}, u32[]{:S(2)}, u32[]{:S(2)}) async-start(f32[16,2,128,256]{3,2,1,0:T(8,128)} %copy.34), calls=%async_computation.2 | async-start | bytes 8388608 | tf_op jit(solution)/shard_map/all_to_all | solution.py:83
  37.8 1.2 fusion.24
  39.0 5.7 %fusion.8 = f32[256,256,8]{1,2,0:T(8,128)} fusion(s32[256,256]{1,0:T(8,128)S(1)} %subtract_add_fusion, f32[2,8,41]{2,1,0:T(8,128)S(1)} %copy-done.1), kind=kOutput, calls=%fused_computation.10 | convolution fusion | flops 260636672 | bytes 2363392 | tf_op jit(solution)/shard_map/act,bt->bac/dot_general | solution.py:26
  45.6 1.2 convolution_bitcast_fusion.1
  46.8 42.2 %all-to-all-done.2 = f32[16,2,128,256]{3,2,1,0:T(8,128)} async-done(((f32[16,2,128,256]{3,2,1,0:T(8,128)}), f32[16,2,128,256]{3,2,1,0:T(8,128)}, u32[]{:S(2)}, u32[]{:S(2)}) %all-to-all-start.2) | async-done | bytes 4194336 | tf_op jit(solution)/shard_map/all_to_all | solution.py:83
  89.0 2.7 bitcast_multiply_fusion.1
  91.8 30.8 %convolution_bitcast_fusion = f32[32,8,128,256]{2,1,0,3:T(8,128)} fusion(f32[32,128,256]{2,1,0:T(8,128)S(1)} %bitcast_multiply_fusion.1, f32[256,256,8]{1,2,0:T(8,128)S(1)} %copy-done), kind=kOutput, calls=%fused_computation.5 | convolution fusion | flops 25769803776 | bytes 39845888 | tf_op jit(solution)/shard_map/kpj,bij->kbpi/dot_general | solution.py:33
  122.7 55.6 %fusion.3 = f32[32,8,128,256]{2,3,0,1:T(8,128)} fusion(f32[32,8,128,256]{2,1,0,3:T(8,128)} %convolution_bitcast_fusion, f32[8,128,128,1]{2,0,1,3:T(8,128)S(1)} %fusion.24), kind=kOutput, calls=%fused_computation.4 | convolution fusion | flops 12884901888 | bytes 67633152 | tf_op jit(solution)/shard_map/bqp,kbpi->kbqi/dot_general | solution.py:34
  178.3 33.5 %copy.42 = f32[32,8,128,256]{3,1,2,0:T(8,128)} copy(f32[32,8,128,256]{2,3,0,1:T(8,128)} %fusion.3) | data formatting | bytes 67108864 | tf_op jit(solution)/shard_map/bqp,kbpi->kbqi/transpose | solution.py:34
  211.7 33.9 %fusion.78 = f32[32,1,128,256]{3,1,2,0:T(1,128)S(1)} fusion(f32[32,8,1,1]{1,2,3,0:T(1,128)S(1)} %bitcast.77, f32[32,8,128,256]{3,1,2,0:T(8,128)} %copy.42), kind=kOutput, calls=%fused_computation.108 | convolution fusion | flops 100663296 | bytes 37749760 | tf_op jit(solution)/shard_map/kb,kbqi->kqi/dot_general | solution.py:35
  245.6 12.5 %fusion.2 = f32[32,128,768]{2,1,0:T(8,128)S(1)} fusion(s32[32,256]{1,0:T(8,128)S(1)} %iota_add_fusion, f32[32,1,128,256]{3,1,2,0:T(1,128)S(1)} %fusion.78, f32[32]{0:T(128)S(1)} %slice_reduce_fusion.1, f32[32,128]{1,0:T(8,128)S(1)} %fusion.57), kind=kOutput, calls=%fused_computation.3 | convolution fusion | flops 9672065024 | bytes 16826496 | tf_op jit(solution)/shard_map/spj,sjc->spc/dot_general | solution.py:116
  258.1 16.9 %fusion.22 = f32[1,768,768]{2,1,0:T(8,128)S(1)} fusion(f32[32,128,768]{2,1,0:T(8,128)S(1)} %fusion.2, s32[32,128]{1,0:T(8,128)S(1)} %iota_add_fusion.1), kind=kOutput, calls=%fused_computation.34 | convolution fusion | flops 28994174976 | bytes 14958592 | tf_op jit(solution)/shard_map/dot_general | solution.py:120
  275.1 1.9 collective-permute-start
  277.0 0.3 pad_maximum_fusion
  277.4 17.5 %collective-permute-done = f32[2,768,128]{2,1,0:T(8,128)S(1)} collective-permute-done((f32[2,768,128]{2,1,0:T(8,128)S(1)}, f32[2,768,128]{2,1,0:T(8,128)S(1)}, u32[]{:S(2)}, u32[]{:S(2)}) %collective-permute-start) | collective-permute-done | bytes 786464 | tf_op jit(solution)/shard_map/ppermute | solution.py:18
  295.0 2.0 collective-permute-start.1
  297.0 18.9 %collective-permute-done.1 = f32[2,768,128]{2,1,0:T(8,128)S(1)} collective-permute-done((f32[2,768,128]{2,1,0:T(8,128)S(1)}, f32[2,768,128]{2,1,0:T(8,128)S(1)}, u32[]{:S(2)}, u32[]{:S(2)}) %collective-permute-start.1) | collective-permute-done | bytes 786464 | tf_op jit(solution)/shard_map/ppermute | solution.py:18
  316.1 6.2 %collective-permute-start.2 = (f32[2,128,768]{2,1,0:T(8,128)S(1)}, f32[2,128,768]{2,1,0:T(8,128)S(1)}, u32[]{:S(2)}, u32[]{:S(2)}) collective-permute-start(f32[2,128,768]{2,1,0:T(8,128)S(1)} %slice.177), channel_id=1, source_target_pairs={{0,1},{1,2},{2,3},{3,4},{4,5},{5,6},{6,7},{8,9},{9,10},{10,11},{11... | collective-permute-start | bytes 2359304 | tf_op jit(solution)/shard_map/ppermute | solution.py:18
  322.3 8.9 %collective-permute-done.2 = f32[2,128,768]{2,1,0:T(8,128)S(1)} collective-permute-done((f32[2,128,768]{2,1,0:T(8,128)S(1)}, f32[2,128,768]{2,1,0:T(8,128)S(1)}, u32[]{:S(2)}, u32[]{:S(2)}) %collective-permute-start.2) | collective-permute-done | bytes 786464 | tf_op jit(solution)/shard_map/ppermute | solution.py:18
  331.5 3.2 collective-permute-start.3
  334.7 10.9 %collective-permute-done.3 = f32[2,128,768]{2,1,0:T(8,128)S(1)} collective-permute-done((f32[2,128,768]{2,1,0:T(8,128)S(1)}, f32[2,128,768]{2,1,0:T(8,128)S(1)}, u32[]{:S(2)}, u32[]{:S(2)}) %collective-permute-start.3) | collective-permute-done | bytes 786464 | tf_op jit(solution)/shard_map/ppermute | solution.py:18
  345.8 1.5 fusion.25
  (26 shorter events, 2.2 us)
Async XLA Ops:
  3.8 10.3 %all-to-all-start = ((s32[16,2,3]{2,1,0:T(2,128)}), s32[16,2,3]{2,1,0:T(2,128)S(1)}, u32[]{:S(2)}, u32[]{:S(2)}) async-start(s32[16,2,3]{2,1,0:T(2,128)} %bitcast.4), calls=%async_computation | async-start | bytes 32768 | tf_op jit(solution)/shard_map/all_to_all | solution.py:91
  14.0 16.2 %all-to-all-start.1 = ((f32[16,2,9]{2,1,0:T(2,128)}), f32[16,2,9]{2,1,0:T(2,128)S(1)}, u32[]{:S(2)}, u32[]{:S(2)}) async-start(f32[16,2,9]{2,1,0:T(2,128)} %bitcast.9), calls=%async_computation.1 | async-start | bytes 32768 | tf_op jit(solution)/shard_map/all_to_all | solution.py:90
  30.2 7.6 %copy-start.1 = (f32[2,8,41]{2,1,0:T(8,128)S(1)}, f32[2,8,41]{2,1,0:T(8,128)}, u32[]{:S(2)}) copy-start(f32[2,8,41]{2,1,0:T(8,128)} %param.23) | copy-start | bytes 7876
  30.2 58.7 %all-to-all-start.2 = ((f32[16,2,128,256]{3,2,1,0:T(8,128)}), f32[16,2,128,256]{3,2,1,0:T(8,128)}, u32[]{:S(2)}, u32[]{:S(2)}) async-start(f32[16,2,128,256]{3,2,1,0:T(8,128)} %copy.34), calls=%async_computation.2 | async-start | bytes 8388608 | tf_op jit(solution)/shard_map/all_to_all | solution.py:83
  89.0 2.9 copy-start
  275.1 19.7 %collective-permute-start = (f32[2,768,128]{2,1,0:T(8,128)S(1)}, f32[2,768,128]{2,1,0:T(8,128)S(1)}, u32[]{:S(2)}, u32[]{:S(2)}) collective-permute-start(f32[2,768,128]{2,1,0:T(8,128)S(1)} %fusion.29), channel_id=1, source_target_pairs={{0,8},{8,16},{16,24},{24,32},{32,40},{40,48},{48,56},{56,64},{64,7... | collective-permute-start | bytes 2359304 | tf_op jit(solution)/shard_map/ppermute | solution.py:18
  295.0 20.9 %collective-permute-start.1 = (f32[2,768,128]{2,1,0:T(8,128)S(1)}, f32[2,768,128]{2,1,0:T(8,128)S(1)}, u32[]{:S(2)}, u32[]{:S(2)}) collective-permute-start(f32[2,768,128]{2,1,0:T(8,128)S(1)} %get-tuple-element.54), channel_id=1, source_target_pairs={{8,0},{16,8},{24,16},{32,24},{40,32},{48,40},{56,48},{64,56},{72,6... | collective-permute-start | bytes 2359304 | tf_op jit(solution)/shard_map/ppermute | solution.py:18
  316.1 15.1 %collective-permute-start.2 = (f32[2,128,768]{2,1,0:T(8,128)S(1)}, f32[2,128,768]{2,1,0:T(8,128)S(1)}, u32[]{:S(2)}, u32[]{:S(2)}) collective-permute-start(f32[2,128,768]{2,1,0:T(8,128)S(1)} %slice.177), channel_id=1, source_target_pairs={{0,1},{1,2},{2,3},{3,4},{4,5},{5,6},{6,7},{8,9},{9,10},{10,11},{11... | collective-permute-start | bytes 2359304 | tf_op jit(solution)/shard_map/ppermute | solution.py:18
  331.5 14.1 %collective-permute-start.3 = (f32[2,128,768]{2,1,0:T(8,128)S(1)}, f32[2,128,768]{2,1,0:T(8,128)S(1)}, u32[]{:S(2)}, u32[]{:S(2)}) collective-permute-start(f32[2,128,768]{2,1,0:T(8,128)S(1)} %get-tuple-element.52), channel_id=1, source_target_pairs={{1,0},{2,1},{3,2},{4,3},{5,4},{6,5},{7,6},{9,8},{10,9},{11,10},{12... | collective-permute-start | bytes 2359304 | tf_op jit(solution)/shard_map/ppermute | solution.py:18
where the time goes:
time: 355 us; the launch traced here: 348 us
  matrix products  165 us (46%)
  waiting for transfers between devices  101 us (28%)
  local copies, waits for them, and re-layouts  39.4 us (11%)
  starting transfers between devices  33.2 us (9%)
  other arithmetic  8.15 us (2%)
    ppermute x4, waiting for transfers between devices, shifted_2(): return lax.ppermute(block, axis, route)  56.1 us
    dot_general x1, matrix products, match_psf(): downward = jnp.einsum('bqp,kbpi->kbqi', row_band, across, precision=highest)  55.6 us
    all_to_all x1, waiting for transfers between devices, per_device(): lax.all_to_all(routed.reshape(num_columns, CAP, patch_rows, patch_cols),...  42.2 us
    dot_general x1, matrix products, match_psf(): matched = jnp.einsum('kb,kbqi->kqi', coeffs, downward, precision=highest)  33.9 us
    transpose x1, local copies, waits for them, and re-layouts, match_psf(): downward = jnp.einsum('bqp,kbpi->kbqi', row_band, across, precision=highest)  33.5 us
    dot_general x1, matrix products, match_psf(): across = jnp.einsum('kpj,bij->kbpi', masked, col_band, precision=highest)  30.8 us
    dot_general x1, matrix products, per_device(): jnp.dot(row_place.reshape(side_total, slots_total * patch_rows), shifted....  16.9 us
    ppermute x4, starting transfers between devices, shifted_2(): return lax.ppermute(block, axis, route)  13.3 us
  transfers between devices with their start and end apart: 7, of which 6 were waited for; matrix products, arithmetic and copies ran while one was open for 6% of the time, Pallas kernels for 0%

commit v1 on v0

v1 whole, which is shorter than its diff:
```python
import jax
import jax.numpy as jnp
from jax import lax
from jax.experimental import pallas as pl
from jax.experimental.pallas import tpu as pltpu
from jax.sharding import PartitionSpec as P

TILE = 512
MARGIN = 128
CAP = 2
PH = 128
PW = 256
NB = 8
TAPS = 41
HALF = TAPS // 2
SIDE = TILE + 2 * MARGIN
CANVAS_ROWS = SIDE + 8
CANVAS_COLS = SIDE + 128
META = 8
VMEM_LIMIT = 48 * 1024 * 1024

prior_weight = 0.5
f32 = jnp.float32
bf16 = jnp.bfloat16
i32 = jnp.int32


def whole(shape):
    return pl.BlockSpec(shape, lambda *_: (0,) * len(shape))


smem = pl.BlockSpec(memory_space=pltpu.SMEM)
vmem = pl.BlockSpec(memory_space=pltpu.VMEM)
anywhere = pl.BlockSpec(memory_space=pl.ANY)


def split(x):
    high = x.astype(bf16)
    return high, (x - high.astype(f32)).astype(bf16)


def bands_kernel(basis, down_high, down_low, across_high, across_low):
    for b in range(NB):
        taps = jnp.broadcast_to(basis[1, b : b + 1, :], (PW, PW + 128))
        table = pltpu.roll(taps, 0, 1, stride=1, stride_axis=0)[:, :PW]
        high, low = split(table)
        across_high[b * PW : (b + 1) * PW, :] = high
        across_low[b * PW : (b + 1) * PW, :] = low
        taps = jnp.broadcast_to(basis[0, b : b + 1, :], (PH, PW + 128))
        table = pltpu.roll(taps, 0, 1, stride=1, stride_axis=0)[:, :PH]
        high, low = split(table)
        down_high[b * PH : (b + 1) * PH, :PH] = high
        down_high[b * PH : (b + 1) * PH, PH:] = high
        down_low[b * PH : (b + 1) * PH, :] = low


def make_bands(basis):
    vertical = basis[0][:, ::-1]
    taps = jnp.stack([vertical, basis[1]])
    gap = jnp.zeros((2, NB, PW + 128 - TAPS), f32)
    padded = jnp.concatenate([taps[:, :, HALF:], gap, taps[:, :, :HALF]], axis=2)
    return pl.pallas_call(
        bands_kernel,
        out_shape=(
            jax.ShapeDtypeStruct((NB * PH, 2 * PH), bf16),
            jax.ShapeDtypeStruct((NB * PH, PH), bf16),
            jax.ShapeDtypeStruct((NB * PW, PW), bf16),
            jax.ShapeDtypeStruct((NB * PW, PW), bf16),
        ),
        in_specs=[vmem],
        out_specs=(vmem,) * 4,
        compiler_params=pltpu.CompilerParams(vmem_limit_bytes=VMEM_LIMIT),
        name="bands",
    )(padded)


def pack_kernel(
    dest, row_offset, col_offset, live, weight, coefs, dest_v, row_v, col_v, live_v, weight_v, patches, out, second,
    slots, meta, patch_sems, meta_sem,
):
    count = patches.shape[0]
    tiles = out.shape[0]

    def clear(t, carry):
        slots[0, t] = -1
        slots[1, t] = -1
        return carry

    lax.fori_loop(0, tiles, clear, 0)

    def assign(k, carry):
        t = dest[0, k]
        rank = jnp.where(slots[0, t] >= 0, 1, 0)
        slots[rank, t] = k
        return carry

    lax.fori_loop(0, count, assign, 0)

    def send(t, carry):
        k = slots[0, t]

        @pl.when(k >= 0)
        def _():
            pltpu.make_async_copy(patches.at[k], out.at[t, pl.ds(0, PH)], patch_sems.at[t]).start()

        return carry

    lax.fori_loop(0, tiles, send, 0)

    def list_second(t, n):
        k = slots[1, t]

        @pl.when(k >= 0)
        def _():
            second[0, n] = k
            second[1, n] = t

        return n + jnp.where(k >= 0, 1, 0)

    def fill(j, carry):
        second[0, j] = 0
        second[1, j] = 0
        return carry

    lax.fori_loop(0, tiles, fill, 0)
    n_second = lax.fori_loop(0, tiles, list_second, 0)

    def repeat_last(j, carry):
        last = jnp.maximum(n_second - 1, 0)

        @pl.when(j >= n_second)
        def _():
            second[0, j] = second[0, last]
            second[1, j] = second[1, last]

        return carry

    lax.fori_loop(0, tiles, repeat_last, 0)
    second[2, 0] = n_second

    lane = lax.broadcasted_iota(i32, (1, 128), 1)
    base = jnp.zeros((META, PW), f32)
    meta[...] = jnp.broadcast_to(base[None], meta.shape)
    for row, values in enumerate((dest_v, row_v, col_v, live_v, weight_v)):
        line = values[...].astype(f32)
        for t in range(tiles):
            meta[t, row : row + 1, 0:count] = line

    def describe(t, carry):
        first = slots[0, t]
        k = jnp.maximum(first, 0)
        meta[t, 5:6, 0:NB] = coefs[pl.ds(k, 1), :] * weight[0, k]
        late = slots[1, t]
        j = jnp.maximum(late, 0)
        numbers = (
            jnp.where(first >= 0, 1, 0), row_offset[0, k], col_offset[0, k], live[0, k],
            jnp.where(late >= 0, 1, 0), row_offset[0, j], col_offset[0, j], live[0, j],
        )
        line = jnp.zeros((1, 128), i32)
        for place, number in enumerate(numbers):
            line = jnp.where(lane == place, number, line)
        meta[t, 6:7, 0:128] = line.astype(f32)
        return carry

    lax.fori_loop(0, tiles, describe, 0)
    about = pltpu.make_async_copy(meta, out.at[:, pl.ds(PH, META)], meta_sem)
    about.start()
    about.wait()

    def finish(t, carry):
        k = slots[0, t]

        @pl.when(k >= 0)
        def _():
            pltpu.make_async_copy(patches.at[k], out.at[t, pl.ds(0, PH)], patch_sems.at[t]).wait()

        return carry

    lax.fori_loop(0, tiles, finish, 0)


def pack(patches, dest, row_offset, col_offset, live_rows, weight, coefficient, tiles):
    return pl.pallas_call(
        pack_kernel,
        out_shape=(
            jax.ShapeDtypeStruct((tiles, PH + META, PW), f32),
            jax.ShapeDtypeStruct((3, tiles), i32),
        ),
        in_specs=[smem] * 5 + [vmem] * 6 + [anywhere],
        out_specs=(anywhere, smem),
        scratch_shapes=[
            pltpu.SMEM((CAP, tiles), i32),
            pltpu.VMEM((tiles, META, PW), f32),
            pltpu.SemaphoreType.DMA((tiles,)),
            pltpu.SemaphoreType.DMA,
        ],
        compiler_params=pltpu.CompilerParams(vmem_limit_bytes=VMEM_LIMIT),
        name="pack",
    )(
        dest, row_offset, col_offset, live_rows, weight, coefficient,
        dest, row_offset, col_offset, live_rows, weight, patches,
    )


def match(image, coefs, down_high, down_low, across_high, across_low, terms):
    high, low = split(image)
    both = jnp.concatenate([high, low], axis=0)
    downward = jnp.dot(down_high[...], both, preferred_element_type=f32)
    downward += jnp.dot(down_low[...], high, preferred_element_type=f32)
    for b in range(NB):
        high, low = split(downward[b * PH : (b + 1) * PH] * coefs[b])
        terms[:PH, b * PW : (b + 1) * PW] = high
        terms[PH:, b * PW : (b + 1) * PW] = low
    wide = jnp.dot(terms[...], across_high[...], preferred_element_type=f32)
    fine = jnp.dot(terms[:PH], across_low[...], preferred_element_type=f32)
    return wide[:PH] + wide[PH:] + fine


def live_mask(live):
    return lax.broadcasted_iota(i32, (PH, PW), 0) < live


def second_kernel(second, coefs, live, weight, patch, down_high, down_low, across_high, across_low, out, terms):
    j = pl.program_id(0)

    @pl.when(j < second[2, 0])
    def _():
        k = second[0, j]
        mask = live_mask(live[0, k])
        scaled = [coefs[k, b] * weight[0, k] for b in range(NB)]
        image = jnp.where(mask, patch[0], 0.0)
        matched = match(image, scaled, down_high, down_low, across_high, across_low, terms)
        out[0] = jnp.where(mask, matched, 0.0)


BAND_SHAPES = ((NB * PH, 2 * PH), (NB * PH, PH), (NB * PW, PW), (NB * PW, PW))


def match_second(second, coefficient, live_rows, weight, patches, bands, tiles):
    steps = patches.shape[0] // CAP
    return pl.pallas_call(
        second_kernel,
        out_shape=jax.ShapeDtypeStruct((tiles, PH, PW), f32),
        grid_spec=pltpu.PrefetchScalarGridSpec(
            num_scalar_prefetch=1,
            grid=(steps,),
            in_specs=[smem] * 3
            + [pl.BlockSpec((1, PH, PW), lambda j, second: (second[0, j], 0, 0))]
            + [whole(s) for s in BAND_SHAPES],
            out_specs=pl.BlockSpec((1, PH, PW), lambda j, second: (second[1, j], 0, 0)),
            scratch_shapes=[pltpu.VMEM((2 * PH, NB * PW), bf16)],
        ),
        compiler_params=pltpu.CompilerParams(vmem_limit_bytes=VMEM_LIMIT),
        cost_estimate=pl.CostEstimate(flops=5_000_000_000, bytes_accessed=6_000_000, transcendentals=0),
        name="match_second",
    )(second, coefficient, live_rows, weight, patches, *bands)


def place(canvas, piece, top, left):
    down = top % 8
    right = left % 128
    row = pl.multiple_of(top - down, 8)
    col = pl.multiple_of(left - right, 128)
    piece = jnp.concatenate([piece, jnp.zeros((8, PW), f32)], axis=0)
    piece = pltpu.roll(piece, down, 0)
    lane = lax.broadcasted_iota(i32, (PH + 8, 128), 1)
    near = pltpu.roll(piece[:, :128], right, 1)
    far = pltpu.roll(piece[:, 128:], right, 1)
    inside = lane >= right
    shifted = jnp.concatenate(
        [jnp.where(inside, near, 0.0), jnp.where(inside, far, near), jnp.where(inside, 0.0, far)], axis=1
    )
    canvas[pl.ds(row, PH + 8), pl.ds(col, PW + 128)] += shifted


def first_kernel(numbers, coefs, slot, down_high, down_low, across_high, across_low, canvas, terms):
    s = pl.program_id(0)

    @pl.when(s == 0)
    def _():
        canvas[...] = jnp.zeros_like(canvas)

    @pl.when(numbers[s, 0] > 0)
    def _():
        mask = live_mask(numbers[s, 3])
        image = jnp.where(mask, slot[0, :PH, :], 0.0)
        scaled = [coefs[s, b] for b in range(NB)]
        matched = match(image, scaled, down_high, down_low, across_high, across_low, terms)
        place(canvas, jnp.where(mask, matched, 0.0), numbers[s, 1] + MARGIN, numbers[s, 2] + MARGIN)


def match_first(numbers, coefs, slots, bands):
    tiles = slots.shape[0]
    return pl.pallas_call(
        first_kernel,
        out_shape=jax.ShapeDtypeStruct((CANVAS_ROWS, CANVAS_COLS), f32),
        grid=(tiles,),
        in_specs=[smem] * 2
        + [pl.BlockSpec((1, PH + META, PW), lambda s: (s, 0, 0))]
        + [whole(s) for s in BAND_SHAPES],
        out_specs=whole((CANVAS_ROWS, CANVAS_COLS)),
        scratch_shapes=[pltpu.VMEM((2 * PH, NB * PW), bf16)],
        compiler_params=pltpu.CompilerParams(vmem_limit_bytes=VMEM_LIMIT),
        cost_estimate=pl.CostEstimate(flops=10_000_000_000, bytes_accessed=8_000_000, transcendentals=0),
        name="match_first",
    )(numbers, coefs, slots, *bands)


def second_place_kernel(numbers, start, slot, north, south, middle, canvas):
    s = pl.program_id(0)

    @pl.when(s == 0)
    def _():
        canvas[...] = start[...]

    @pl.when(numbers[s, 4] > 0)
    def _():
        place(canvas, slot[0], numbers[s, 5] + MARGIN, numbers[s, 6] + MARGIN)

    @pl.when(s == pl.num_programs(0) - 1)
    def _():
        north[...] = canvas[:MARGIN, :SIDE]
        south[...] = canvas[MARGIN + TILE : SIDE, :SIDE]
        middle[...] = canvas[MARGIN : MARGIN + TILE, :SIDE]


def place_second(numbers, canvas, slots):
    tiles = slots.shape[0]
    strip = (MARGIN, SIDE)
    return pl.pallas_call(
        second_place_kernel,
        out_shape=(
            jax.ShapeDtypeStruct(strip, f32),
            jax.ShapeDtypeStruct(strip, f32),
            jax.ShapeDtypeStruct((TILE, SIDE), f32),
        ),
        grid=(tiles,),
        in_specs=[smem, whole((CANVAS_ROWS, CANVAS_COLS)), pl.BlockSpec((1, PH, PW), lambda s: (s, 0, 0))],
        out_specs=(whole(strip), whole(strip), whole((TILE, SIDE))),
        scratch_shapes=[pltpu.VMEM((CANVAS_ROWS, CANVAS_COLS), f32)],
        compiler_params=pltpu.CompilerParams(vmem_limit_bytes=VMEM_LIMIT),
        name="place_second",
    )(numbers, canvas, slots)


def depth_kernel(own, above, below, depth):
    total = jnp.zeros((TILE, TILE), f32)
    for about, step in ((own, 0), (above, -TILE), (below, TILE)):
        count = about.shape[1]
        place_at = lax.broadcasted_iota(i32, (TILE, count), 0).astype(f32)
        from_top = place_at - (about[0:1, :] + step)
        rows = jnp.where((from_top >= 0) & (from_top < about[2:3, :]), about[3:4, :], 0.0)
        from_left = place_at - about[1:2, :]
        cols = jnp.where((from_left >= 0) & (from_left < PW), 1.0, 0.0).astype(bf16)
        for part in split(rows):
            total += lax.dot_general(part, cols, (((1,), (1,)), ((), ())), preferred_element_type=f32)
    depth[...] = total


def make_depth(own, above, below):
    return pl.pallas_call(
        depth_kernel,
        out_shape=jax.ShapeDtypeStruct((TILE, TILE), f32),
        in_specs=[vmem] * 3,
        out_specs=vmem,
        compiler_params=pltpu.CompilerParams(vmem_limit_bytes=VMEM_LIMIT),
        cost_estimate=pl.CostEstimate(flops=1_000_000_000, bytes_accessed=1_000_000, transcendentals=0),
        name="make_depth",
    )(own, above, below)


def shifted(block, axis, distance):
    devices = range(lax.axis_size(axis))
    return lax.ppermute(block, axis, [(i - distance, i) for i in devices if i - distance in devices])


def edges_kernel(middle, from_above, from_below, west, east):
    low = TILE - MARGIN
    for out, cols in ((west, slice(0, MARGIN)), (east, slice(MARGIN + TILE, SIDE))):
        out[:MARGIN] = middle[:MARGIN, cols] + from_above[:, cols]
        out[MARGIN:low] = middle[MARGIN:low, cols]
        out[low:] = middle[low:, cols] + from_below[:, cols]


def make_edges(middle, from_above, from_below):
    edge = jax.ShapeDtypeStruct((TILE, MARGIN), f32)
    return pl.pallas_call(
        edges_kernel,
        out_shape=(edge, edge),
        in_specs=[vmem] * 3,
        out_specs=(vmem, vmem),
        compiler_params=pltpu.CompilerParams(vmem_limit_bytes=VMEM_LIMIT),
        name="make_edges",
    )(middle, from_above, from_below)


def final_kernel(middle, from_above, from_below, from_west, from_east, depth, coadd):
    core = slice(MARGIN, MARGIN + TILE)
    low = TILE - MARGIN
    coadd[...] = middle[:, core]
    coadd[:MARGIN] += from_above[:, core]
    coadd[low:] += from_below[:, core]
    coadd[:, :MARGIN] += from_west[...]
    coadd[:, low:] += from_east[...]
    coadd[...] = coadd[...] / (depth[...] + prior_weight)


def make_coadd(*parts):
    return pl.pallas_call(
        final_kernel,
        out_shape=jax.ShapeDtypeStruct((TILE, TILE), f32),
        in_specs=[vmem] * 6,
        out_specs=vmem,
        compiler_params=pltpu.CompilerParams(vmem_limit_bytes=VMEM_LIMIT),
        name="make_coadd",
    )(*parts)


def per_device(patches, dest, row_offset, col_offset, live_rows, weight, coefficient, basis):
    tiles = lax.axis_size("skyx")
    images = patches[0]
    outgoing, second = pack(
        images, dest[:, :, 0], row_offset, col_offset, live_rows, weight, coefficient[0], tiles
    )
    arrived = lax.all_to_all(outgoing, "skyx", split_axis=0, concat_axis=0, tiled=True)
    bands = make_bands(basis)
    late = match_second(second, coefficient[0], live_rows, weight, images, bands, tiles)
    late = lax.all_to_all(late, "skyx", split_axis=0, concat_axis=0, tiled=True)

    about = arrived[:, PH:, :128]
    numbers = about[:, 6, :16].astype(i32)
    coefs = about[:, 5, :NB]
    canvas = match_first(numbers, coefs, arrived, bands)

    band = jnp.transpose(about[:, :5, : images.shape[0]], (1, 0, 2)).reshape(5, -1)
    left = band[2] + (band[0] - lax.axis_index("skyx").astype(f32)) * TILE
    own = jnp.pad(jnp.stack([band[1], left, band[3], band[4]]), ((0, 4), (0, 0)))
    depth = make_depth(own, shifted(own, "skyy", 1), shifted(own, "skyy", -1))

    north, south, middle = place_second(numbers, canvas, late)
    from_above = shifted(south, "skyy", 1)
    from_below = shifted(north, "skyy", -1)
    west, east = make_edges(middle, from_above, from_below)
    from_west = shifted(east, "skyx", 1)
    from_east = shifted(west, "skyx", -1)
    coadd = make_coadd(middle, from_above, from_below, from_west, from_east, depth)
    return (coadd, depth)


def solution(mesh):
    in_specs = (
        P("skyy", "skyx", None, None),
        P("skyy", "skyx", None),
        P("skyy", "skyx"),
        P("skyy", "skyx"),
        P("skyy", "skyx"),
        P("skyy", "skyx"),
        P("skyy", "skyx", None),
        P(),
    )
    out_specs = (P("skyy", "skyx"), P("skyy", "skyx"))
    return jax.shard_map(
        per_device, mesh=mesh, in_specs=in_specs, out_specs=out_specs, check_vma=False
    )
```

time: 355 us -> 129 us (0.36)
  the two profiles are of different devices: /device:TPU:107 before, /device:TPU:10 now
where the time goes in v1:
time: 129 us
  Pallas kernels  43.5 us (34%)
  starting transfers between devices  34.2 us (27%)
  waiting for transfers between devices  26.9 us (21%)
  local copies, waits for them, and re-layouts  23.4 us (18%)
    pallas_call x1, Pallas kernels, match_first(): pl.pallas_call(first_kernel, out_shape=jax.ShapeDtypeStruct((CANVAS_ROWS,...  25.1 us
    unnamed x46, local copies, waits for them, and re-layouts  19.6 us
    all_to_all x1, waiting for transfers between devices, per_device(): lax.all_to_all(outgoing, 'skyx', split_axis=0, concat_axis=0, tiled=True)  19.5 us
    ppermute x6, starting transfers between devices, shifted(): lax.ppermute(block, axis, [(i - distance, i) for i in devices if i - dist...  18.8 us
    all_to_all x1, starting transfers between devices, per_device(): lax.all_to_all(outgoing, 'skyx', split_axis=0, concat_axis=0, tiled=True)  8.45 us
    ppermute x6, waiting for transfers between devices, shifted(): lax.ppermute(block, axis, [(i - distance, i) for i in devices if i - dist...  7.46 us
    all_to_all x1, starting transfers between devices, per_device(): late = lax.all_to_all(late, 'skyx', split_axis=0, concat_axis=0, tiled=True)  6.9 us
    pallas_call x1, Pallas kernels, pack(): pl.pallas_call(pack_kernel, out_shape=(jax.ShapeDtypeStruct((tiles, PH +...  5.21 us
  transfers between devices with their start and end apart: 8, of which 4 were waited for; matrix products, arithmetic and copies ran while one was open for 3% of the time, Pallas kernels for 25%

profile of v1, /device:TPU:10, one launch (start us, length us, event | category | flops | bytes accessed | tf_op | source)
XLA Modules:
  0.0 129.1 jit_solution(9232782011358901606)
XLA Ops:
  1.4 1.6 %copy-done.6 = f32[1,16,128,256]{3,2,1,0:T(8,128)S(1)} copy-done((f32[1,16,128,256]{3,2,1,0:T(8,128)S(1)}, f32[1,16,128,256]{3,2,1,0:T(8,128)}, u32[]{:S(2)}) %copy-start.6) | copy-done | bytes 2097176
  6.3 5.2 %pack.1 = (f32[16,136,256]{2,1,0:T(8,128)S(1)}, s32[3,16]{1,0:T(4,128)S(1)}) custom-call(s32[1,16]{1,0:T(1,128)S(1)} %bitcast.18, s32[1,16]{1,0:T(1,128)S(1)} %copy-done.10, s32[1,16]{1,0:T(1,128)S(1)} %copy-done.11, s32[1,16]{1,0:T(1,128)S(1)} %copy-done.12, f32[1,16]{1,0:T(1,128)S(1)} %copy-done.14, f32[16,8]{1,0:T(8,128)S(1)} %copy.16.coefs, ...), custom_call_target="tpu_custom_call" | custom-call | tf_op jit(solution)/shard_map/pack/pallas_call | solution.py:183
  11.5 1.4 %copy-done.5 = f32[16,136,256]{2,1,0:T(8,128)} copy-done((f32[16,136,256]{2,1,0:T(8,128)}, f32[16,136,256]{2,1,0:T(8,128)S(1)}, u32[]{:S(2)}) %copy-start.5) | copy-done | bytes 2228248
  13.4 8.5 %all-to-all-start = ((f32[16,136,256]{2,1,0:T(8,128)}), f32[16,136,256]{2,1,0:T(8,128)S(1)}, u32[]{:S(2)}, u32[]{:S(2)}) async-start(f32[16,136,256]{2,1,0:T(8,128)} %copy-done.5), calls=%async_computation | async-start | bytes 4456448 | tf_op jit(solution)/shard_map/all_to_all | solution.py:425
  23.7 4.4 %match_second.1 = f32[16,128,256]{2,1,0:T(8,128)S(1)} custom-call(s32[3,16]{1,0:T(4,128)S(1)} %copy-done.21, f32[16,8]{1,0:T(8,128)S(1)} %copy.16.coefs, s32[1,16]{1,0:T(1,128)S(1)} %copy-done.13, f32[1,16]{1,0:T(1,128)S(1)} %copy-done.15, f32[16,128,256]{2,1,0:T(8,128)} %bitcast.15, bf16[1024,256]{1,0:T(8,128)(2,1)S(1)} %get-tuple-element.14.down_high, ...), custom_call_target="tpu_custom_call" | custom-call | flops 5000000000 | bytes 6000000 | tf_op jit(solution)/shard_map/match_second/pallas_call | solution.py:241
  28.1 1.3 %copy-done.7 = f32[16,128,256]{2,1,0:T(8,128)} copy-done((f32[16,128,256]{2,1,0:T(8,128)}, f32[16,128,256]{2,1,0:T(8,128)S(1)}, u32[]{:S(2)}) %copy-start.7) | copy-done | bytes 2097176
  29.4 1.0 copy-done.16
  31.1 19.5 %all-to-all-done.slot = f32[16,136,256]{2,1,0:T(8,128)S(1)} async-done(((f32[16,136,256]{2,1,0:T(8,128)}), f32[16,136,256]{2,1,0:T(8,128)S(1)}, u32[]{:S(2)}, u32[]{:S(2)}) %all-to-all-start) | async-done | bytes 2228256 | tf_op jit(solution)/shard_map/all_to_all | solution.py:425
  50.6 1.4 %copy-done.3 = f32[16,136,256]{2,1,0:T(8,128)} copy-done((f32[16,136,256]{2,1,0:T(8,128)}, f32[16,136,256]{2,1,0:T(8,128)S(1)}, u32[]{:S(2)}) %copy-start.3) | copy-done | bytes 2228248
  52.0 6.9 %all-to-all-start.1 = ((f32[16,128,256]{2,1,0:T(8,128)}), f32[16,128,256]{2,1,0:T(8,128)S(1)}, u32[]{:S(2)}, u32[]{:S(2)}) async-start(f32[16,128,256]{2,1,0:T(8,128)} %copy-done.7), calls=%async_computation.1 | async-start | bytes 4194304 | tf_op jit(solution)/shard_map/all_to_all | solution.py:428
  58.9 0.8 slice.67
  59.8 0.8 slice.66
  60.6 1.6 %copy-done.4 = f32[16,136,256]{2,1,0:T(8,128)S(1)} copy-done((f32[16,136,256]{2,1,0:T(8,128)S(1)}, f32[16,136,256]{2,1,0:T(8,128)}, u32[]{:S(2)}) %copy-start.4) | copy-done | bytes 2228248
  62.2 1.2 copy-done.17
  63.5 1.0 copy-done.19
  64.5 25.1 %match_first.1.start = f32[776,896]{1,0:T(8,128)} custom-call(s32[16,16]{1,0:T(8,128)S(1)} %convert_bitcast_fusion.numbers, f32[16,8]{1,0:T(8,128)S(1)} %bitcast.17, f32[16,136,256]{2,1,0:T(8,128)S(1)} %copy-done.4, bf16[1024,256]{1,0:T(8,128)(2,1)S(1)} %copy-done.19, bf16[1024,128]{1,0:T(8,128)(2,1)S(1)} %get-tuple-element.15.down_low, ...), custom_call_target="tpu_custom_call" | custom-call | flops 10000000000 | bytes 8000000 | tf_op jit(solution)/shard_map/match_first/pallas_call | solution.py:294
  89.6 4.7 %place_second.1 = (f32[128,768]{1,0:T(8,128)S(1)}, f32[128,768]{1,0:T(8,128)S(1)}, f32[512,768]{1,0:T(8,128)S(1)}) custom-call(s32[16,16]{1,0:T(8,128)S(1)} %convert_bitcast_fusion.numbers, f32[776,896]{1,0:T(8,128)} %match_first.1.start, f32[16,128,256]{2,1,0:T(8,128)S(1)} %all-to-all-done.1.slot), custom_call_target="tpu_custom_call" | custom-call | tf_op jit(solution)/shard_map/place_second/pallas_call | solution.py:330
  94.3 1.1 copy-done
  95.5 1.9 %collective-permute-start = (f32[128,768]{1,0:T(8,128)S(1)}, f32[128,768]{1,0:T(8,128)S(1)}, u32[]{:S(2)}, u32[]{:S(2)}) collective-permute-start(f32[128,768]{1,0:T(8,128)S(1)} %get-tuple-element.20), channel_id=1, source_target_pairs={{0,1},{1,2},{2,3},{3,4},{4,5},{5,6},{6,7},{8,9},{9,10},{10,11},{11... | collective-permute-start | bytes 1179656 | tf_op jit(solution)/shard_map/ppermute | solution.py:374
  97.4 3.6 %collective-permute-start.1 = (f32[128,768]{1,0:T(8,128)S(1)}, f32[128,768]{1,0:T(8,128)S(1)}, u32[]{:S(2)}, u32[]{:S(2)}) collective-permute-start(f32[128,768]{1,0:T(8,128)S(1)} %get-tuple-element.21), channel_id=1, source_target_pairs={{1,0},{2,1},{3,2},{4,3},{5,4},{6,5},{7,6},{9,8},{10,9},{11,10},{12... | collective-permute-start | bytes 1179656 | tf_op jit(solution)/shard_map/ppermute | solution.py:374
  101.0 0.8 slice_bitcast_fusion
  101.9 2.7 %collective-permute-done.from_above = f32[128,768]{1,0:T(8,128)S(1)} collective-permute-done((f32[128,768]{1,0:T(8,128)S(1)}, f32[128,768]{1,0:T(8,128)S(1)}, u32[]{:S(2)}, u32[]{:S(2)}) %collective-permute-start) | collective-permute-done | bytes 393248 | tf_op jit(solution)/shard_map/ppermute | solution.py:374
  104.5 1.8 %collective-permute-done.1.from_below = f32[128,768]{1,0:T(8,128)S(1)} collective-permute-done((f32[128,768]{1,0:T(8,128)S(1)}, f32[128,768]{1,0:T(8,128)S(1)}, u32[]{:S(2)}, u32[]{:S(2)}) %collective-permute-start.1) | collective-permute-done | bytes 393248 | tf_op jit(solution)/shard_map/ppermute | solution.py:374
  106.3 1.4 %copy-done.1 = f32[512,768]{1,0:T(8,128)S(1)} copy-done((f32[512,768]{1,0:T(8,128)S(1)}, f32[512,768]{1,0:T(8,128)}, u32[]{:S(2)}) %copy-start.1) | copy-done | bytes 1572888
  107.8 2.1 %collective-permute-start.2 = (f32[512,128]{1,0:T(8,128)S(1)}, f32[512,128]{1,0:T(8,128)S(1)}, u32[]{:S(2)}, u32[]{:S(2)}) collective-permute-start(f32[512,128]{1,0:T(8,128)S(1)} %get-tuple-element.22), channel_id=1, source_target_pairs={{0,8},{8,16},{16,24},{24,32},{32,40},{40,48},{48,56},{56,64},{64,7... | collective-permute-start | bytes 786440 | tf_op jit(solution)/shard_map/ppermute | solution.py:374
  109.8 6.0 %collective-permute-start.3 = (f32[512,128]{1,0:T(8,128)S(1)}, f32[512,128]{1,0:T(8,128)S(1)}, u32[]{:S(2)}, u32[]{:S(2)}) collective-permute-start(f32[512,128]{1,0:T(8,128)S(1)} %get-tuple-element.23), channel_id=1, source_target_pairs={{8,0},{16,8},{24,16},{32,24},{40,32},{48,40},{56,48},{64,56},{72,6... | collective-permute-start | bytes 786440 | tf_op jit(solution)/shard_map/ppermute | solution.py:374
  116.3 3.3 %collective-permute-start.5 = (f32[8,256]{1,0:T(8,128)S(1)}, f32[8,256]{1,0:T(8,128)S(1)}, u32[]{:S(2)}, u32[]{:S(2)}) collective-permute-start(f32[8,256]{1,0:T(8,128)S(1)} %select_maximum_fusion.own), channel_id=1, source_target_pairs={{1,0},{2,1},{3,2},{4,3},{5,4},{6,5},{7,6},{9,8},{10,9},{11,10},{12... | collective-permute-start | bytes 24584 | tf_op jit(solution)/shard_map/ppermute | solution.py:374
  119.6 1.9 %collective-permute-start.4 = (f32[8,256]{1,0:T(8,128)S(1)}, f32[8,256]{1,0:T(8,128)S(1)}, u32[]{:S(2)}, u32[]{:S(2)}) collective-permute-start(f32[8,256]{1,0:T(8,128)S(1)} %select_maximum_fusion.own), channel_id=1, source_target_pairs={{0,1},{1,2},{2,3},{3,4},{4,5},{5,6},{6,7},{8,9},{9,10},{10,11},{11... | collective-permute-start | bytes 24584 | tf_op jit(solution)/shard_map/ppermute | solution.py:374
  121.5 3.0 %collective-permute-done.4.above = f32[8,256]{1,0:T(8,128)S(1)} collective-permute-done((f32[8,256]{1,0:T(8,128)S(1)}, f32[8,256]{1,0:T(8,128)S(1)}, u32[]{:S(2)}, u32[]{:S(2)}) %collective-permute-start.4) | collective-permute-done | bytes 8224 | tf_op jit(solution)/shard_map/ppermute | solution.py:374
  124.6 2.1 %make_depth.1.depth = f32[512,512]{1,0:T(8,128)} custom-call(f32[8,256]{1,0:T(8,128)S(1)} %select_maximum_fusion.own, f32[8,256]{1,0:T(8,128)S(1)} %collective-permute-done.4.above, f32[8,256]{1,0:T(8,128)S(1)} %collective-permute-done.5.below), custom_call_target="tpu_custom_call" | custom-call | flops 1000000000 | bytes 1000000 | tf_op jit(solution)/shard_map/make_depth/pallas_call | solution.py:361
  126.7 1.2 copy-done.8
  127.9 1.2 make_coadd.1
  (55 shorter events, 7.7 us)
Async XLA Ops:
  1.4 1.6 %copy-start.6 = (f32[1,16,128,256]{3,2,1,0:T(8,128)S(1)}, f32[1,16,128,256]{3,2,1,0:T(8,128)}, u32[]{:S(2)}) copy-start(f32[1,16,128,256]{3,2,1,0:T(8,128)} %param.8) | copy-start | bytes 6291460
  3.0 0.7 copy-start.9
  3.6 0.7 copy-start.10
  4.3 0.7 copy-start.11
  4.9 0.7 copy-start.12
  5.6 0.7 copy-start.14
  11.5 1.4 %copy-start.5 = (f32[16,136,256]{2,1,0:T(8,128)}, f32[16,136,256]{2,1,0:T(8,128)S(1)}, u32[]{:S(2)}) copy-start(f32[16,136,256]{2,1,0:T(8,128)S(1)} %get-tuple-element.13) | copy-start | bytes 6684676
  12.9 0.6 copy-start.20
  13.4 8.5 %copy-start.22 = (f32[2,8,41]{2,1,0:T(8,128)S(1)}, f32[2,8,41]{2,1,0:T(8,128)}, u32[]{:S(2)}) copy-start(f32[2,8,41]{2,1,0:T(8,128)} %param.15) | copy-start | bytes 7876
  13.4 9.5 %copy-start.13 = (s32[1,16]{1,0:T(1,128)S(1)}, s32[1,16]{1,0:T(1,128)}, u32[]{:S(2)}) copy-start(s32[1,16]{1,0:T(1,128)} %live.3) | copy-start | bytes 196
  13.4 9.5 %copy-start.15 = (f32[1,16]{1,0:T(1,128)S(1)}, f32[1,16]{1,0:T(1,128)}, u32[]{:S(2)}) copy-start(f32[1,16]{1,0:T(1,128)} %weight.3) | copy-start | bytes 196
  13.4 37.2 %all-to-all-start = ((f32[16,136,256]{2,1,0:T(8,128)}), f32[16,136,256]{2,1,0:T(8,128)S(1)}, u32[]{:S(2)}, u32[]{:S(2)}) async-start(f32[16,136,256]{2,1,0:T(8,128)} %copy-done.5), calls=%async_computation | async-start | bytes 4456448 | tf_op jit(solution)/shard_map/all_to_all | solution.py:425
  23.0 0.7 copy-start.21
  28.1 1.3 %copy-start.7 = (f32[16,128,256]{2,1,0:T(8,128)}, f32[16,128,256]{2,1,0:T(8,128)S(1)}, u32[]{:S(2)}) copy-start(f32[16,128,256]{2,1,0:T(8,128)S(1)} %match_second.1) | copy-start | bytes 6291460
  29.4 1.0 copy-start.16
  30.4 0.8 copy-start.18
  50.6 1.4 %copy-start.3 = (f32[16,136,256]{2,1,0:T(8,128)}, f32[16,136,256]{2,1,0:T(8,128)S(1)}, u32[]{:S(2)}) copy-start(f32[16,136,256]{2,1,0:T(8,128)S(1)} %all-to-all-done.slot) | copy-start | bytes 6684676
  52.0 37.6 %all-to-all-start.1 = ((f32[16,128,256]{2,1,0:T(8,128)}), f32[16,128,256]{2,1,0:T(8,128)S(1)}, u32[]{:S(2)}, u32[]{:S(2)}) async-start(f32[16,128,256]{2,1,0:T(8,128)} %copy-done.7), calls=%async_computation.1 | async-start | bytes 4194304 | tf_op jit(solution)/shard_map/all_to_all | solution.py:428
  60.6 1.6 %copy-start.4 = (f32[16,136,256]{2,1,0:T(8,128)S(1)}, f32[16,136,256]{2,1,0:T(8,128)}, u32[]{:S(2)}) copy-start(f32[16,136,256]{2,1,0:T(8,128)} %copy-done.3) | copy-start | bytes 6684676
  62.2 1.2 copy-start.17
  63.5 1.0 copy-start.19
  94.3 1.1 copy-start
  95.5 9.1 %collective-permute-start = (f32[128,768]{1,0:T(8,128)S(1)}, f32[128,768]{1,0:T(8,128)S(1)}, u32[]{:S(2)}, u32[]{:S(2)}) collective-permute-start(f32[128,768]{1,0:T(8,128)S(1)} %get-tuple-element.20), channel_id=1, source_target_pairs={{0,1},{1,2},{2,3},{3,4},{4,5},{5,6},{6,7},{8,9},{9,10},{10,11},{11... | collective-permute-start | bytes 1179656 | tf_op jit(solution)/shard_map/ppermute | solution.py:374
  97.4 8.9 %collective-permute-start.1 = (f32[128,768]{1,0:T(8,128)S(1)}, f32[128,768]{1,0:T(8,128)S(1)}, u32[]{:S(2)}, u32[]{:S(2)}) collective-permute-start(f32[128,768]{1,0:T(8,128)S(1)} %get-tuple-element.21), channel_id=1, source_target_pairs={{1,0},{2,1},{3,2},{4,3},{5,4},{6,5},{7,6},{9,8},{10,9},{11,10},{12... | collective-permute-start | bytes 1179656 | tf_op jit(solution)/shard_map/ppermute | solution.py:374
  106.3 1.4 %copy-start.1 = (f32[512,768]{1,0:T(8,128)S(1)}, f32[512,768]{1,0:T(8,128)}, u32[]{:S(2)}) copy-start(f32[512,768]{1,0:T(8,128)} %copy-done) | copy-start | bytes 4718596
  107.8 18.9 %copy-start.2 = (f32[512,768]{1,0:T(8,128)S(1)}, f32[512,768]{1,0:T(8,128)}, u32[]{:S(2)}) copy-start(f32[512,768]{1,0:T(8,128)} %copy-done) | copy-start | bytes 4718596
  107.8 18.9 %collective-permute-start.2 = (f32[512,128]{1,0:T(8,128)S(1)}, f32[512,128]{1,0:T(8,128)S(1)}, u32[]{:S(2)}, u32[]{:S(2)}) collective-permute-start(f32[512,128]{1,0:T(8,128)S(1)} %get-tuple-element.22), channel_id=1, source_target_pairs={{0,8},{8,16},{16,24},{24,32},{32,40},{40,48},{48,56},{56,64},{64,7... | collective-permute-start | bytes 786440 | tf_op jit(solution)/shard_map/ppermute | solution.py:374
  109.8 16.8 %collective-permute-start.3 = (f32[512,128]{1,0:T(8,128)S(1)}, f32[512,128]{1,0:T(8,128)S(1)}, u32[]{:S(2)}, u32[]{:S(2)}) collective-permute-start(f32[512,128]{1,0:T(8,128)S(1)} %get-tuple-element.23), channel_id=1, source_target_pairs={{8,0},{16,8},{24,16},{32,24},{40,32},{48,40},{56,48},{64,56},{72,6... | collective-permute-start | bytes 786440 | tf_op jit(solution)/shard_map/ppermute | solution.py:374
  116.3 5.2 %collective-permute-start.5 = (f32[8,256]{1,0:T(8,128)S(1)}, f32[8,256]{1,0:T(8,128)S(1)}, u32[]{:S(2)}, u32[]{:S(2)}) collective-permute-start(f32[8,256]{1,0:T(8,128)S(1)} %select_maximum_fusion.own), channel_id=1, source_target_pairs={{1,0},{2,1},{3,2},{4,3},{5,4},{6,5},{7,6},{9,8},{10,9},{11,10},{12... | collective-permute-start | bytes 24584 | tf_op jit(solution)/shard_map/ppermute | solution.py:374
  119.6 5.0 %collective-permute-start.4 = (f32[8,256]{1,0:T(8,128)S(1)}, f32[8,256]{1,0:T(8,128)S(1)}, u32[]{:S(2)}, u32[]{:S(2)}) collective-permute-start(f32[8,256]{1,0:T(8,128)S(1)} %select_maximum_fusion.own), channel_id=1, source_target_pairs={{0,1},{1,2},{2,3},{3,4},{4,5},{5,6},{6,7},{8,9},{9,10},{10,11},{11... | collective-permute-start | bytes 24584 | tf_op jit(solution)/shard_map/ppermute | solution.py:374
  126.7 1.2 copy-start.8

commit v2 on v1

v2 whole, which is shorter than its diff:
```python
import jax
import jax.numpy as jnp
from jax import lax
from jax.experimental import pallas as pl
from jax.experimental.pallas import tpu as pltpu
from jax.sharding import PartitionSpec as P

TILE = 512
MARGIN = 128
CAP = 2
PH = 128
PW = 256
NB = 8
TAPS = 41
HALF = TAPS // 2
SIDE = TILE + 2 * MARGIN
CANVAS_ROWS = SIDE + 8
CANVAS_COLS = SIDE + 128
META = 8
GROUP = 4
MIB = 1024 * 1024

prior_weight = 0.5
f32 = jnp.float32
bf16 = jnp.bfloat16
i32 = jnp.int32


def whole(shape):
    return pl.BlockSpec(shape, lambda *_: (0,) * len(shape))


smem = pl.BlockSpec(memory_space=pltpu.SMEM)
vmem = pl.BlockSpec(memory_space=pltpu.VMEM)
anywhere = pl.BlockSpec(memory_space=pl.ANY)


def split(x):
    high = x.astype(bf16)
    return high, (x - high.astype(f32)).astype(bf16)


def fill_bands(basis, down_high, down_low, across_high, across_low):
    for b in range(NB):
        taps = jnp.broadcast_to(basis[1, b : b + 1, :], (PW, PW + 128))
        table = pltpu.roll(taps, 0, 1, stride=1, stride_axis=0)[:, :PW]
        high, low = split(table)
        across_high[b * PW : (b + 1) * PW, :] = high
        across_low[b * PW : (b + 1) * PW, :] = low
        taps = jnp.broadcast_to(basis[0, b : b + 1, :], (PH, PW + 128))
        table = pltpu.roll(taps, 0, 1, stride=1, stride_axis=0)[:, :PH]
        high, low = split(table)
        down_high[b * PH : (b + 1) * PH, :PH] = high
        down_high[b * PH : (b + 1) * PH, PH:] = high
        down_low[b * PH : (b + 1) * PH, :] = low


BANDS = [
    pltpu.VMEM((NB * PH, 2 * PH), bf16),
    pltpu.VMEM((NB * PH, PH), bf16),
    pltpu.VMEM((NB * PW, PW), bf16),
    pltpu.VMEM((NB * PW, PW), bf16),
]


def spread_taps(basis):
    taps = jnp.stack([basis[0][:, ::-1], basis[1]])
    gap = jnp.zeros((2, NB, PW + 128 - TAPS), f32)
    return jnp.concatenate([taps[:, :, HALF:], gap, taps[:, :, :HALF]], axis=2)


def pack_kernel(*refs):
    given, patches, out, second = refs[:6], refs[6], refs[7], refs[8]
    scalars, vectors = refs[9:15], refs[15:20]
    slots, held, meta, small_sems, in_sems, out_sems, meta_sem = refs[20:]
    dest, row_offset, col_offset, live, weight, coefs = scalars
    count = patches.shape[0]
    tiles = out.shape[0]

    def bring(k):
        return pltpu.make_async_copy(patches.at[k], held.at[k], in_sems.at[k])

    def give(k, t):
        return pltpu.make_async_copy(held.at[k], out.at[t, pl.ds(0, PH)], out_sems.at[k])

    small = [
        pltpu.make_async_copy(source, target, small_sems.at[n])
        for n, (source, target) in enumerate(zip(given + given[:5], scalars + vectors))
    ]
    for copy in small:
        copy.start()
    for k in range(count):
        bring(k).start()
    for copy in small:
        copy.wait()

    def clear(t, carry):
        slots[0, t] = -1
        slots[1, t] = -1
        return carry

    lax.fori_loop(0, tiles, clear, 0)

    def assign(k, carry):
        t = dest[0, k]
        rank = jnp.where(slots[0, t] >= 0, 1, 0)
        slots[rank, t] = k
        return carry

    lax.fori_loop(0, count, assign, 0)

    meta[...] = jnp.zeros_like(meta)
    for row, values in enumerate(vectors):
        line = values[...].astype(f32)
        for t in range(tiles):
            meta[t, row : row + 1, 0:count] = line

    def forward(k, carry):
        bring(k).wait()
        t = dest[0, k]

        @pl.when(slots[0, t] == k)
        def _():
            give(k, t).start()

        return carry

    lax.fori_loop(0, count, forward, 0)

    def list_second(t, n):
        k = slots[1, t]

        @pl.when(k >= 0)
        def _():
            second[0, n] = k
            second[1, n] = t

        return n + jnp.where(k >= 0, 1, 0)

    def fill(j, carry):
        second[0, j] = 0
        second[1, j] = 0
        return carry

    lax.fori_loop(0, tiles, fill, 0)
    n_second = lax.fori_loop(0, tiles, list_second, 0)

    def repeat_last(j, carry):
        last = jnp.maximum(n_second - 1, 0)

        @pl.when(j >= n_second)
        def _():
            second[0, j] = second[0, last]
            second[1, j] = second[1, last]

        return carry

    lax.fori_loop(0, tiles, repeat_last, 0)
    second[2, 0] = n_second

    lane = lax.broadcasted_iota(i32, (1, 128), 1)

    def describe(t, carry):
        first = slots[0, t]
        k = jnp.maximum(first, 0)
        late = slots[1, t]
        j = jnp.maximum(late, 0)
        numbers = (
            jnp.where(first >= 0, 1, 0), row_offset[0, k], col_offset[0, k], live[0, k],
            jnp.where(late >= 0, 1, 0), row_offset[0, j], col_offset[0, j], live[0, j],
        )
        line = jnp.zeros((1, 128), i32)
        for place, number in enumerate(numbers):
            line = jnp.where(lane == place, number, line)
        meta[t, 6:7, 0:128] = line.astype(f32)
        line = jnp.zeros((1, 128), f32)
        for b in range(NB):
            line = jnp.where(lane == b, coefs[b, k] * weight[0, k], line)
        meta[t, 5:6, 0:128] = line
        return carry

    lax.fori_loop(0, tiles, describe, 0, unroll=4)

    about = pltpu.make_async_copy(meta, out.at[:, pl.ds(PH, META)], meta_sem)
    about.start()

    def finish(k, carry):
        t = dest[0, k]

        @pl.when(slots[0, t] == k)
        def _():
            give(k, t).wait()

        return carry

    lax.fori_loop(0, count, finish, 0)
    about.wait()


def pack(patches, dest, row_offset, col_offset, live_rows, weight, coefficient, tiles):
    given = (dest, row_offset, col_offset, live_rows, weight, coefficient)
    return pl.pallas_call(
        pack_kernel,
        out_shape=(
            jax.ShapeDtypeStruct((tiles, PH + META, PW), f32),
            jax.ShapeDtypeStruct((3, tiles), i32),
        ),
        in_specs=[anywhere] * 7,
        out_specs=(anywhere, smem),
        scratch_shapes=[pltpu.SMEM(x.shape, x.dtype) for x in given]
        + [pltpu.VMEM(x.shape, x.dtype) for x in given[:5]]
        + [
            pltpu.SMEM((CAP, tiles), i32),
            pltpu.VMEM(patches.shape, f32),
            pltpu.VMEM((tiles, META, PW), f32),
            pltpu.SemaphoreType.DMA((11,)),
            pltpu.SemaphoreType.DMA(patches.shape[:1]),
            pltpu.SemaphoreType.DMA(patches.shape[:1]),
            pltpu.SemaphoreType.DMA,
        ],
        compiler_params=pltpu.CompilerParams(vmem_limit_bytes=62 * MIB),
        name="pack",
    )(*given, patches)


def match(images, coefs, terms, down_high, down_low, across_high, across_low):
    middle = PH * len(images)
    for g, (image, scales) in enumerate(zip(images, coefs)):
        high, low = split(image)
        both = jnp.concatenate([high, low], axis=0)
        rows = slice(g * PH, (g + 1) * PH)
        low_rows = slice(middle + g * PH, middle + (g + 1) * PH)
        for b in range(NB):
            taps = slice(b * PH, (b + 1) * PH)
            cols = slice(b * PW, (b + 1) * PW)
            downward = jnp.dot(down_high[taps], both, preferred_element_type=f32)
            downward += jnp.dot(down_low[taps], high, preferred_element_type=f32)
            terms[rows, cols], terms[low_rows, cols] = split(downward * scales[b])
    wide = jnp.dot(terms[...], across_high[...], preferred_element_type=f32)
    fine = jnp.dot(terms[:middle], across_low[...], preferred_element_type=f32)
    total = wide[:middle] + wide[middle:] + fine
    return [total[g * PH : (g + 1) * PH] for g in range(len(images))]


def live_mask(live):
    return lax.broadcasted_iota(i32, (PH, PW), 0) < live


def second_kernel(second, coefs, live, weight, row_offset, col_offset, patch, taps, out, terms, *bands):
    j = pl.program_id(0)

    @pl.when(j == 0)
    def _():
        fill_bands(taps, *bands)

    @pl.when(j < second[2, 0])
    def _():
        k = second[0, j]
        mask = live_mask(live[0, k])
        scaled = [coefs[b, k] * weight[0, k] for b in range(NB)]
        image = jnp.where(mask, patch[0], 0.0)
        (matched,) = match([image], [scaled], terms, *bands)
        out[0] = turn(jnp.where(mask, matched, 0.0), row_offset[0, k] + MARGIN, col_offset[0, k] + MARGIN)


def match_second(second, coefficient, live_rows, weight, row_offset, col_offset, patches, taps, tiles):
    steps = patches.shape[0] // CAP
    return pl.pallas_call(
        second_kernel,
        out_shape=jax.ShapeDtypeStruct((tiles, PH, PW), f32),
        grid_spec=pltpu.PrefetchScalarGridSpec(
            num_scalar_prefetch=1,
            grid=(steps,),
            in_specs=[smem] * 5
            + [pl.BlockSpec((1, PH, PW), lambda j, second: (second[0, j], 0, 0))]
            + [whole((2, NB, PW + 128))],
            out_specs=pl.BlockSpec((1, PH, PW), lambda j, second: (second[1, j], 0, 0)),
            scratch_shapes=[pltpu.VMEM((2 * PH, NB * PW), bf16)] + BANDS,
        ),
        compiler_params=pltpu.CompilerParams(vmem_limit_bytes=24 * MIB),
        cost_estimate=pl.CostEstimate(flops=5_000_000_000, bytes_accessed=6_000_000, transcendentals=0),
        name="match_second",
    )(second, coefficient, live_rows, weight, row_offset, col_offset, patches, taps)


def turn(piece, top, left):
    down = top % 8
    right = left % 128
    tiles = pltpu.roll(piece.reshape(PH // 8, 8, PW), down, 1)
    before = jnp.concatenate([tiles[-1:], tiles[:-1]], axis=0)
    wrapped = lax.broadcasted_iota(i32, tiles.shape, 1) < down
    piece = jnp.where(wrapped, before, tiles).reshape(PH, PW)
    near = pltpu.roll(piece[:, :128], right, 1)
    far = pltpu.roll(piece[:, 128:], right, 1)
    wrapped = lax.broadcasted_iota(i32, near.shape, 1) < right
    return jnp.concatenate([jnp.where(wrapped, far, near), jnp.where(wrapped, near, far)], axis=1)


def add_turned(canvas, piece, top, left):
    down = top % 8
    right = left % 128
    row = pl.multiple_of(top - down, 8)
    col = pl.multiple_of(left - right, 128)
    near = piece[:, :128]
    wrapped = lax.broadcasted_iota(i32, near.shape, 1) < right
    columns = (jnp.where(wrapped, 0.0, near), piece[:, 128:], jnp.where(wrapped, near, 0.0))
    over = lax.broadcasted_iota(i32, (8, 128), 0) < down
    for place, part in enumerate(columns):
        at = pl.ds(pl.multiple_of(col + 128 * place, 128), 128)
        canvas[pl.ds(row, 8), at] += jnp.where(over, 0.0, part[:8])
        canvas[pl.ds(pl.multiple_of(row + 8, 8), PH - 8), at] += part[8:]
        canvas[pl.ds(pl.multiple_of(row + PH, 8), 8), at] += jnp.where(over, part[:8], 0.0)


def first_kernel(slots, group, taps, out, numbers, canvas, about, sem, out_sem, terms, *bands):
    step = pl.program_id(0)
    tiles = slots.shape[0]
    told = pltpu.make_async_copy(slots.at[:, pl.ds(PH, META), pl.ds(0, 128)], about, sem)

    @pl.when(step == 0)
    def _():
        told.start()
        fill_bands(taps, *bands)
        canvas[...] = jnp.zeros_like(canvas)

    images, coefs, masks = [], [], []
    for g in range(GROUP):
        line = group[g, PH + 6 : PH + 7, 0:8]
        rows = jnp.broadcast_to(line[:, 3:4] * line[:, 0:1], (PH, PW)).astype(i32)
        mask = live_mask(rows)
        masks.append(mask)
        images.append(jnp.where(mask, group[g, :PH, :], 0.0))
        line = group[g, PH + 5 : PH + 6, 0:NB]
        coefs.append([line[:, b : b + 1] for b in range(NB)])
    matched = match(images, coefs, terms, *bands)

    @pl.when(step == 0)
    def _():
        told.wait()

        def tell(t, carry):
            for place in range(8):
                numbers[t, place] = about[t, 6, place].astype(i32)
            return carry

        lax.fori_loop(0, tiles, tell, 0)

    for g, (mask, image) in enumerate(zip(masks, matched)):
        t = step * GROUP + g
        corner = numbers[t, 1] + MARGIN, numbers[t, 2] + MARGIN
        add_turned(canvas, turn(jnp.where(mask, image, 0.0), *corner), *corner)

    @pl.when(step == pl.num_programs(0) - 1)
    def _():
        give = pltpu.make_async_copy(canvas.at[pl.ds(0, SIDE), pl.ds(0, SIDE)], out, out_sem)
        give.start()
        give.wait()


def match_first(slots, taps):
    tiles = slots.shape[0]
    return pl.pallas_call(
        first_kernel,
        out_shape=(
            jax.ShapeDtypeStruct((SIDE, SIDE), f32),
            jax.ShapeDtypeStruct((tiles, 8), i32),
        ),
        grid=(tiles // GROUP,),
        in_specs=[
            anywhere,
            pl.BlockSpec((GROUP, PH + META, PW), lambda s: (s, 0, 0)),
            whole((2, NB, PW + 128)),
        ],
        out_specs=(anywhere, smem),
        scratch_shapes=[
            pltpu.VMEM((CANVAS_ROWS, CANVAS_COLS), f32),
            pltpu.SMEM((tiles, META, 128), f32),
            pltpu.SemaphoreType.DMA,
            pltpu.SemaphoreType.DMA,
            pltpu.VMEM((2 * GROUP * PH, NB * PW), bf16),
        ]
        + BANDS,
        compiler_params=pltpu.CompilerParams(vmem_limit_bytes=62 * MIB),
        cost_estimate=pl.CostEstimate(flops=10_000_000_000, bytes_accessed=8_000_000, transcendentals=0),
        name="match_first",
    )(slots, slots, taps)


def second_place_kernel(numbers, start, slots, north, south, middle, west, east, canvas, held, base, sems, base_sem):
    tiles = slots.shape[0]

    def bring(t):
        return pltpu.make_async_copy(slots.at[t], held.at[t], sems.at[t])

    def fetch(t, carry):
        @pl.when(numbers[t, 4] > 0)
        def _():
            bring(t).start()

        return carry

    lax.fori_loop(0, tiles, fetch, 0)
    copy = pltpu.make_async_copy(start, base, base_sem)
    copy.start()
    canvas[...] = jnp.zeros_like(canvas)

    def add(t, carry):
        @pl.when(numbers[t, 4] > 0)
        def _():
            bring(t).wait()
            add_turned(canvas, held[t], numbers[t, 5] + MARGIN, numbers[t, 6] + MARGIN)

        return carry

    lax.fori_loop(0, tiles, add, 0)
    copy.wait()
    middle_rows = slice(MARGIN, MARGIN + TILE)
    inner = slice(2 * MARGIN, TILE)
    parts = (
        (north, slice(0, MARGIN), slice(0, SIDE)),
        (south, slice(MARGIN + TILE, SIDE), slice(0, SIDE)),
        (middle, middle_rows, slice(0, SIDE)),
        (west, inner, slice(0, MARGIN)),
        (east, inner, slice(MARGIN + TILE, SIDE)),
    )
    for out, rows, cols in parts:
        out[...] = base[rows, cols] + canvas[rows, cols]


def place_second(numbers, canvas, slots):
    strip = jax.ShapeDtypeStruct((MARGIN, SIDE), f32)
    side = jax.ShapeDtypeStruct((TILE - 2 * MARGIN, MARGIN), f32)
    return pl.pallas_call(
        second_place_kernel,
        out_shape=(strip, strip, jax.ShapeDtypeStruct((TILE, SIDE), f32), side, side),
        in_specs=[smem, anywhere, anywhere],
        out_specs=(vmem,) * 5,
        scratch_shapes=[
            pltpu.VMEM((CANVAS_ROWS, CANVAS_COLS), f32),
            pltpu.VMEM(slots.shape, f32),
            pltpu.VMEM(canvas.shape, f32),
            pltpu.SemaphoreType.DMA(slots.shape[:1]),
            pltpu.SemaphoreType.DMA,
        ],
        compiler_params=pltpu.CompilerParams(vmem_limit_bytes=20 * MIB),
        name="place_second",
    )(numbers, canvas, slots)


def depth_kernel(own, above, below, depth):
    total = jnp.zeros((TILE, TILE), f32)
    for about, step in ((own, 0), (above, -TILE), (below, TILE)):
        count = about.shape[1]
        place_at = lax.broadcasted_iota(i32, (TILE, count), 0).astype(f32)
        from_top = place_at - (about[0:1, :] + step)
        rows = jnp.where((from_top >= 0) & (from_top < about[2:3, :]), about[3:4, :], 0.0)
        from_left = place_at - about[1:2, :]
        cols = jnp.where((from_left >= 0) & (from_left < PW), 1.0, 0.0).astype(bf16)
        for part in split(rows):
            total += lax.dot_general(part, cols, (((1,), (1,)), ((), ())), preferred_element_type=f32)
    depth[...] = total


def make_depth(own, above, below):
    return pl.pallas_call(
        depth_kernel,
        out_shape=jax.ShapeDtypeStruct((TILE, TILE), f32),
        in_specs=[vmem] * 3,
        out_specs=vmem,
        compiler_params=pltpu.CompilerParams(vmem_limit_bytes=16 * MIB),
        cost_estimate=pl.CostEstimate(flops=1_000_000_000, bytes_accessed=1_000_000, transcendentals=0),
        name="make_depth",
    )(own, above, below)


def shifted(block, axis, distance):
    devices = range(lax.axis_size(axis))
    return lax.ppermute(block, axis, [(i - distance, i) for i in devices if i - distance in devices])


def edges_kernel(middle, from_above, from_below, west, east):
    low = TILE - MARGIN
    for out, cols in ((west, slice(0, MARGIN)), (east, slice(MARGIN + TILE, SIDE))):
        out[:MARGIN] = middle[:MARGIN, cols] + from_above[:, cols]
        out[MARGIN:] = middle[low:, cols] + from_below[:, cols]


def make_edges(middle, from_above, from_below):
    edge = jax.ShapeDtypeStruct((2 * MARGIN, MARGIN), f32)
    return pl.pallas_call(
        edges_kernel,
        out_shape=(edge, edge),
        in_specs=[vmem] * 3,
        out_specs=(vmem, vmem),
        compiler_params=pltpu.CompilerParams(vmem_limit_bytes=12 * MIB),
        name="make_edges",
    )(middle, from_above, from_below)


def final_kernel(middle, from_above, from_below, inner_west, inner_east, outer_west, outer_east, depth, coadd):
    core = slice(MARGIN, MARGIN + TILE)
    low = TILE - MARGIN
    coadd[...] = middle[:, core]
    coadd[:MARGIN] += from_above[:, core]
    coadd[low:] += from_below[:, core]
    for cols, inner, outer in ((slice(0, MARGIN), inner_west, outer_west), (slice(low, TILE), inner_east, outer_east)):
        coadd[:MARGIN, cols] += outer[:MARGIN]
        coadd[MARGIN:low, cols] += inner[...]
        coadd[low:, cols] += outer[MARGIN:]
    coadd[...] = coadd[...] / (depth[...] + prior_weight)


def make_coadd(*parts):
    return pl.pallas_call(
        final_kernel,
        out_shape=jax.ShapeDtypeStruct((TILE, TILE), f32),
        in_specs=[vmem] * 8,
        out_specs=vmem,
        compiler_params=pltpu.CompilerParams(vmem_limit_bytes=16 * MIB),
        name="make_coadd",
    )(*parts)


def per_device(patches, dest, row_offset, col_offset, live_rows, weight, coefficient, basis):
    tiles = lax.axis_size("skyx")
    images = patches[0]
    outgoing, second = pack(
        images, dest[:, :, 0], row_offset, col_offset, live_rows, weight, coefficient[0].T, tiles
    )
    arrived = lax.all_to_all(outgoing, "skyx", split_axis=0, concat_axis=0, tiled=True)
    taps = spread_taps(basis)
    late = match_second(second, coefficient[0].T, live_rows, weight, row_offset, col_offset, images, taps, tiles)
    late = lax.all_to_all(late, "skyx", split_axis=0, concat_axis=0, tiled=True)

    canvas, numbers = match_first(arrived, taps)

    about = arrived[:, PH : PH + 5, : images.shape[0]]
    band = jnp.transpose(about, (1, 0, 2)).reshape(5, -1)
    left = band[2] + (band[0] - lax.axis_index("skyx").astype(f32)) * TILE
    own = jnp.pad(jnp.stack([band[1], left, band[3], band[4]]), ((0, 4), (0, 0)))
    depth = make_depth(own, shifted(own, "skyy", 1), shifted(own, "skyy", -1))

    numbers, depth = lax.optimization_barrier((numbers, depth))
    north, south, middle, west, east = place_second(numbers, canvas, late)
    from_above = shifted(south, "skyy", 1)
    from_below = shifted(north, "skyy", -1)
    inner_west = shifted(east, "skyx", 1)
    inner_east = shifted(west, "skyx", -1)
    west, east = make_edges(middle, from_above, from_below)
    outer_west = shifted(east, "skyx", 1)
    outer_east = shifted(west, "skyx", -1)
    coadd = make_coadd(
        middle, from_above, from_below, inner_west, inner_east, outer_west, outer_east, depth
    )
    return (coadd, depth)


def solution(mesh):
    in_specs = (
        P("skyy", "skyx", None, None),
        P("skyy", "skyx", None),
        P("skyy", "skyx"),
        P("skyy", "skyx"),
        P("skyy", "skyx"),
        P("skyy", "skyx"),
        P("skyy", "skyx", None),
        P(),
    )
    out_specs = (P("skyy", "skyx"), P("skyy", "skyx"))
    return jax.shard_map(
        per_device, mesh=mesh, in_specs=in_specs, out_specs=out_specs, check_vma=False
    )
```

time: 129 us -> 104 us (0.81); the launches traced: 129 us -> 103 us
  local copies, waits for them, and re-layouts: 23.4 us -> 2.78 us
  Pallas kernels: 43.5 us -> 31.3 us
  starting transfers between devices: 34.2 us -> 42 us
  waiting for transfers between devices: 26.9 us -> 25.3 us
    unnamed x46 -> x26, local copies, waits for them, and re-layouts: 19.6 us -> 1.47 us
    pallas_call x3 -> x2, Pallas kernels: 30.5 us -> 19.7 us  [the longest x1 17.9 us: match_first(): pl.pallas_call(first_kernel, out_shape=(jax.ShapeDtypeStruct((SIDE, SIDE)...]
    ppermute x6 -> x8, starting transfers between devices: 18.8 us -> 25.9 us  [shifted(): lax.ppermute(block, axis, [(i - distance, i) for i in devices if i - dist...]
    ppermute x6 -> x8, waiting for transfers between devices: 7.46 us -> 2.49 us  [shifted(): lax.ppermute(block, axis, [(i - distance, i) for i in devices if i - dist...]
    all_to_all x1, waiting for transfers between devices: 19.5 us -> 22.8 us  [per_device(): lax.all_to_all(outgoing, 'skyx', split_axis=0, concat_axis=0, tiled=True)]
    slice x2 -> x0, local copies, waits for them, and re-layouts: 1.69 us -> none  [the longest x1 0.85 us: per_device(): coefs = about[:, 5, :NB]]
  transfers between devices with their start and end apart: 8 -> 10, of which waited for: 4 -> 3; matrix products, arithmetic and copies ran while one was open for 3% -> 2% of each run, Pallas kernels for 25% -> 24%
where the time goes in v2:
time: 104 us; the launch traced here: 103 us
  starting transfers between devices  42 us (40%)
  Pallas kernels  31.3 us (30%)
  waiting for transfers between devices  25.3 us (24%)
  local copies, waits for them, and re-layouts  2.78 us (3%)
    ppermute x8, starting transfers between devices, shifted(): lax.ppermute(block, axis, [(i - distance, i) for i in devices if i - dist...  25.9 us
    all_to_all x1, waiting for transfers between devices, per_device(): lax.all_to_all(outgoing, 'skyx', split_axis=0, concat_axis=0, tiled=True)  22.8 us
    pallas_call x1, Pallas kernels, match_first(): pl.pallas_call(first_kernel, out_shape=(jax.ShapeDtypeStruct((SIDE, SIDE)...  17.9 us
    all_to_all x1, starting transfers between devices, per_device(): lax.all_to_all(outgoing, 'skyx', split_axis=0, concat_axis=0, tiled=True)  8.47 us
    all_to_all x1, starting transfers between devices, per_device(): late = lax.all_to_all(late, 'skyx', split_axis=0, concat_axis=0, tiled=True)  7.56 us
    pallas_call x1, Pallas kernels, match_second(): pl.pallas_call(second_kernel, out_shape=jax.ShapeDtypeStruct((tiles, PH,...  4.25 us
    pallas_call x1, Pallas kernels, pack(): pl.pallas_call(pack_kernel, out_shape=(jax.ShapeDtypeStruct((tiles, PH +...  4.01 us
    ppermute x8, waiting for transfers between devices, shifted(): lax.ppermute(block, axis, [(i - distance, i) for i in devices if i - dist...  2.49 us
  transfers between devices with their start and end apart: 10, of which 3 were waited for; matrix products, arithmetic and copies ran while one was open for 2% of the time, Pallas kernels for 24%

profile of v2, /device:TPU:10, one launch (start us, length us, event | category | flops | bytes accessed | tf_op | source)
XLA Modules:
  0.0 102.5 jit_solution(387000286496437348)
XLA Ops:
  0.6 4.0 %pack.1 = (f32[16,136,256]{2,1,0:T(8,128)}, s32[3,16]{1,0:T(4,128)}) custom-call(s32[1,16]{1,0:T(1,128)} %bitcast.16, s32[1,16]{1,0:T(1,128)} %row_offset.1, s32[1,16]{1,0:T(1,128)} %col_offset.1, s32[1,16]{1,0:T(1,128)} %live.1, f32[1,16]{1,0:T(1,128)} %weight.1, f32[8,16]{1,0:T(8,128)} %bitcast.12, f32[16,128,256]{2,1,0:T(8,128)} %bitcast.10), custom_call_target="tpu_custom_call" | custom-call | tf_op jit(solution)/shard_map/pack/pallas_call | solution.py:202
  4.6 0.0 copy-start.12
  4.7 0.0 copy-start.1
  4.7 8.5 %all-to-all-start = ((f32[16,136,256]{2,1,0:T(8,128)}), f32[16,136,256]{2,1,0:T(8,128)}, u32[]{:S(2)}, u32[]{:S(2)}) async-start(f32[16,136,256]{2,1,0:T(8,128)} %get-tuple-element.15), calls=%async_computation | async-start | bytes 4456448 | tf_op jit(solution)/shard_map/all_to_all | solution.py:530
  13.2 0.1 rev.3
  13.3 0.1 pad.10.clone
  13.4 0.1 slice_maximum_fusion
  13.4 0.1 fusion.taps
  13.6 4.3 %match_second.1 = f32[16,128,256]{2,1,0:T(8,128)S(1)} custom-call(s32[3,16]{1,0:T(4,128)S(1)} %copy-done.11, f32[8,16]{1,0:T(8,128)S(1)} %bitcast.13, s32[1,16]{1,0:T(1,128)S(1)} %copy-done.9, f32[1,16]{1,0:T(1,128)S(1)} %copy-done.10, s32[1,16]{1,0:T(1,128)S(1)} %copy-done.7, s32[1,16]{1,0:T(1,128)S(1)} %copy-done.8, f32[16,128,256]{2,1,0:T(8,128)S(1)} %bitcast.11, ...), custom_call_target="tpu_custom_call" | custom-call | flops 5000000000 | bytes 6000000 | tf_op jit(solution)/shard_map/match_second/pallas_call | solution.py:268
  17.9 1.4 %copy-done.2 = f32[16,128,256]{2,1,0:T(8,128)} copy-done((f32[16,128,256]{2,1,0:T(8,128)}, f32[16,128,256]{2,1,0:T(8,128)S(1)}, u32[]{:S(2)}) %copy-start.2) | copy-done | bytes 2097176
  19.3 22.8 %all-to-all-done.slots.group = f32[16,136,256]{2,1,0:T(8,128)} async-done(((f32[16,136,256]{2,1,0:T(8,128)}), f32[16,136,256]{2,1,0:T(8,128)}, u32[]{:S(2)}, u32[]{:S(2)}) %all-to-all-start) | async-done | bytes 2228256 | tf_op jit(solution)/shard_map/all_to_all | solution.py:530
  42.0 7.6 %all-to-all-start.1 = ((f32[16,128,256]{2,1,0:T(8,128)}), f32[16,128,256]{2,1,0:T(8,128)}, u32[]{:S(2)}, u32[]{:S(2)}) async-start(f32[16,128,256]{2,1,0:T(8,128)} %copy-done.2), calls=%async_computation.1 | async-start | bytes 4194304 | tf_op jit(solution)/shard_map/all_to_all | solution.py:533
  49.6 0.8 slice_bitcast_fusion
  50.4 0.1 slice_reduce_fusion.2
  50.5 0.1 slice.47
  50.6 0.1 slice.51
  50.7 0.1 add.16
  50.8 0.1 slice.53
  50.9 1.9 %collective-permute-start.1 = (f32[8,256]{1,0:T(8,128)S(1)}, f32[8,256]{1,0:T(8,128)S(1)}, u32[]{:S(2)}, u32[]{:S(2)}) collective-permute-start(f32[8,256]{1,0:T(8,128)S(1)} %select_maximum_fusion.own), channel_id=1, source_target_pairs={{1,0},{2,1},{3,2},{4,3},{5,4},{6,5},{7,6},{9,8},{10,9},{11,10},{12... | collective-permute-start | bytes 24584 | tf_op jit(solution)/shard_map/ppermute | solution.py:478
  52.8 2.4 %collective-permute-start = (f32[8,256]{1,0:T(8,128)S(1)}, f32[8,256]{1,0:T(8,128)S(1)}, u32[]{:S(2)}, u32[]{:S(2)}) collective-permute-start(f32[8,256]{1,0:T(8,128)S(1)} %select_maximum_fusion.own), channel_id=1, source_target_pairs={{0,1},{1,2},{2,3},{3,4},{4,5},{5,6},{6,7},{8,9},{9,10},{10,11},{11... | collective-permute-start | bytes 24584 | tf_op jit(solution)/shard_map/ppermute | solution.py:478
  55.2 17.9 %match_first.1 = (f32[768,768]{1,0:T(8,128)}, s32[16,8]{1,0:T(8,128)}) custom-call(f32[16,136,256]{2,1,0:T(8,128)} %all-to-all-done.slots.group, f32[16,136,256]{2,1,0:T(8,128)} %all-to-all-done.slots.group, f32[2,8,384]{2,1,0:T(8,128)} %copy-done.4), custom_call_target="tpu_custom_call" | custom-call | flops 10000000000 | bytes 8000000 | tf_op jit(solution)/shard_map/match_first/pallas_call | solution.py:362
  73.2 2.1 %make_depth.1.depth = f32[512,512]{1,0:T(8,128)} custom-call(f32[8,256]{1,0:T(8,128)S(1)} %select_maximum_fusion.own, f32[8,256]{1,0:T(8,128)S(1)} %collective-permute-done.above, f32[8,256]{1,0:T(8,128)S(1)} %collective-permute-done.1.below), custom_call_target="tpu_custom_call" | custom-call | flops 1000000000 | bytes 1000000 | tf_op jit(solution)/shard_map/make_depth/pallas_call | solution.py:465
  75.3 1.8 %place_second.1 = (f32[128,768]{1,0:T(8,128)S(1)}, f32[128,768]{1,0:T(8,128)S(1)}, f32[512,768]{1,0:T(8,128)S(1)}, f32[256,128]{1,0:T(8,128)S(1)}, f32[256,128]{1,0:T(8,128)S(1)}) custom-call(s32[16,8]{1,0:T(8,128)S(1)} %copy-done.5, f32[768,768]{1,0:T(8,128)S(1)} %copy-done, f32[16,128,256]{2,1,0:T(8,128)} %all-to-all-done.1.slots), custom_call_target="tpu_custom_call" | custom-call | tf_op jit(solution)/shard_map/place_second/pallas_call | solution.py:433
  77.1 3.2 %collective-permute-start.2 = (f32[128,768]{1,0:T(8,128)S(1)}, f32[128,768]{1,0:T(8,128)S(1)}, u32[]{:S(2)}, u32[]{:S(2)}) collective-permute-start(f32[128,768]{1,0:T(8,128)S(1)} %get-tuple-element.21), channel_id=1, source_target_pairs={{0,1},{1,2},{2,3},{3,4},{4,5},{5,6},{6,7},{8,9},{9,10},{10,11},{11... | collective-permute-start | bytes 1179656 | tf_op jit(solution)/shard_map/ppermute | solution.py:478
  80.3 2.5 %collective-permute-start.3 = (f32[128,768]{1,0:T(8,128)S(1)}, f32[128,768]{1,0:T(8,128)S(1)}, u32[]{:S(2)}, u32[]{:S(2)}) collective-permute-start(f32[128,768]{1,0:T(8,128)S(1)} %get-tuple-element.22), channel_id=1, source_target_pairs={{1,0},{2,1},{3,2},{4,3},{5,4},{6,5},{7,6},{9,8},{10,9},{11,10},{12... | collective-permute-start | bytes 1179656 | tf_op jit(solution)/shard_map/ppermute | solution.py:478
  82.8 3.4 %collective-permute-start.4 = (f32[256,128]{1,0:T(8,128)S(1)}, f32[256,128]{1,0:T(8,128)S(1)}, u32[]{:S(2)}, u32[]{:S(2)}) collective-permute-start(f32[256,128]{1,0:T(8,128)S(1)} %get-tuple-element.23), channel_id=1, source_target_pairs={{0,8},{8,16},{16,24},{24,32},{32,40},{40,48},{48,56},{56,64},{64,7... | collective-permute-start | bytes 393224 | tf_op jit(solution)/shard_map/ppermute | solution.py:478
  86.2 4.6 %collective-permute-start.5 = (f32[256,128]{1,0:T(8,128)S(1)}, f32[256,128]{1,0:T(8,128)S(1)}, u32[]{:S(2)}, u32[]{:S(2)}) collective-permute-start(f32[256,128]{1,0:T(8,128)S(1)} %get-tuple-element.24), channel_id=1, source_target_pairs={{8,0},{16,8},{24,16},{32,24},{40,32},{48,40},{56,48},{64,56},{72,6... | collective-permute-start | bytes 393224 | tf_op jit(solution)/shard_map/ppermute | solution.py:478
  90.9 1.9 %collective-permute-start.6 = (f32[256,128]{1,0:T(8,128)S(1)}, f32[256,128]{1,0:T(8,128)S(1)}, u32[]{:S(2)}, u32[]{:S(2)}) collective-permute-start(f32[256,128]{1,0:T(8,128)S(1)} %get-tuple-element.25), channel_id=1, source_target_pairs={{0,8},{8,16},{16,24},{24,32},{32,40},{40,48},{48,56},{56,64},{64,7... | collective-permute-start | bytes 393224 | tf_op jit(solution)/shard_map/ppermute | solution.py:478
  92.8 6.0 %collective-permute-start.7 = (f32[256,128]{1,0:T(8,128)S(1)}, f32[256,128]{1,0:T(8,128)S(1)}, u32[]{:S(2)}, u32[]{:S(2)}) collective-permute-start(f32[256,128]{1,0:T(8,128)S(1)} %get-tuple-element.26), channel_id=1, source_target_pairs={{8,0},{16,8},{24,16},{32,24},{40,32},{48,40},{56,48},{64,56},{72,6... | collective-permute-start | bytes 393224 | tf_op jit(solution)/shard_map/ppermute | solution.py:478
  98.8 1.0 collective-permute-done.6.outer_west
  99.8 1.5 %collective-permute-done.7.outer_east = f32[256,128]{1,0:T(8,128)S(1)} collective-permute-done((f32[256,128]{1,0:T(8,128)S(1)}, f32[256,128]{1,0:T(8,128)S(1)}, u32[]{:S(2)}, u32[]{:S(2)}) %collective-permute-start.7) | collective-permute-done | bytes 131104 | tf_op jit(solution)/shard_map/ppermute | solution.py:478
  101.3 1.2 %make_coadd.1 = f32[512,512]{1,0:T(8,128)} custom-call(f32[512,768]{1,0:T(8,128)S(1)} %get-tuple-element.20.middle, f32[128,768]{1,0:T(8,128)S(1)} %collective-permute-done.2.from_above, f32[128,768]{1,0:T(8,128)S(1)} %collective-permute-done.3.from_below, f32[256,128]{1,0:T(8,128)S(1)} %collective-permute-done.4.inner_west, ...), custom_call_target="tpu_custom_call" | custom-call | tf_op jit(solution)/shard_map/make_coadd/pallas_call | solution.py:514
  (34 shorter events, 0.1 us)
Async XLA Ops:
  4.6 8.6 %copy-start.12 = (f32[2,8,41]{2,1,0:T(8,128)S(1)}, f32[2,8,41]{2,1,0:T(8,128)}, u32[]{:S(2)}) copy-start(f32[2,8,41]{2,1,0:T(8,128)} %param.15) | copy-start | bytes 7876
  4.7 8.9 %copy-start.1 = (f32[1,16,128,256]{3,2,1,0:T(8,128)S(1)}, f32[1,16,128,256]{3,2,1,0:T(8,128)}, u32[]{:S(2)}) copy-start(f32[1,16,128,256]{3,2,1,0:T(8,128)} %param.8) | copy-start | bytes 6291460
  4.7 8.9 %copy-start.6 = (f32[1,16,8]{1,2,0:T(8,128)S(1)}, f32[1,16,8]{1,2,0:T(8,128)}, u32[]{:S(2)}) copy-start(f32[1,16,8]{1,2,0:T(8,128)} %param.14) | copy-start | bytes 1540
  4.7 8.9 %copy-start.7 = (s32[1,16]{1,0:T(1,128)S(1)}, s32[1,16]{1,0:T(1,128)}, u32[]{:S(2)}) copy-start(s32[1,16]{1,0:T(1,128)} %row_offset.1) | copy-start | bytes 196
  4.7 8.9 %copy-start.8 = (s32[1,16]{1,0:T(1,128)S(1)}, s32[1,16]{1,0:T(1,128)}, u32[]{:S(2)}) copy-start(s32[1,16]{1,0:T(1,128)} %col_offset.1) | copy-start | bytes 196
  4.7 8.9 %copy-start.9 = (s32[1,16]{1,0:T(1,128)S(1)}, s32[1,16]{1,0:T(1,128)}, u32[]{:S(2)}) copy-start(s32[1,16]{1,0:T(1,128)} %live.1) | copy-start | bytes 196
  4.7 8.9 %copy-start.10 = (f32[1,16]{1,0:T(1,128)S(1)}, f32[1,16]{1,0:T(1,128)}, u32[]{:S(2)}) copy-start(f32[1,16]{1,0:T(1,128)} %weight.1) | copy-start | bytes 196
  4.7 8.9 %copy-start.11 = (s32[3,16]{1,0:T(4,128)S(1)}, s32[3,16]{1,0:T(4,128)}, u32[]{:S(2)}) copy-start(s32[3,16]{1,0:T(4,128)} %get-tuple-element.19.second) | copy-start | bytes 580
  4.7 37.3 %all-to-all-start = ((f32[16,136,256]{2,1,0:T(8,128)}), f32[16,136,256]{2,1,0:T(8,128)}, u32[]{:S(2)}, u32[]{:S(2)}) async-start(f32[16,136,256]{2,1,0:T(8,128)} %get-tuple-element.15), calls=%async_computation | async-start | bytes 4456448 | tf_op jit(solution)/shard_map/all_to_all | solution.py:530
  13.5 4.3 %copy-start.4 = (f32[2,8,384]{2,1,0:T(8,128)}, f32[2,8,384]{2,1,0:T(8,128)S(1)}, u32[]{:S(2)}) copy-start(f32[2,8,384]{2,1,0:T(8,128)S(1)} %fusion.taps) | copy-start | bytes 73732
  17.9 1.4 %copy-start.2 = (f32[16,128,256]{2,1,0:T(8,128)}, f32[16,128,256]{2,1,0:T(8,128)S(1)}, u32[]{:S(2)}) copy-start(f32[16,128,256]{2,1,0:T(8,128)S(1)} %match_second.1) | copy-start | bytes 6291460
  42.0 33.3 %all-to-all-start.1 = ((f32[16,128,256]{2,1,0:T(8,128)}), f32[16,128,256]{2,1,0:T(8,128)}, u32[]{:S(2)}, u32[]{:S(2)}) async-start(f32[16,128,256]{2,1,0:T(8,128)} %copy-done.2), calls=%async_computation.1 | async-start | bytes 4194304 | tf_op jit(solution)/shard_map/all_to_all | solution.py:533
  50.9 22.3 %collective-permute-start.1 = (f32[8,256]{1,0:T(8,128)S(1)}, f32[8,256]{1,0:T(8,128)S(1)}, u32[]{:S(2)}, u32[]{:S(2)}) collective-permute-start(f32[8,256]{1,0:T(8,128)S(1)} %select_maximum_fusion.own), channel_id=1, source_target_pairs={{1,0},{2,1},{3,2},{4,3},{5,4},{6,5},{7,6},{9,8},{10,9},{11,10},{12... | collective-permute-start | bytes 24584 | tf_op jit(solution)/shard_map/ppermute | solution.py:478
  52.8 20.4 %collective-permute-start = (f32[8,256]{1,0:T(8,128)S(1)}, f32[8,256]{1,0:T(8,128)S(1)}, u32[]{:S(2)}, u32[]{:S(2)}) collective-permute-start(f32[8,256]{1,0:T(8,128)S(1)} %select_maximum_fusion.own), channel_id=1, source_target_pairs={{0,1},{1,2},{2,3},{3,4},{4,5},{5,6},{6,7},{8,9},{9,10},{10,11},{11... | collective-permute-start | bytes 24584 | tf_op jit(solution)/shard_map/ppermute | solution.py:478
  73.1 2.2 %copy-start = (f32[768,768]{1,0:T(8,128)S(1)}, f32[768,768]{1,0:T(8,128)}, u32[]{:S(2)}) copy-start(f32[768,768]{1,0:T(8,128)} %get-tuple-element.18.start) | copy-start | bytes 7077892
  73.2 2.2 %copy-start.5 = (s32[16,8]{1,0:T(8,128)S(1)}, s32[16,8]{1,0:T(8,128)}, u32[]{:S(2)}) copy-start(s32[16,8]{1,0:T(8,128)} %get-tuple-element.17.numbers) | copy-start | bytes 1540
  77.1 24.2 %copy-start.3 = (f32[512,512]{1,0:T(8,128)S(1)}, f32[512,512]{1,0:T(8,128)}, u32[]{:S(2)}) copy-start(f32[512,512]{1,0:T(8,128)} %make_depth.1.depth) | copy-start | bytes 3145732
  77.1 13.7 %collective-permute-start.2 = (f32[128,768]{1,0:T(8,128)S(1)}, f32[128,768]{1,0:T(8,128)S(1)}, u32[]{:S(2)}, u32[]{:S(2)}) collective-permute-start(f32[128,768]{1,0:T(8,128)S(1)} %get-tuple-element.21), channel_id=1, source_target_pairs={{0,1},{1,2},{2,3},{3,4},{4,5},{5,6},{6,7},{8,9},{9,10},{10,11},{11... | collective-permute-start | bytes 1179656 | tf_op jit(solution)/shard_map/ppermute | solution.py:478
  80.3 10.5 %collective-permute-start.3 = (f32[128,768]{1,0:T(8,128)S(1)}, f32[128,768]{1,0:T(8,128)S(1)}, u32[]{:S(2)}, u32[]{:S(2)}) collective-permute-start(f32[128,768]{1,0:T(8,128)S(1)} %get-tuple-element.22), channel_id=1, source_target_pairs={{1,0},{2,1},{3,2},{4,3},{5,4},{6,5},{7,6},{9,8},{10,9},{11,10},{12... | collective-permute-start | bytes 1179656 | tf_op jit(solution)/shard_map/ppermute | solution.py:478
  82.8 16.0 %collective-permute-start.4 = (f32[256,128]{1,0:T(8,128)S(1)}, f32[256,128]{1,0:T(8,128)S(1)}, u32[]{:S(2)}, u32[]{:S(2)}) collective-permute-start(f32[256,128]{1,0:T(8,128)S(1)} %get-tuple-element.23), channel_id=1, source_target_pairs={{0,8},{8,16},{16,24},{24,32},{32,40},{40,48},{48,56},{56,64},{64,7... | collective-permute-start | bytes 393224 | tf_op jit(solution)/shard_map/ppermute | solution.py:478
  86.2 12.6 %collective-permute-start.5 = (f32[256,128]{1,0:T(8,128)S(1)}, f32[256,128]{1,0:T(8,128)S(1)}, u32[]{:S(2)}, u32[]{:S(2)}) collective-permute-start(f32[256,128]{1,0:T(8,128)S(1)} %get-tuple-element.24), channel_id=1, source_target_pairs={{8,0},{16,8},{24,16},{32,24},{40,32},{48,40},{56,48},{64,56},{72,6... | collective-permute-start | bytes 393224 | tf_op jit(solution)/shard_map/ppermute | solution.py:478
  90.9 9.0 %collective-permute-start.6 = (f32[256,128]{1,0:T(8,128)S(1)}, f32[256,128]{1,0:T(8,128)S(1)}, u32[]{:S(2)}, u32[]{:S(2)}) collective-permute-start(f32[256,128]{1,0:T(8,128)S(1)} %get-tuple-element.25), channel_id=1, source_target_pairs={{0,8},{8,16},{16,24},{24,32},{32,40},{40,48},{48,56},{56,64},{64,7... | collective-permute-start | bytes 393224 | tf_op jit(solution)/shard_map/ppermute | solution.py:478
  92.8 8.5 %collective-permute-start.7 = (f32[256,128]{1,0:T(8,128)S(1)}, f32[256,128]{1,0:T(8,128)S(1)}, u32[]{:S(2)}, u32[]{:S(2)}) collective-permute-start(f32[256,128]{1,0:T(8,128)S(1)} %get-tuple-element.26), channel_id=1, source_target_pairs={{8,0},{16,8},{24,16},{32,24},{40,32},{48,40},{56,48},{64,56},{72,6... | collective-permute-start | bytes 393224 | tf_op jit(solution)/shard_map/ppermute | solution.py:478

commit v3 on v2

--- a/solution.py
+++ b/solution.py
@@ -18,6 +18,7 @@
 CANVAS_COLS = SIDE + 128
 META = 8
 GROUP = 4
+KEPT_ROWS = 20 * SIDE
 MIB = 1024 * 1024
 
 prior_weight = 0.5
@@ -33,6 +34,7 @@
 smem = pl.BlockSpec(memory_space=pltpu.SMEM)
 vmem = pl.BlockSpec(memory_space=pltpu.VMEM)
 anywhere = pl.BlockSpec(memory_space=pl.ANY)
+hbm = pl.BlockSpec(memory_space=pltpu.HBM)
 
 
 def split(x):
@@ -312,7 +314,7 @@
         canvas[pl.ds(pl.multiple_of(row + PH, 8), 8), at] += jnp.where(over, part[:8], 0.0)
 
 
-def first_kernel(slots, group, taps, out, numbers, canvas, about, sem, out_sem, terms, *bands):
+def first_kernel(slots, group, taps, out, canvas, about, numbers, lines, sem, out_sem, terms, *bands):
     step = pl.program_id(0)
     tiles = slots.shape[0]
     told = pltpu.make_async_copy(slots.at[:, pl.ds(PH, META), pl.ds(0, 128)], about, sem)
@@ -325,6 +327,7 @@
 
     images, coefs, masks = [], [], []
     for g in range(GROUP):
+        lines[pl.ds(step * GROUP + g, 1), :] = group[g, PH + 6 : PH + 7, 0:128]
         line = group[g, PH + 6 : PH + 7, 0:8]
         rows = jnp.broadcast_to(line[:, 3:4] * line[:, 0:1], (PH, PW)).astype(i32)
         mask = live_mask(rows)
@@ -352,31 +355,34 @@
 
     @pl.when(step == pl.num_programs(0) - 1)
     def _():
-        give = pltpu.make_async_copy(canvas.at[pl.ds(0, SIDE), pl.ds(0, SIDE)], out, out_sem)
-        give.start()
-        give.wait()
+        parts = (canvas.at[pl.ds(0, SIDE), pl.ds(0, SIDE)], lines)
+        places = (out.at[pl.ds(0, SIDE)], out.at[pl.ds(SIDE, tiles), pl.ds(0, 128)])
+        copies = [pltpu.make_async_copy(part, at, out_sem.at[n]) for n, (part, at) in enumerate(zip(parts, places))]
+        for copy in copies:
+            copy.start()
+        for copy in copies:
+            copy.wait()
 
 
 def match_first(slots, taps):
     tiles = slots.shape[0]
     return pl.pallas_call(
         first_kernel,
-        out_shape=(
-            jax.ShapeDtypeStruct((SIDE, SIDE), f32),
-            jax.ShapeDtypeStruct((tiles, 8), i32),
-        ),
+        out_shape=jax.ShapeDtypeStruct((KEPT_ROWS, SIDE), f32),
         grid=(tiles // GROUP,),
         in_specs=[
             anywhere,
             pl.BlockSpec((GROUP, PH + META, PW), lambda s: (s, 0, 0)),
             whole((2, NB, PW + 128)),
         ],
-        out_specs=(anywhere, smem),
+        out_specs=anywhere,
         scratch_shapes=[
             pltpu.VMEM((CANVAS_ROWS, CANVAS_COLS), f32),
             pltpu.SMEM((tiles, META, 128), f32),
+            pltpu.SMEM((tiles, 8), i32),
+            pltpu.VMEM((tiles, 128), f32),
             pltpu.SemaphoreType.DMA,
-            pltpu.SemaphoreType.DMA,
+            pltpu.SemaphoreType.DMA((2,)),
             pltpu.VMEM((2 * GROUP * PH, NB * PW), bf16),
         ]
         + BANDS,
@@ -386,13 +392,26 @@
     )(slots, slots, taps)
 
 
-def second_place_kernel(numbers, start, slots, north, south, middle, west, east, canvas, held, base, sems, base_sem):
+def second_place_kernel(
+    kept, band, slots, rows_next, rows_last, middle, cols_next, cols_last,
+    told, numbers, canvas, held, base, sems, base_sem, told_sem,
+):
     tiles = slots.shape[0]
 
     def bring(t):
         return pltpu.make_async_copy(slots.at[t], held.at[t], sems.at[t])
 
+    tell = pltpu.make_async_copy(kept.at[pl.ds(SIDE, tiles), pl.ds(0, 128)], told, told_sem)
+    tell.start()
+    copy = pltpu.make_async_copy(kept.at[pl.ds(0, SIDE)], base, base_sem)
+    copy.start()
+    canvas[...] = jnp.zeros_like(canvas)
+    tell.wait()
+
     def fetch(t, carry):
+        for place in range(4, 7):
+            numbers[t, place] = told[t, place].astype(i32)
+
         @pl.when(numbers[t, 4] > 0)
         def _():
             bring(t).start()
@@ -400,9 +419,6 @@
         return carry
 
     lax.fori_loop(0, tiles, fetch, 0)
-    copy = pltpu.make_async_copy(start, base, base_sem)
-    copy.start()
-    canvas[...] = jnp.zeros_like(canvas)
 
     def add(t, carry):
         @pl.when(numbers[t, 4] > 0)
@@ -414,43 +430,52 @@
 
     lax.fori_loop(0, tiles, add, 0)
     copy.wait()
-    middle_rows = slice(MARGIN, MARGIN + TILE)
-    inner = slice(2 * MARGIN, TILE)
-    parts = (
-        (north, slice(0, MARGIN), slice(0, SIDE)),
-        (south, slice(MARGIN + TILE, SIDE), slice(0, SIDE)),
-        (middle, middle_rows, slice(0, SIDE)),
-        (west, inner, slice(0, MARGIN)),
-        (east, inner, slice(MARGIN + TILE, SIDE)),
-    )
-    for out, rows, cols in parts:
-        out[...] = base[rows, cols] + canvas[rows, cols]
-
-
-def place_second(numbers, canvas, slots):
-    strip = jax.ShapeDtypeStruct((MARGIN, SIDE), f32)
+    low, high = slice(0, MARGIN), slice(MARGIN + TILE, SIDE)
+    core, inner = slice(MARGIN, MARGIN + TILE), slice(2 * MARGIN, TILE)
+    middle[...] = base[core] + canvas[core, :SIDE]
+    for out in (rows_next, rows_last):
+        out[MARGIN:] = jnp.zeros((META, SIDE), f32)
+        out[MARGIN:, : band.shape[1]] = band[...]
+    for axis, outs in (("skyy", (rows_next, rows_last)), ("skyx", (cols_next, cols_last))):
+        for parity in range(2):
+
+            @pl.when(lax.axis_index(axis) % 2 == parity)
+            def _():
+                for out, strip in zip(outs, (high, low) if parity == 0 else (low, high)):
+                    rows, cols = (strip, slice(0, SIDE)) if axis == "skyy" else (inner, strip)
+                    out[: rows.stop - rows.start] = base[rows, cols] + canvas[rows, cols]
+
+
+def place_second(kept, band, slots):
+    tiles = slots.shape[0]
+    strip = jax.ShapeDtypeStruct((MARGIN + META, SIDE), f32)
     side = jax.ShapeDtypeStruct((TILE - 2 * MARGIN, MARGIN), f32)
     return pl.pallas_call(
         second_place_kernel,
         out_shape=(strip, strip, jax.ShapeDtypeStruct((TILE, SIDE), f32), side, side),
-        in_specs=[smem, anywhere, anywhere],
+        in_specs=[anywhere, vmem, anywhere],
         out_specs=(vmem,) * 5,
         scratch_shapes=[
+            pltpu.SMEM((tiles, 128), f32),
+            pltpu.SMEM((tiles, 8), i32),
             pltpu.VMEM((CANVAS_ROWS, CANVAS_COLS), f32),
             pltpu.VMEM(slots.shape, f32),
-            pltpu.VMEM(canvas.shape, f32),
+            pltpu.VMEM((SIDE, SIDE), f32),
             pltpu.SemaphoreType.DMA(slots.shape[:1]),
+            pltpu.SemaphoreType.DMA,
             pltpu.SemaphoreType.DMA,
         ],
         compiler_params=pltpu.CompilerParams(vmem_limit_bytes=20 * MIB),
         name="place_second",
-    )(numbers, canvas, slots)
-
-
-def depth_kernel(own, above, below, depth):
+    )(kept, band, slots)
+
+
+def depth_kernel(own, rows_next, rows_last, depth, divisor):
     total = jnp.zeros((TILE, TILE), f32)
-    for about, step in ((own, 0), (above, -TILE), (below, TILE)):
-        count = about.shape[1]
+    count = own.shape[1]
+    toward = jnp.where(lax.axis_index("skyy") % 2 == 0, TILE, -TILE).astype(f32)
+    for about, step in ((own, 0.0), (rows_next, toward), (rows_last, -toward)):
+        about = about[-META:, :count]
         place_at = lax.broadcasted_iota(i32, (TILE, count), 0).astype(f32)
         from_top = place_at - (about[0:1, :] + step)
         rows = jnp.where((from_top >= 0) & (from_top < about[2:3, :]), about[3:4, :], 0.0)
@@ -459,33 +484,45 @@
         for part in split(rows):
             total += lax.dot_general(part, cols, (((1,), (1,)), ((), ())), preferred_element_type=f32)
     depth[...] = total
-
-
-def make_depth(own, above, below):
+    divisor[...] = total + prior_weight
+
+
+def make_depth(own, rows_next, rows_last):
     return pl.pallas_call(
         depth_kernel,
-        out_shape=jax.ShapeDtypeStruct((TILE, TILE), f32),
+        out_shape=(jax.ShapeDtypeStruct((TILE, TILE), f32),) * 2,
         in_specs=[vmem] * 3,
-        out_specs=vmem,
+        out_specs=(vmem, vmem),
         compiler_params=pltpu.CompilerParams(vmem_limit_bytes=16 * MIB),
         cost_estimate=pl.CostEstimate(flops=1_000_000_000, bytes_accessed=1_000_000, transcendentals=0),
         name="make_depth",
-    )(own, above, below)
-
-
-def shifted(block, axis, distance):
-    devices = range(lax.axis_size(axis))
-    return lax.ppermute(block, axis, [(i - distance, i) for i in devices if i - distance in devices])
-
-
-def edges_kernel(middle, from_above, from_below, west, east):
+    )(own, rows_next, rows_last)
+
+
+def exchange(block, axis, first):
+    pairs = [(i, i + 1) for i in range(first, lax.axis_size(axis) - 1, 2)]
+    return lax.ppermute(block, axis, pairs + [(j, i) for i, j in pairs])
+
+
+def by_side(axis, following, preceding):
+    even = lax.axis_index(axis) % 2 == 0
+    return jnp.where(even, preceding, following), jnp.where(even, following, preceding)
+
+
+def edges_kernel(middle, rows_next, rows_last, cols_next, cols_last):
     low = TILE - MARGIN
-    for out, cols in ((west, slice(0, MARGIN)), (east, slice(MARGIN + TILE, SIDE))):
-        out[:MARGIN] = middle[:MARGIN, cols] + from_above[:, cols]
-        out[MARGIN:] = middle[low:, cols] + from_below[:, cols]
-
-
-def make_edges(middle, from_above, from_below):
+    strips = slice(0, MARGIN), slice(MARGIN + TILE, SIDE)
+    for parity in range(2):
+
+        @pl.when(lax.axis_index("skyx") % 2 == parity)
+        def _():
+            for out, cols in zip((cols_next, cols_last), strips[::-1] if parity == 0 else strips):
+                above, below = by_side("skyy", rows_next[:MARGIN, cols], rows_last[:MARGIN, cols])
+                out[:MARGIN] = middle[:MARGIN, cols] + above
+                out[MARGIN:] = middle[low:, cols] + below
+
+
+def make_edges(middle, rows_next, rows_last):
     edge = jax.ShapeDtypeStruct((2 * MARGIN, MARGIN), f32)
     return pl.pallas_call(
         edges_kernel,
@@ -494,20 +531,23 @@
         out_specs=(vmem, vmem),
         compiler_params=pltpu.CompilerParams(vmem_limit_bytes=12 * MIB),
         name="make_edges",
-    )(middle, from_above, from_below)
-
-
-def final_kernel(middle, from_above, from_below, inner_west, inner_east, outer_west, outer_east, depth, coadd):
+    )(middle, rows_next, rows_last)
+
+
+def final_kernel(middle, rows_next, rows_last, inner_next, inner_last, outer_next, outer_last, divisor, coadd):
     core = slice(MARGIN, MARGIN + TILE)
     low = TILE - MARGIN
+    above, below = by_side("skyy", rows_next[:MARGIN, core], rows_last[:MARGIN, core])
     coadd[...] = middle[:, core]
-    coadd[:MARGIN] += from_above[:, core]
-    coadd[low:] += from_below[:, core]
-    for cols, inner, outer in ((slice(0, MARGIN), inner_west, outer_west), (slice(low, TILE), inner_east, outer_east)):
-        coadd[:MARGIN, cols] += outer[:MARGIN]
-        coadd[MARGIN:low, cols] += inner[...]
-        coadd[low:, cols] += outer[MARGIN:]
-    coadd[...] = coadd[...] / (depth[...] + prior_weight)
+    coadd[:MARGIN] += above
+    coadd[low:] += below
+    inner = by_side("skyx", inner_next[...], inner_last[...])
+    outer = by_side("skyx", outer_next[...], outer_last[...])
+    for cols, close, far in zip((slice(0, MARGIN), slice(low, TILE)), inner, outer):
+        coadd[:MARGIN, cols] += far[:MARGIN]
+        coadd[MARGIN:low, cols] += close
+        coadd[low:, cols] += far[MARGIN:]
+    coadd[...] = coadd[...] / divisor[...]
 
 
 def make_coadd(*parts):
@@ -532,25 +572,24 @@
     late = match_second(second, coefficient[0].T, live_rows, weight, row_offset, col_offset, images, taps, tiles)
     late = lax.all_to_all(late, "skyx", split_axis=0, concat_axis=0, tiled=True)
 
-    canvas, numbers = match_first(arrived, taps)
+    kept = match_first(arrived, taps)
 
     about = arrived[:, PH : PH + 5, : images.shape[0]]
     band = jnp.transpose(about, (1, 0, 2)).reshape(5, -1)
     left = band[2] + (band[0] - lax.axis_index("skyx").astype(f32)) * TILE
-    own = jnp.pad(jnp.stack([band[1], left, band[3], band[4]]), ((0, 4), (0, 0)))
-    depth = make_depth(own, shifted(own, "skyy", 1), shifted(own, "skyy", -1))
-
-    numbers, depth = lax.optimization_barrier((numbers, depth))
-    north, south, middle, west, east = place_second(numbers, canvas, late)
-    from_above = shifted(south, "skyy", 1)
-    from_below = shifted(north, "skyy", -1)
-    inner_west = shifted(east, "skyx", 1)
-    inner_east = shifted(west, "skyx", -1)
-    west, east = make_edges(middle, from_above, from_below)
-    outer_west = shifted(east, "skyx", 1)
-    outer_east = shifted(west, "skyx", -1)
+    own = jnp.pad(jnp.stack([band[1], left, band[3], band[4]]), ((0, META - 4), (0, 0)))
+
+    rows_next, rows_last, middle, cols_next, cols_last = place_second(kept, own, late)
+    rows_last = exchange(rows_last, "skyy", 1)
+    rows_next = exchange(rows_next, "skyy", 0)
+    inner_last = exchange(cols_last, "skyx", 1)
+    inner_next = exchange(cols_next, "skyx", 0)
+    cols_next, cols_last = make_edges(middle, rows_next, rows_last)
+    outer_last = exchange(cols_last, "skyx", 1)
+    outer_next = exchange(cols_next, "skyx", 0)
+    depth, divisor = make_depth(own, rows_next, rows_last)
     coadd = make_coadd(
-        middle, from_above, from_below, inner_west, inner_east, outer_west, outer_east, depth
+        middle, rows_next, rows_last, inner_next, inner_last, outer_next, outer_last, divisor
     )
     return (coadd, depth)
 

time: 104 us -> 99.6 us (0.958)
  starting transfers between devices: 42 us -> 32.2 us
  waiting for transfers between devices: 25.3 us -> 31.3 us
    ppermute x8 -> x6, starting transfers between devices: 25.9 us -> 16.2 us  [exchange(): return lax.ppermute(block, axis, pairs + [(j, i) for i, j in pairs])]
    all_to_all x1, waiting for transfers between devices: 0.01 us -> 6.41 us  [per_device(): late = lax.all_to_all(late, 'skyx', split_axis=0, concat_axis=0, tiled=True)]
    ppermute x8 -> x6, waiting for transfers between devices: 2.49 us -> 2.07 us  [exchange(): return lax.ppermute(block, axis, pairs + [(j, i) for i, j in pairs])]
  transfers between devices with their start and end apart: 10 -> 8, of which waited for: 3 -> 3; matrix products, arithmetic and copies ran while one was open for 2% -> 2% of each run, Pallas kernels for 24% -> 24%
where the time goes in v3:
time: 99.6 us; the launch traced here: 98.4 us
  starting transfers between devices  32.2 us (32%)
  waiting for transfers between devices  31.3 us (31%)
  Pallas kernels  31 us (31%)
  local copies, waits for them, and re-layouts  2.68 us (3%)
    all_to_all x1, waiting for transfers between devices, per_device(): lax.all_to_all(outgoing, 'skyx', split_axis=0, concat_axis=0, tiled=True)  22.9 us
    pallas_call x1, Pallas kernels, match_first(): pl.pallas_call(first_kernel, out_shape=jax.ShapeDtypeStruct((KEPT_ROWS, S...  17.2 us
    ppermute x6, starting transfers between devices, exchange(): return lax.ppermute(block, axis, pairs + [(j, i) for i, j in pairs])  16.2 us
    all_to_all x1, starting transfers between devices, per_device(): lax.all_to_all(outgoing, 'skyx', split_axis=0, concat_axis=0, tiled=True)  8.47 us
    all_to_all x1, starting transfers between devices, per_device(): late = lax.all_to_all(late, 'skyx', split_axis=0, concat_axis=0, tiled=True)  7.56 us
    all_to_all x1, waiting for transfers between devices, per_device(): late = lax.all_to_all(late, 'skyx', split_axis=0, concat_axis=0, tiled=True)  6.41 us
    pallas_call x1, Pallas kernels, match_second(): pl.pallas_call(second_kernel, out_shape=jax.ShapeDtypeStruct((tiles, PH,...  4.25 us
    pallas_call x1, Pallas kernels, pack(): pl.pallas_call(pack_kernel, out_shape=(jax.ShapeDtypeStruct((tiles, PH +...  4.01 us
  transfers between devices with their start and end apart: 8, of which 3 were waited for; matrix products, arithmetic and copies ran while one was open for 2% of the time, Pallas kernels for 24%

profile of v3, /device:TPU:10, one launch (start us, length us, event | category | flops | bytes accessed | tf_op | source)
XLA Modules:
  0.0 98.4 jit_solution(3099420633941408908)
XLA Ops:
  0.6 4.0 %pack.1 = (f32[16,136,256]{2,1,0:T(8,128)}, s32[3,16]{1,0:T(4,128)}) custom-call(s32[1,16]{1,0:T(1,128)} %bitcast.16, s32[1,16]{1,0:T(1,128)} %row_offset.1, s32[1,16]{1,0:T(1,128)} %col_offset.1, s32[1,16]{1,0:T(1,128)} %live.1, f32[1,16]{1,0:T(1,128)} %weight.1, f32[8,16]{1,0:T(8,128)} %bitcast.12, f32[16,128,256]{2,1,0:T(8,128)} %bitcast.10), custom_call_target="tpu_custom_call" | custom-call | tf_op jit(solution)/shard_map/pack/pallas_call | solution.py:204
  4.7 0.0 copy-start
  4.7 0.0 copy-start.3
  4.7 0.0 copy-start.6
  4.7 8.5 %all-to-all-start = ((f32[16,136,256]{2,1,0:T(8,128)}), f32[16,136,256]{2,1,0:T(8,128)}, u32[]{:S(2)}, u32[]{:S(2)}) async-start(f32[16,136,256]{2,1,0:T(8,128)} %get-tuple-element.13), calls=%async_computation | async-start | bytes 4456448 | tf_op jit(solution)/shard_map/all_to_all | solution.py:570
  13.2 0.1 rev.3
  13.3 0.1 pad.10.clone
  13.4 0.1 slice_maximum_fusion
  13.5 0.1 fusion.taps
  13.6 4.3 %match_second.1 = f32[16,128,256]{2,1,0:T(8,128)S(1)} custom-call(s32[3,16]{1,0:T(4,128)S(1)} %copy-done.8, f32[8,16]{1,0:T(8,128)S(1)} %bitcast.13, s32[1,16]{1,0:T(1,128)S(1)} %copy-done.6, f32[1,16]{1,0:T(1,128)S(1)} %copy-done.7, s32[1,16]{1,0:T(1,128)S(1)} %copy-done.4, s32[1,16]{1,0:T(1,128)S(1)} %copy-done.5, f32[16,128,256]{2,1,0:T(8,128)S(1)} %bitcast.11, ...), custom_call_target="tpu_custom_call" | custom-call | flops 5000000000 | bytes 6000000 | tf_op jit(solution)/shard_map/match_second/pallas_call | solution.py:270
  17.9 1.3 %copy-done.1 = f32[16,128,256]{2,1,0:T(8,128)} copy-done((f32[16,128,256]{2,1,0:T(8,128)}, f32[16,128,256]{2,1,0:T(8,128)S(1)}, u32[]{:S(2)}) %copy-start.1) | copy-done | bytes 2097176
  19.2 22.9 %all-to-all-done.slots.group = f32[16,136,256]{2,1,0:T(8,128)} async-done(((f32[16,136,256]{2,1,0:T(8,128)}), f32[16,136,256]{2,1,0:T(8,128)}, u32[]{:S(2)}, u32[]{:S(2)}) %all-to-all-start) | async-done | bytes 2228256 | tf_op jit(solution)/shard_map/all_to_all | solution.py:570
  42.0 7.6 %all-to-all-start.1 = ((f32[16,128,256]{2,1,0:T(8,128)}), f32[16,128,256]{2,1,0:T(8,128)}, u32[]{:S(2)}, u32[]{:S(2)}) async-start(f32[16,128,256]{2,1,0:T(8,128)} %copy-done.1), calls=%async_computation.1 | async-start | bytes 4194304 | tf_op jit(solution)/shard_map/all_to_all | solution.py:573
  49.6 0.8 slice_bitcast_fusion
  50.4 0.1 slice_reduce_fusion.2
  50.6 0.1 slice.47
  50.6 0.1 slice.51
  50.7 0.1 add.16
  50.8 0.1 slice.53
  50.9 17.2 %match_first.1.kept = f32[15360,768]{1,0:T(8,128)} custom-call(f32[16,136,256]{2,1,0:T(8,128)} %all-to-all-done.slots.group, f32[16,136,256]{2,1,0:T(8,128)} %all-to-all-done.slots.group, f32[2,8,384]{2,1,0:T(8,128)} %copy-done.2), custom_call_target="tpu_custom_call" | custom-call | flops 10000000000 | bytes 8000000 | tf_op jit(solution)/shard_map/match_first/pallas_call | solution.py:369
  68.1 6.4 %all-to-all-done.1.slots = f32[16,128,256]{2,1,0:T(8,128)} async-done(((f32[16,128,256]{2,1,0:T(8,128)}), f32[16,128,256]{2,1,0:T(8,128)}, u32[]{:S(2)}, u32[]{:S(2)}) %all-to-all-start.1) | async-done | bytes 2097184 | tf_op jit(solution)/shard_map/all_to_all | solution.py:573
  74.5 2.1 %place_second.1 = (f32[136,768]{1,0:T(8,128)S(1)}, f32[136,768]{1,0:T(8,128)S(1)}, f32[512,768]{1,0:T(8,128)S(1)}, f32[256,128]{1,0:T(8,128)S(1)}, f32[256,128]{1,0:T(8,128)S(1)}) custom-call(f32[15360,768]{1,0:T(8,128)} %match_first.1.kept, f32[8,256]{1,0:T(8,128)S(1)} %select_maximum_fusion.band.own, f32[16,128,256]{2,1,0:T(8,128)} %all-to-all-done.1.slots), custom_call_target="tpu_custom_call" | custom-call | tf_op jit(solution)/shard_map/place_second/pallas_call | solution.py:453
  76.7 0.1 collective-permute-start
  76.7 2.4 %collective-permute-start.1 = (f32[136,768]{1,0:T(8,128)S(1)}, f32[136,768]{1,0:T(8,128)S(1)}, u32[]{:S(2)}, u32[]{:S(2)}) collective-permute-start(f32[136,768]{1,0:T(8,128)S(1)} %get-tuple-element.17), channel_id=1, source_target_pairs={{1,2},{3,4},{5,6},{2,1},{4,3},{6,5},{9,10},{11,12},{13,14},{10,9},... | collective-permute-start | bytes 1253384 | tf_op jit(solution)/shard_map/ppermute | solution.py:504
  79.2 0.7 collective-permute-start.2
  79.9 6.2 %collective-permute-start.3 = (f32[256,128]{1,0:T(8,128)S(1)}, f32[256,128]{1,0:T(8,128)S(1)}, u32[]{:S(2)}, u32[]{:S(2)}) collective-permute-start(f32[256,128]{1,0:T(8,128)S(1)} %get-tuple-element.19), channel_id=1, source_target_pairs={{8,16},{24,32},{40,48},{56,64},{72,80},{88,96},{104,112},{16,8},{3... | collective-permute-start | bytes 393224 | tf_op jit(solution)/shard_map/ppermute | solution.py:504
  86.1 0.0 collective-permute-done.1.rows_last
  86.2 0.7 collective-permute-start.4
  86.8 6.2 %collective-permute-start.5 = (f32[256,128]{1,0:T(8,128)S(1)}, f32[256,128]{1,0:T(8,128)S(1)}, u32[]{:S(2)}, u32[]{:S(2)}) collective-permute-start(f32[256,128]{1,0:T(8,128)S(1)} %get-tuple-element.21), channel_id=1, source_target_pairs={{8,16},{24,32},{40,48},{56,64},{72,80},{88,96},{104,112},{16,8},{3... | collective-permute-start | bytes 393224 | tf_op jit(solution)/shard_map/ppermute | solution.py:504
  93.0 2.1 %make_depth.1 = (f32[512,512]{1,0:T(8,128)}, f32[512,512]{1,0:T(8,128)S(1)}) custom-call(f32[8,256]{1,0:T(8,128)S(1)} %select_maximum_fusion.band.own, f32[136,768]{1,0:T(8,128)S(1)} %collective-permute-done.rows_next, f32[136,768]{1,0:T(8,128)S(1)} %collective-permute-done.1.rows_last), custom_call_target="tpu_custom_call" | custom-call | flops 1000000000 | bytes 1000000 | tf_op jit(solution)/shard_map/make_depth/pallas_call | solution.py:491
  95.1 2.0 %collective-permute-done.5.outer_last = f32[256,128]{1,0:T(8,128)S(1)} collective-permute-done((f32[256,128]{1,0:T(8,128)S(1)}, f32[256,128]{1,0:T(8,128)S(1)}, u32[]{:S(2)}, u32[]{:S(2)}) %collective-permute-start.5) | collective-permute-done | bytes 131104 | tf_op jit(solution)/shard_map/ppermute | solution.py:504
  97.2 1.3 %make_coadd.1 = f32[512,512]{1,0:T(8,128)} custom-call(f32[512,768]{1,0:T(8,128)S(1)} %get-tuple-element.15.middle, f32[136,768]{1,0:T(8,128)S(1)} %collective-permute-done.rows_next, f32[136,768]{1,0:T(8,128)S(1)} %collective-permute-done.1.rows_last, f32[256,128]{1,0:T(8,128)S(1)} %collective-permute-done.2.inner_next, ...), custom_call_target="tpu_custom_call" | custom-call | tf_op jit(solution)/shard_map/make_coadd/pallas_call | solution.py:554
  (24 shorter events, 0.1 us)
Async XLA Ops:
  4.7 8.6 %copy-start.9 = (f32[2,8,41]{2,1,0:T(8,128)S(1)}, f32[2,8,41]{2,1,0:T(8,128)}, u32[]{:S(2)}) copy-start(f32[2,8,41]{2,1,0:T(8,128)} %param.15) | copy-start | bytes 7876
  4.7 8.9 %copy-start = (f32[1,16,128,256]{3,2,1,0:T(8,128)S(1)}, f32[1,16,128,256]{3,2,1,0:T(8,128)}, u32[]{:S(2)}) copy-start(f32[1,16,128,256]{3,2,1,0:T(8,128)} %param.8) | copy-start | bytes 6291460
  4.7 8.9 %copy-start.3 = (f32[1,16,8]{1,2,0:T(8,128)S(1)}, f32[1,16,8]{1,2,0:T(8,128)}, u32[]{:S(2)}) copy-start(f32[1,16,8]{1,2,0:T(8,128)} %param.14) | copy-start | bytes 1540
  4.7 8.9 %copy-start.4 = (s32[1,16]{1,0:T(1,128)S(1)}, s32[1,16]{1,0:T(1,128)}, u32[]{:S(2)}) copy-start(s32[1,16]{1,0:T(1,128)} %row_offset.1) | copy-start | bytes 196
  4.7 8.9 %copy-start.5 = (s32[1,16]{1,0:T(1,128)S(1)}, s32[1,16]{1,0:T(1,128)}, u32[]{:S(2)}) copy-start(s32[1,16]{1,0:T(1,128)} %col_offset.1) | copy-start | bytes 196
  4.7 8.9 %copy-start.6 = (s32[1,16]{1,0:T(1,128)S(1)}, s32[1,16]{1,0:T(1,128)}, u32[]{:S(2)}) copy-start(s32[1,16]{1,0:T(1,128)} %live.1) | copy-start | bytes 196
  4.7 8.9 %copy-start.7 = (f32[1,16]{1,0:T(1,128)S(1)}, f32[1,16]{1,0:T(1,128)}, u32[]{:S(2)}) copy-start(f32[1,16]{1,0:T(1,128)} %weight.1) | copy-start | bytes 196
  4.7 8.9 %copy-start.8 = (s32[3,16]{1,0:T(4,128)S(1)}, s32[3,16]{1,0:T(4,128)}, u32[]{:S(2)}) copy-start(s32[3,16]{1,0:T(4,128)} %get-tuple-element.14.second) | copy-start | bytes 580
  4.7 37.3 %all-to-all-start = ((f32[16,136,256]{2,1,0:T(8,128)}), f32[16,136,256]{2,1,0:T(8,128)}, u32[]{:S(2)}, u32[]{:S(2)}) async-start(f32[16,136,256]{2,1,0:T(8,128)} %get-tuple-element.13), calls=%async_computation | async-start | bytes 4456448 | tf_op jit(solution)/shard_map/all_to_all | solution.py:570
  13.5 4.3 %copy-start.2 = (f32[2,8,384]{2,1,0:T(8,128)}, f32[2,8,384]{2,1,0:T(8,128)S(1)}, u32[]{:S(2)}) copy-start(f32[2,8,384]{2,1,0:T(8,128)S(1)} %fusion.taps) | copy-start | bytes 73732
  17.9 1.3 %copy-start.1 = (f32[16,128,256]{2,1,0:T(8,128)}, f32[16,128,256]{2,1,0:T(8,128)S(1)}, u32[]{:S(2)}) copy-start(f32[16,128,256]{2,1,0:T(8,128)S(1)} %match_second.1) | copy-start | bytes 6291460
  42.0 32.5 %all-to-all-start.1 = ((f32[16,128,256]{2,1,0:T(8,128)}), f32[16,128,256]{2,1,0:T(8,128)}, u32[]{:S(2)}, u32[]{:S(2)}) async-start(f32[16,128,256]{2,1,0:T(8,128)} %copy-done.1), calls=%async_computation.1 | async-start | bytes 4194304 | tf_op jit(solution)/shard_map/all_to_all | solution.py:573
  76.7 9.4 %collective-permute-start = (f32[136,768]{1,0:T(8,128)S(1)}, f32[136,768]{1,0:T(8,128)S(1)}, u32[]{:S(2)}, u32[]{:S(2)}) collective-permute-start(f32[136,768]{1,0:T(8,128)S(1)} %get-tuple-element.16), channel_id=1, source_target_pairs={{0,1},{2,3},{4,5},{6,7},{1,0},{3,2},{5,4},{7,6},{8,9},{10,11},{12,... | collective-permute-start | bytes 1253384 | tf_op jit(solution)/shard_map/ppermute | solution.py:504
  76.7 9.4 %collective-permute-start.1 = (f32[136,768]{1,0:T(8,128)S(1)}, f32[136,768]{1,0:T(8,128)S(1)}, u32[]{:S(2)}, u32[]{:S(2)}) collective-permute-start(f32[136,768]{1,0:T(8,128)S(1)} %get-tuple-element.17), channel_id=1, source_target_pairs={{1,2},{3,4},{5,6},{2,1},{4,3},{6,5},{9,10},{11,12},{13,14},{10,9},... | collective-permute-start | bytes 1253384 | tf_op jit(solution)/shard_map/ppermute | solution.py:504
  79.2 15.9 %collective-permute-start.2 = (f32[256,128]{1,0:T(8,128)S(1)}, f32[256,128]{1,0:T(8,128)S(1)}, u32[]{:S(2)}, u32[]{:S(2)}) collective-permute-start(f32[256,128]{1,0:T(8,128)S(1)} %get-tuple-element.18), channel_id=1, source_target_pairs={{0,8},{16,24},{32,40},{48,56},{64,72},{80,88},{96,104},{112,120},{... | collective-permute-start | bytes 393224 | tf_op jit(solution)/shard_map/ppermute | solution.py:504
  79.9 15.3 %collective-permute-start.3 = (f32[256,128]{1,0:T(8,128)S(1)}, f32[256,128]{1,0:T(8,128)S(1)}, u32[]{:S(2)}, u32[]{:S(2)}) collective-permute-start(f32[256,128]{1,0:T(8,128)S(1)} %get-tuple-element.19), channel_id=1, source_target_pairs={{8,16},{24,32},{40,48},{56,64},{72,80},{88,96},{104,112},{16,8},{3... | collective-permute-start | bytes 393224 | tf_op jit(solution)/shard_map/ppermute | solution.py:504
  86.2 9.0 %collective-permute-start.4 = (f32[256,128]{1,0:T(8,128)S(1)}, f32[256,128]{1,0:T(8,128)S(1)}, u32[]{:S(2)}, u32[]{:S(2)}) collective-permute-start(f32[256,128]{1,0:T(8,128)S(1)} %get-tuple-element.20), channel_id=1, source_target_pairs={{0,8},{16,24},{32,40},{48,56},{64,72},{80,88},{96,104},{112,120},{... | collective-permute-start | bytes 393224 | tf_op jit(solution)/shard_map/ppermute | solution.py:504
  86.8 10.3 %collective-permute-start.5 = (f32[256,128]{1,0:T(8,128)S(1)}, f32[256,128]{1,0:T(8,128)S(1)}, u32[]{:S(2)}, u32[]{:S(2)}) collective-permute-start(f32[256,128]{1,0:T(8,128)S(1)} %get-tuple-element.21), channel_id=1, source_target_pairs={{8,16},{24,32},{40,48},{56,64},{72,80},{88,96},{104,112},{16,8},{3... | collective-permute-start | bytes 393224 | tf_op jit(solution)/shard_map/ppermute | solution.py:504

commit v4 on v3

--- a/solution.py
+++ b/solution.py
@@ -17,6 +17,8 @@
 CANVAS_ROWS = SIDE + 8
 CANVAS_COLS = SIDE + 128
 META = 8
+HALF_COLS = PW // 2
+SLOT = 2 * PH
 GROUP = 4
 KEPT_ROWS = 20 * SIDE
 MIB = 1024 * 1024
@@ -71,19 +73,28 @@
     return jnp.concatenate([taps[:, :, HALF:], gap, taps[:, :, :HALF]], axis=2)
 
 
+def assign_slots(dest, slots):
+    tiles = slots.shape[1]
+    for t in range(tiles):
+        slots[0, t] = -1
+        slots[1, t] = -1
+    for k in range(dest.shape[1]):
+        t = dest[0, k]
+        rank = jnp.where(slots[0, t] >= 0, 1, 0)
+        slots[rank, t] = k
+
+
 def pack_kernel(*refs):
-    given, patches, out, second = refs[:6], refs[6], refs[7], refs[8]
-    scalars, vectors = refs[9:15], refs[15:20]
-    slots, held, meta, small_sems, in_sems, out_sems, meta_sem = refs[20:]
+    given, patches, out = refs[:6], refs[6], refs[7]
+    scalars, vectors = refs[8:14], refs[14:19]
+    slots, held, meta, small_sems, in_sem, out_sems, meta_sem = refs[19:]
     dest, row_offset, col_offset, live, weight, coefs = scalars
     count = patches.shape[0]
     tiles = out.shape[0]
 
-    def bring(k):
-        return pltpu.make_async_copy(patches.at[k], held.at[k], in_sems.at[k])
-
-    def give(k, t):
-        return pltpu.make_async_copy(held.at[k], out.at[t, pl.ds(0, PH)], out_sems.at[k])
+    def give(k, t, half):
+        source = held.at[k, :, pl.ds(half * HALF_COLS, HALF_COLS)]
+        return pltpu.make_async_copy(source, out.at[t, pl.ds(half * PH, PH)], out_sems.at[k, half])
 
     small = [
         pltpu.make_async_copy(source, target, small_sems.at[n])
@@ -91,74 +102,17 @@
     ]
     for copy in small:
         copy.start()
-    for k in range(count):
-        bring(k).start()
+    bring = pltpu.make_async_copy(patches, held, in_sem)
+    bring.start()
+    meta[...] = jnp.zeros_like(meta)
     for copy in small:
         copy.wait()
 
-    def clear(t, carry):
-        slots[0, t] = -1
-        slots[1, t] = -1
-        return carry
-
-    lax.fori_loop(0, tiles, clear, 0)
-
-    def assign(k, carry):
-        t = dest[0, k]
-        rank = jnp.where(slots[0, t] >= 0, 1, 0)
-        slots[rank, t] = k
-        return carry
-
-    lax.fori_loop(0, count, assign, 0)
-
-    meta[...] = jnp.zeros_like(meta)
+    assign_slots(dest, slots)
     for row, values in enumerate(vectors):
         line = values[...].astype(f32)
         for t in range(tiles):
             meta[t, row : row + 1, 0:count] = line
-
-    def forward(k, carry):
-        bring(k).wait()
-        t = dest[0, k]
-
-        @pl.when(slots[0, t] == k)
-        def _():
-            give(k, t).start()
-
-        return carry
-
-    lax.fori_loop(0, count, forward, 0)
-
-    def list_second(t, n):
-        k = slots[1, t]
-
-        @pl.when(k >= 0)
-        def _():
-            second[0, n] = k
-            second[1, n] = t
-
-        return n + jnp.where(k >= 0, 1, 0)
-
-    def fill(j, carry):
-        second[0, j] = 0
-        second[1, j] = 0
-        return carry
-
-    lax.fori_loop(0, tiles, fill, 0)
-    n_second = lax.fori_loop(0, tiles, list_second, 0)
-
-    def repeat_last(j, carry):
-        last = jnp.maximum(n_second - 1, 0)
-
-        @pl.when(j >= n_second)
-        def _():
-            second[0, j] = second[0, last]
-            second[1, j] = second[1, last]
-
-        return carry
-
-    lax.fori_loop(0, tiles, repeat_last, 0)
-    second[2, 0] = n_second
 
     lane = lax.broadcasted_iota(i32, (1, 128), 1)
 
@@ -182,20 +136,26 @@
         return carry
 
     lax.fori_loop(0, tiles, describe, 0, unroll=4)
-
-    about = pltpu.make_async_copy(meta, out.at[:, pl.ds(PH, META)], meta_sem)
+    about = pltpu.make_async_copy(meta, out.at[:, pl.ds(SLOT, META)], meta_sem)
     about.start()
 
-    def finish(k, carry):
+    bring.wait()
+    for k in range(count):
         t = dest[0, k]
 
         @pl.when(slots[0, t] == k)
         def _():
-            give(k, t).wait()
-
-        return carry
-
-    lax.fori_loop(0, count, finish, 0)
+            give(k, t, 0).start()
+            give(k, t, 1).start()
+
+    for k in range(count):
+        t = dest[0, k]
+
+        @pl.when(slots[0, t] == k)
+        def _():
+            give(k, t, 0).wait()
+            give(k, t, 1).wait()
+
     about.wait()
 
 
@@ -203,26 +163,64 @@
     given = (dest, row_offset, col_offset, live_rows, weight, coefficient)
     return pl.pallas_call(
         pack_kernel,
-        out_shape=(
-            jax.ShapeDtypeStruct((tiles, PH + META, PW), f32),
-            jax.ShapeDtypeStruct((3, tiles), i32),
-        ),
+        out_shape=jax.ShapeDtypeStruct((tiles, SLOT + META, HALF_COLS), f32),
         in_specs=[anywhere] * 7,
-        out_specs=(anywhere, smem),
+        out_specs=anywhere,
         scratch_shapes=[pltpu.SMEM(x.shape, x.dtype) for x in given]
         + [pltpu.VMEM(x.shape, x.dtype) for x in given[:5]]
         + [
             pltpu.SMEM((CAP, tiles), i32),
             pltpu.VMEM(patches.shape, f32),
-            pltpu.VMEM((tiles, META, PW), f32),
+            pltpu.VMEM((tiles, META, HALF_COLS), f32),
             pltpu.SemaphoreType.DMA((11,)),
-            pltpu.SemaphoreType.DMA(patches.shape[:1]),
-            pltpu.SemaphoreType.DMA(patches.shape[:1]),
+            pltpu.SemaphoreType.DMA,
+            pltpu.SemaphoreType.DMA((patches.shape[0], 2)),
             pltpu.SemaphoreType.DMA,
         ],
         compiler_params=pltpu.CompilerParams(vmem_limit_bytes=62 * MIB),
         name="pack",
     )(*given, patches)
+
+
+def list_kernel(dest, second, slots):
+    tiles = slots.shape[1]
+    assign_slots(dest, slots)
+    for j in range(tiles):
+        second[0, j] = 0
+        second[1, j] = 0
+
+    def note(t, n):
+        k = slots[1, t]
+
+        @pl.when(k >= 0)
+        def _():
+            second[0, n] = k
+            second[1, n] = t
+
+        return n + jnp.where(k >= 0, 1, 0)
+
+    number = lax.fori_loop(0, tiles, note, 0)
+    last = jnp.maximum(number - 1, 0)
+
+    def repeat_last(j, carry):
+        second[0, j] = second[0, last]
+        second[1, j] = second[1, last]
+        return carry
+
+    lax.fori_loop(number, tiles, repeat_last, 0)
+    for j in range(tiles):
+        second[2, j] = number
+
+
+def list_second(dest, tiles):
+    return pl.pallas_call(
+        list_kernel,
+        out_shape=jax.ShapeDtypeStruct((3, tiles), i32),
+        in_specs=[smem],
+        out_specs=smem,
+        scratch_shapes=[pltpu.SMEM((CAP, tiles), i32)],
+        name="list_second",
+    )(dest)
 
 
 def match(images, coefs, terms, down_high, down_low, across_high, across_low):
@@ -317,7 +315,7 @@
 def first_kernel(slots, group, taps, out, canvas, about, numbers, lines, sem, out_sem, terms, *bands):
     step = pl.program_id(0)
     tiles = slots.shape[0]
-    told = pltpu.make_async_copy(slots.at[:, pl.ds(PH, META), pl.ds(0, 128)], about, sem)
+    told = pltpu.make_async_copy(slots.at[:, pl.ds(SLOT, META)], about, sem)
 
     @pl.when(step == 0)
     def _():
@@ -327,13 +325,14 @@
 
     images, coefs, masks = [], [], []
     for g in range(GROUP):
-        lines[pl.ds(step * GROUP + g, 1), :] = group[g, PH + 6 : PH + 7, 0:128]
-        line = group[g, PH + 6 : PH + 7, 0:8]
+        lines[pl.ds(step * GROUP + g, 1), :] = group[g, SLOT + 6 : SLOT + 7, :]
+        line = group[g, SLOT + 6 : SLOT + 7, 0:8]
         rows = jnp.broadcast_to(line[:, 3:4] * line[:, 0:1], (PH, PW)).astype(i32)
         mask = live_mask(rows)
         masks.append(mask)
-        images.append(jnp.where(mask, group[g, :PH, :], 0.0))
-        line = group[g, PH + 5 : PH + 6, 0:NB]
+        image = jnp.concatenate([group[g, :PH, :], group[g, PH:SLOT, :]], axis=1)
+        images.append(jnp.where(mask, image, 0.0))
+        line = group[g, SLOT + 5 : SLOT + 6, 0:NB]
         coefs.append([line[:, b : b + 1] for b in range(NB)])
     matched = match(images, coefs, terms, *bands)
 
@@ -372,7 +371,7 @@
         grid=(tiles // GROUP,),
         in_specs=[
             anywhere,
-            pl.BlockSpec((GROUP, PH + META, PW), lambda s: (s, 0, 0)),
+            pl.BlockSpec((GROUP, SLOT + META, HALF_COLS), lambda s: (s, 0, 0)),
             whole((2, NB, PW + 128)),
         ],
         out_specs=anywhere,
@@ -564,17 +563,18 @@
 def per_device(patches, dest, row_offset, col_offset, live_rows, weight, coefficient, basis):
     tiles = lax.axis_size("skyx")
     images = patches[0]
-    outgoing, second = pack(
+    outgoing = pack(
         images, dest[:, :, 0], row_offset, col_offset, live_rows, weight, coefficient[0].T, tiles
     )
     arrived = lax.all_to_all(outgoing, "skyx", split_axis=0, concat_axis=0, tiled=True)
     taps = spread_taps(basis)
+    second = list_second(dest[:, :, 0], tiles)
     late = match_second(second, coefficient[0].T, live_rows, weight, row_offset, col_offset, images, taps, tiles)
     late = lax.all_to_all(late, "skyx", split_axis=0, concat_axis=0, tiled=True)
 
     kept = match_first(arrived, taps)
 
-    about = arrived[:, PH : PH + 5, : images.shape[0]]
+    about = arrived[:, SLOT : SLOT + 5, : images.shape[0]]
     band = jnp.transpose(about, (1, 0, 2)).reshape(5, -1)
     left = band[2] + (band[0] - lax.axis_index("skyx").astype(f32)) * TILE
     own = jnp.pad(jnp.stack([band[1], left, band[3], band[4]]), ((0, META - 4), (0, 0)))

time: 99.6 us -> 97.4 us (0.978)
  waiting for transfers between devices: 31.3 us -> 27.7 us
  Pallas kernels: 31 us -> 32.6 us
    all_to_all x1, waiting for transfers between devices: 22.9 us -> 19.7 us  [per_device(): lax.all_to_all(outgoing, 'skyx', split_axis=0, concat_axis=0, tiled=True)]
    pallas_call x1 -> x2, Pallas kernels: 4.01 us -> 5.04 us  [the longest x1 3.32 us: pack(): pl.pallas_call(pack_kernel, out_shape=jax.ShapeDtypeStruct((tiles, SLOT +...]
  transfers between devices with their start and end apart: 8 -> 8, of which waited for: 3 -> 4; matrix products, arithmetic and copies ran while one was open for 2% -> 2% of each run, Pallas kernels for 24% -> 27%
where the time goes in v4:
time: 97.4 us; the launch traced here: 97 us
  Pallas kernels  32.6 us (33%)
  starting transfers between devices  32.2 us (33%)
  waiting for transfers between devices  27.7 us (28%)
  local copies, waits for them, and re-layouts  3.34 us (3%)
    all_to_all x1, waiting for transfers between devices, per_device(): lax.all_to_all(outgoing, 'skyx', split_axis=0, concat_axis=0, tiled=True)  19.7 us
    pallas_call x1, Pallas kernels, match_first(): pl.pallas_call(first_kernel, out_shape=jax.ShapeDtypeStruct((KEPT_ROWS, S...  17.8 us
    ppermute x6, starting transfers between devices, exchange(): return lax.ppermute(block, axis, pairs + [(j, i) for i, j in pairs])  16.1 us
    all_to_all x1, starting transfers between devices, per_device(): lax.all_to_all(outgoing, 'skyx', split_axis=0, concat_axis=0, tiled=True)  8.48 us
    all_to_all x1, starting transfers between devices, per_device(): late = lax.all_to_all(late, 'skyx', split_axis=0, concat_axis=0, tiled=True)  7.58 us
    all_to_all x1, waiting for transfers between devices, per_device(): late = lax.all_to_all(late, 'skyx', split_axis=0, concat_axis=0, tiled=True)  5.89 us
    pallas_call x1, Pallas kernels, match_second(): pl.pallas_call(second_kernel, out_shape=jax.ShapeDtypeStruct((tiles, PH,...  4.25 us
    pallas_call x1, Pallas kernels, pack(): pl.pallas_call(pack_kernel, out_shape=jax.ShapeDtypeStruct((tiles, SLOT +...  3.32 us
  transfers between devices with their start and end apart: 8, of which 4 were waited for; matrix products, arithmetic and copies ran while one was open for 2% of the time, Pallas kernels for 27%

profile of v4, /device:TPU:10, one launch (start us, length us, event | category | flops | bytes accessed | tf_op | source)
XLA Modules:
  0.0 97.0 jit_solution(1735204198125529448)
XLA Ops:
  0.6 3.3 %pack.1 = f32[16,264,128]{2,1,0:T(8,128)} custom-call(s32[1,16]{1,0:T(1,128)} %bitcast.16, s32[1,16]{1,0:T(1,128)} %row_offset.1, s32[1,16]{1,0:T(1,128)} %col_offset.1, s32[1,16]{1,0:T(1,128)} %live.1, f32[1,16]{1,0:T(1,128)} %weight.1, f32[8,16]{1,0:T(8,128)} %bitcast.12, f32[16,128,256]{2,1,0:T(8,128)} %bitcast.10), custom_call_target="tpu_custom_call" | custom-call | tf_op jit(solution)/shard_map/pack/pallas_call | solution.py:164
  4.0 0.0 copy-start.9
  4.0 8.5 %all-to-all-start = ((f32[16,264,128]{2,1,0:T(8,128)}), f32[16,264,128]{2,1,0:T(8,128)}, u32[]{:S(2)}, u32[]{:S(2)}) async-start(f32[16,264,128]{2,1,0:T(8,128)} %pack.1), calls=%async_computation | async-start | bytes 4325376 | tf_op jit(solution)/shard_map/all_to_all | solution.py:569
  12.5 1.7 %list_second.1.second = s32[3,16]{1,0:T(4,128)} custom-call(s32[1,16]{1,0:T(1,128)} %bitcast.17), custom_call_target="tpu_custom_call" | custom-call | tf_op jit(solution)/shard_map/list_second/pallas_call | solution.py:216
  14.3 0.1 rev.3
  14.3 0.1 pad.10.clone
  14.4 0.1 slice_maximum_fusion
  14.5 0.1 fusion.taps
  14.6 0.7 copy-done.4
  15.3 4.3 %match_second.1 = f32[16,128,256]{2,1,0:T(8,128)S(1)} custom-call(s32[3,16]{1,0:T(4,128)S(1)} %copy-done.4, f32[8,16]{1,0:T(8,128)S(1)} %bitcast.13, s32[1,16]{1,0:T(1,128)S(1)} %copy-done.7, f32[1,16]{1,0:T(1,128)S(1)} %copy-done.8, s32[1,16]{1,0:T(1,128)S(1)} %copy-done.5, s32[1,16]{1,0:T(1,128)S(1)} %copy-done.6, f32[16,128,256]{2,1,0:T(8,128)S(1)} %bitcast.11, ...), custom_call_target="tpu_custom_call" | custom-call | flops 5000000000 | bytes 6000000 | tf_op jit(solution)/shard_map/match_second/pallas_call | solution.py:268
  19.6 1.3 %copy-done.1 = f32[16,128,256]{2,1,0:T(8,128)} copy-done((f32[16,128,256]{2,1,0:T(8,128)}, f32[16,128,256]{2,1,0:T(8,128)S(1)}, u32[]{:S(2)}) %copy-start.1) | copy-done | bytes 2097176
  20.9 19.7 %all-to-all-done.slots.group = f32[16,264,128]{2,1,0:T(8,128)} async-done(((f32[16,264,128]{2,1,0:T(8,128)}), f32[16,264,128]{2,1,0:T(8,128)}, u32[]{:S(2)}, u32[]{:S(2)}) %all-to-all-start) | async-done | bytes 2162720 | tf_op jit(solution)/shard_map/all_to_all | solution.py:569
  40.5 7.6 %all-to-all-start.1 = ((f32[16,128,256]{2,1,0:T(8,128)}), f32[16,128,256]{2,1,0:T(8,128)}, u32[]{:S(2)}, u32[]{:S(2)}) async-start(f32[16,128,256]{2,1,0:T(8,128)} %copy-done.1), calls=%async_computation.1 | async-start | bytes 4194304 | tf_op jit(solution)/shard_map/all_to_all | solution.py:573
  48.1 0.8 slice_bitcast_fusion
  49.0 0.1 slice_reduce_fusion.2
  49.1 0.1 slice.47
  49.1 0.1 slice.51
  49.2 0.1 add.16
  49.3 0.1 slice.53
  49.4 17.8 %match_first.1.kept = f32[15360,768]{1,0:T(8,128)} custom-call(f32[16,264,128]{2,1,0:T(8,128)} %all-to-all-done.slots.group, f32[16,264,128]{2,1,0:T(8,128)} %all-to-all-done.slots.group, f32[2,8,384]{2,1,0:T(8,128)} %copy-done.2), custom_call_target="tpu_custom_call" | custom-call | flops 10000000000 | bytes 8000000 | tf_op jit(solution)/shard_map/match_first/pallas_call | solution.py:368
  67.2 5.9 %all-to-all-done.1.slots = f32[16,128,256]{2,1,0:T(8,128)} async-done(((f32[16,128,256]{2,1,0:T(8,128)}), f32[16,128,256]{2,1,0:T(8,128)}, u32[]{:S(2)}, u32[]{:S(2)}) %all-to-all-start.1) | async-done | bytes 2097184 | tf_op jit(solution)/shard_map/all_to_all | solution.py:573
  73.1 2.1 %place_second.1 = (f32[136,768]{1,0:T(8,128)S(1)}, f32[136,768]{1,0:T(8,128)S(1)}, f32[512,768]{1,0:T(8,128)S(1)}, f32[256,128]{1,0:T(8,128)S(1)}, f32[256,128]{1,0:T(8,128)S(1)}) custom-call(f32[15360,768]{1,0:T(8,128)} %match_first.1.kept, f32[8,256]{1,0:T(8,128)S(1)} %select_maximum_fusion.band.own, f32[16,128,256]{2,1,0:T(8,128)} %all-to-all-done.1.slots), custom_call_target="tpu_custom_call" | custom-call | tf_op jit(solution)/shard_map/place_second/pallas_call | solution.py:452
  75.2 0.1 collective-permute-start
  75.3 2.4 %collective-permute-start.1 = (f32[136,768]{1,0:T(8,128)S(1)}, f32[136,768]{1,0:T(8,128)S(1)}, u32[]{:S(2)}, u32[]{:S(2)}) collective-permute-start(f32[136,768]{1,0:T(8,128)S(1)} %get-tuple-element.13), channel_id=1, source_target_pairs={{1,2},{3,4},{5,6},{2,1},{4,3},{6,5},{9,10},{11,12},{13,14},{10,9},... | collective-permute-start | bytes 1253384 | tf_op jit(solution)/shard_map/ppermute | solution.py:503
  77.7 0.7 collective-permute-start.2
  78.3 6.2 %collective-permute-start.3 = (f32[256,128]{1,0:T(8,128)S(1)}, f32[256,128]{1,0:T(8,128)S(1)}, u32[]{:S(2)}, u32[]{:S(2)}) collective-permute-start(f32[256,128]{1,0:T(8,128)S(1)} %get-tuple-element.15), channel_id=1, source_target_pairs={{8,16},{24,32},{40,48},{56,64},{72,80},{88,96},{104,112},{16,8},{3... | collective-permute-start | bytes 393224 | tf_op jit(solution)/shard_map/ppermute | solution.py:503
  84.5 0.1 collective-permute-done.1.rows_last
  84.7 0.7 collective-permute-start.4
  85.3 6.2 %collective-permute-start.5 = (f32[256,128]{1,0:T(8,128)S(1)}, f32[256,128]{1,0:T(8,128)S(1)}, u32[]{:S(2)}, u32[]{:S(2)}) collective-permute-start(f32[256,128]{1,0:T(8,128)S(1)} %get-tuple-element.17), channel_id=1, source_target_pairs={{8,16},{24,32},{40,48},{56,64},{72,80},{88,96},{104,112},{16,8},{3... | collective-permute-start | bytes 393224 | tf_op jit(solution)/shard_map/ppermute | solution.py:503
  91.5 2.1 %make_depth.1 = (f32[512,512]{1,0:T(8,128)}, f32[512,512]{1,0:T(8,128)S(1)}) custom-call(f32[8,256]{1,0:T(8,128)S(1)} %select_maximum_fusion.band.own, f32[136,768]{1,0:T(8,128)S(1)} %collective-permute-done.rows_next, f32[136,768]{1,0:T(8,128)S(1)} %collective-permute-done.1.rows_last), custom_call_target="tpu_custom_call" | custom-call | flops 1000000000 | bytes 1000000 | tf_op jit(solution)/shard_map/make_depth/pallas_call | solution.py:490
  93.7 2.0 %collective-permute-done.5.outer_last = f32[256,128]{1,0:T(8,128)S(1)} collective-permute-done((f32[256,128]{1,0:T(8,128)S(1)}, f32[256,128]{1,0:T(8,128)S(1)}, u32[]{:S(2)}, u32[]{:S(2)}) %collective-permute-start.5) | collective-permute-done | bytes 131104 | tf_op jit(solution)/shard_map/ppermute | solution.py:503
  95.7 1.3 %make_coadd.1 = f32[512,512]{1,0:T(8,128)} custom-call(f32[512,768]{1,0:T(8,128)S(1)} %get-tuple-element.11.middle, f32[136,768]{1,0:T(8,128)S(1)} %collective-permute-done.rows_next, f32[136,768]{1,0:T(8,128)S(1)} %collective-permute-done.1.rows_last, f32[256,128]{1,0:T(8,128)S(1)} %collective-permute-done.2.inner_next, ...), custom_call_target="tpu_custom_call" | custom-call | tf_op jit(solution)/shard_map/make_coadd/pallas_call | solution.py:553
  (25 shorter events, 0.1 us)
Async XLA Ops:
  4.0 10.3 %copy-start.9 = (f32[2,8,41]{2,1,0:T(8,128)S(1)}, f32[2,8,41]{2,1,0:T(8,128)}, u32[]{:S(2)}) copy-start(f32[2,8,41]{2,1,0:T(8,128)} %param.15) | copy-start | bytes 7876
  4.0 10.6 %copy-start = (f32[1,16,128,256]{3,2,1,0:T(8,128)S(1)}, f32[1,16,128,256]{3,2,1,0:T(8,128)}, u32[]{:S(2)}) copy-start(f32[1,16,128,256]{3,2,1,0:T(8,128)} %param.8) | copy-start | bytes 6291460
  4.0 10.6 %copy-start.3 = (f32[1,16,8]{1,2,0:T(8,128)S(1)}, f32[1,16,8]{1,2,0:T(8,128)}, u32[]{:S(2)}) copy-start(f32[1,16,8]{1,2,0:T(8,128)} %param.14) | copy-start | bytes 1540
  4.0 10.6 %copy-start.5 = (s32[1,16]{1,0:T(1,128)S(1)}, s32[1,16]{1,0:T(1,128)}, u32[]{:S(2)}) copy-start(s32[1,16]{1,0:T(1,128)} %row_offset.1) | copy-start | bytes 196
  4.0 10.6 %copy-start.6 = (s32[1,16]{1,0:T(1,128)S(1)}, s32[1,16]{1,0:T(1,128)}, u32[]{:S(2)}) copy-start(s32[1,16]{1,0:T(1,128)} %col_offset.1) | copy-start | bytes 196
  4.0 10.6 %copy-start.7 = (s32[1,16]{1,0:T(1,128)S(1)}, s32[1,16]{1,0:T(1,128)}, u32[]{:S(2)}) copy-start(s32[1,16]{1,0:T(1,128)} %live.1) | copy-start | bytes 196
  4.0 10.6 %copy-start.8 = (f32[1,16]{1,0:T(1,128)S(1)}, f32[1,16]{1,0:T(1,128)}, u32[]{:S(2)}) copy-start(f32[1,16]{1,0:T(1,128)} %weight.1) | copy-start | bytes 196
  4.0 36.5 %all-to-all-start = ((f32[16,264,128]{2,1,0:T(8,128)}), f32[16,264,128]{2,1,0:T(8,128)}, u32[]{:S(2)}, u32[]{:S(2)}) async-start(f32[16,264,128]{2,1,0:T(8,128)} %pack.1), calls=%async_computation | async-start | bytes 4325376 | tf_op jit(solution)/shard_map/all_to_all | solution.py:569
  14.6 0.7 copy-start.4
  15.3 4.3 %copy-start.2 = (f32[2,8,384]{2,1,0:T(8,128)}, f32[2,8,384]{2,1,0:T(8,128)S(1)}, u32[]{:S(2)}) copy-start(f32[2,8,384]{2,1,0:T(8,128)S(1)} %fusion.taps) | copy-start | bytes 73732
  19.6 1.3 %copy-start.1 = (f32[16,128,256]{2,1,0:T(8,128)}, f32[16,128,256]{2,1,0:T(8,128)S(1)}, u32[]{:S(2)}) copy-start(f32[16,128,256]{2,1,0:T(8,128)S(1)} %match_second.1) | copy-start | bytes 6291460
  40.5 32.5 %all-to-all-start.1 = ((f32[16,128,256]{2,1,0:T(8,128)}), f32[16,128,256]{2,1,0:T(8,128)}, u32[]{:S(2)}, u32[]{:S(2)}) async-start(f32[16,128,256]{2,1,0:T(8,128)} %copy-done.1), calls=%async_computation.1 | async-start | bytes 4194304 | tf_op jit(solution)/shard_map/all_to_all | solution.py:573
  75.2 9.3 %collective-permute-start = (f32[136,768]{1,0:T(8,128)S(1)}, f32[136,768]{1,0:T(8,128)S(1)}, u32[]{:S(2)}, u32[]{:S(2)}) collective-permute-start(f32[136,768]{1,0:T(8,128)S(1)} %get-tuple-element.12), channel_id=1, source_target_pairs={{0,1},{2,3},{4,5},{6,7},{1,0},{3,2},{5,4},{7,6},{8,9},{10,11},{12,... | collective-permute-start | bytes 1253384 | tf_op jit(solution)/shard_map/ppermute | solution.py:503
  75.3 9.4 %collective-permute-start.1 = (f32[136,768]{1,0:T(8,128)S(1)}, f32[136,768]{1,0:T(8,128)S(1)}, u32[]{:S(2)}, u32[]{:S(2)}) collective-permute-start(f32[136,768]{1,0:T(8,128)S(1)} %get-tuple-element.13), channel_id=1, source_target_pairs={{1,2},{3,4},{5,6},{2,1},{4,3},{6,5},{9,10},{11,12},{13,14},{10,9},... | collective-permute-start | bytes 1253384 | tf_op jit(solution)/shard_map/ppermute | solution.py:503
  77.7 16.0 %collective-permute-start.2 = (f32[256,128]{1,0:T(8,128)S(1)}, f32[256,128]{1,0:T(8,128)S(1)}, u32[]{:S(2)}, u32[]{:S(2)}) collective-permute-start(f32[256,128]{1,0:T(8,128)S(1)} %get-tuple-element.14), channel_id=1, source_target_pairs={{0,8},{16,24},{32,40},{48,56},{64,72},{80,88},{96,104},{112,120},{... | collective-permute-start | bytes 393224 | tf_op jit(solution)/shard_map/ppermute | solution.py:503
  78.3 15.3 %collective-permute-start.3 = (f32[256,128]{1,0:T(8,128)S(1)}, f32[256,128]{1,0:T(8,128)S(1)}, u32[]{:S(2)}, u32[]{:S(2)}) collective-permute-start(f32[256,128]{1,0:T(8,128)S(1)} %get-tuple-element.15), channel_id=1, source_target_pairs={{8,16},{24,32},{40,48},{56,64},{72,80},{88,96},{104,112},{16,8},{3... | collective-permute-start | bytes 393224 | tf_op jit(solution)/shard_map/ppermute | solution.py:503
  84.7 9.0 %collective-permute-start.4 = (f32[256,128]{1,0:T(8,128)S(1)}, f32[256,128]{1,0:T(8,128)S(1)}, u32[]{:S(2)}, u32[]{:S(2)}) collective-permute-start(f32[256,128]{1,0:T(8,128)S(1)} %get-tuple-element.16), channel_id=1, source_target_pairs={{0,8},{16,24},{32,40},{48,56},{64,72},{80,88},{96,104},{112,120},{... | collective-permute-start | bytes 393224 | tf_op jit(solution)/shard_map/ppermute | solution.py:503
  85.3 10.3 %collective-permute-start.5 = (f32[256,128]{1,0:T(8,128)S(1)}, f32[256,128]{1,0:T(8,128)S(1)}, u32[]{:S(2)}, u32[]{:S(2)}) collective-permute-start(f32[256,128]{1,0:T(8,128)S(1)} %get-tuple-element.17), channel_id=1, source_target_pairs={{8,16},{24,32},{40,48},{56,64},{72,80},{88,96},{104,112},{16,8},{3... | collective-permute-start | bytes 393224 | tf_op jit(solution)/shard_map/ppermute | solution.py:503

commit v5 on v4

--- a/solution.py
+++ b/solution.py
@@ -385,53 +385,46 @@
             pltpu.VMEM((2 * GROUP * PH, NB * PW), bf16),
         ]
         + BANDS,
-        compiler_params=pltpu.CompilerParams(vmem_limit_bytes=62 * MIB),
+        compiler_params=pltpu.CompilerParams(vmem_limit_bytes=61 * MIB),
         cost_estimate=pl.CostEstimate(flops=10_000_000_000, bytes_accessed=8_000_000, transcendentals=0),
         name="match_first",
     )(slots, slots, taps)
 
 
-def second_place_kernel(
-    kept, band, slots, rows_next, rows_last, middle, cols_next, cols_last,
-    told, numbers, canvas, held, base, sems, base_sem, told_sem,
-):
+LOW, HIGH = slice(0, MARGIN), slice(MARGIN + TILE, SIDE)
+CORE, INNER, ALL = slice(MARGIN, MARGIN + TILE), slice(2 * MARGIN, TILE), slice(0, SIDE)
+STRIPS = ((LOW, ALL), (HIGH, ALL), (INNER, LOW), (INNER, HIGH))
+
+
+def place_slots(kept, slots, parts, told, canvas, base, told_sem, base_sems):
     tiles = slots.shape[0]
-
-    def bring(t):
-        return pltpu.make_async_copy(slots.at[t], held.at[t], sems.at[t])
-
     tell = pltpu.make_async_copy(kept.at[pl.ds(SIDE, tiles), pl.ds(0, 128)], told, told_sem)
     tell.start()
-    copy = pltpu.make_async_copy(kept.at[pl.ds(0, SIDE)], base, base_sem)
-    copy.start()
+    copies = []
+    for n, (rows, cols) in enumerate(parts):
+        at = pl.ds(rows.start, rows.stop - rows.start), pl.ds(cols.start, cols.stop - cols.start)
+        copies.append(pltpu.make_async_copy(kept.at[at], base.at[at], base_sems.at[n]))
+        copies[-1].start()
     canvas[...] = jnp.zeros_like(canvas)
     tell.wait()
 
-    def fetch(t, carry):
-        for place in range(4, 7):
-            numbers[t, place] = told[t, place].astype(i32)
-
-        @pl.when(numbers[t, 4] > 0)
+    def add(t, carry):
+        @pl.when(told[t, 4] > 0)
         def _():
-            bring(t).start()
+            corner = told[t, 5].astype(i32) + MARGIN, told[t, 6].astype(i32) + MARGIN
+            add_turned(canvas, slots[t], *corner)
 
         return carry
 
-    lax.fori_loop(0, tiles, fetch, 0)
-
-    def add(t, carry):
-        @pl.when(numbers[t, 4] > 0)
-        def _():
-            bring(t).wait()
-            add_turned(canvas, held[t], numbers[t, 5] + MARGIN, numbers[t, 6] + MARGIN)
-
-        return carry
-
     lax.fori_loop(0, tiles, add, 0)
-    copy.wait()
-    low, high = slice(0, MARGIN), slice(MARGIN + TILE, SIDE)
-    core, inner = slice(MARGIN, MARGIN + TILE), slice(2 * MARGIN, TILE)
-    middle[...] = base[core] + canvas[core, :SIDE]
+    for copy in copies:
+        copy.wait()
+
+
+def strips_kernel(
+    kept, band, slots, rows_next, rows_last, cols_next, cols_last, told, canvas, base, told_sem, base_sems
+):
+    place_slots(kept, slots, STRIPS, told, canvas, base, told_sem, base_sems)
     for out in (rows_next, rows_last):
         out[MARGIN:] = jnp.zeros((META, SIDE), f32)
         out[MARGIN:, : band.shape[1]] = band[...]
@@ -440,33 +433,51 @@
 
             @pl.when(lax.axis_index(axis) % 2 == parity)
             def _():
-                for out, strip in zip(outs, (high, low) if parity == 0 else (low, high)):
-                    rows, cols = (strip, slice(0, SIDE)) if axis == "skyy" else (inner, strip)
+                for out, strip in zip(outs, (HIGH, LOW) if parity == 0 else (LOW, HIGH)):
+                    rows, cols = (strip, ALL) if axis == "skyy" else (INNER, strip)
                     out[: rows.stop - rows.start] = base[rows, cols] + canvas[rows, cols]
 
 
-def place_second(kept, band, slots):
-    tiles = slots.shape[0]
+def place_scratch(slots, parts):
+    return [
+        pltpu.SMEM((slots.shape[0], 128), f32),
+        pltpu.VMEM((CANVAS_ROWS, CANVAS_COLS), f32),
+        pltpu.VMEM((SIDE, SIDE), f32),
+        pltpu.SemaphoreType.DMA,
+        pltpu.SemaphoreType.DMA((parts,)),
+    ]
+
+
+def make_strips(kept, band, slots):
     strip = jax.ShapeDtypeStruct((MARGIN + META, SIDE), f32)
     side = jax.ShapeDtypeStruct((TILE - 2 * MARGIN, MARGIN), f32)
     return pl.pallas_call(
-        second_place_kernel,
-        out_shape=(strip, strip, jax.ShapeDtypeStruct((TILE, SIDE), f32), side, side),
-        in_specs=[anywhere, vmem, anywhere],
-        out_specs=(vmem,) * 5,
-        scratch_shapes=[
-            pltpu.SMEM((tiles, 128), f32),
-            pltpu.SMEM((tiles, 8), i32),
-            pltpu.VMEM((CANVAS_ROWS, CANVAS_COLS), f32),
-            pltpu.VMEM(slots.shape, f32),
-            pltpu.VMEM((SIDE, SIDE), f32),
-            pltpu.SemaphoreType.DMA(slots.shape[:1]),
-            pltpu.SemaphoreType.DMA,
-            pltpu.SemaphoreType.DMA,
-        ],
+        strips_kernel,
+        out_shape=(strip, strip, side, side),
+        in_specs=[anywhere, vmem, vmem],
+        out_specs=(vmem,) * 4,
+        scratch_shapes=place_scratch(slots, len(STRIPS)),
         compiler_params=pltpu.CompilerParams(vmem_limit_bytes=20 * MIB),
         name="place_second",
     )(kept, band, slots)
+
+
+def middle_kernel(kept, slots, middle, told, canvas, base, told_sem, base_sems):
+    place_slots(kept, slots, ((CORE, ALL),), told, canvas, base, told_sem, base_sems)
+    middle[...] = base[CORE] + canvas[CORE, :SIDE]
+
+
+def make_middle(kept, slots):
+    return pl.pallas_call(
+        middle_kernel,
+        out_shape=jax.ShapeDtypeStruct((TILE, SIDE), f32),
+        in_specs=[anywhere, vmem],
+        out_specs=vmem,
+        scratch_shapes=place_scratch(slots, 1),
+        compiler_params=pltpu.CompilerParams(vmem_limit_bytes=20 * MIB),
+        cost_estimate=pl.CostEstimate(flops=400_000, bytes_accessed=4_000_000, transcendentals=0),
+        name="make_middle",
+    )(kept, slots)
 
 
 def depth_kernel(own, rows_next, rows_last, depth, divisor):
@@ -579,11 +590,12 @@
     left = band[2] + (band[0] - lax.axis_index("skyx").astype(f32)) * TILE
     own = jnp.pad(jnp.stack([band[1], left, band[3], band[4]]), ((0, META - 4), (0, 0)))
 
-    rows_next, rows_last, middle, cols_next, cols_last = place_second(kept, own, late)
+    rows_next, rows_last, cols_next, cols_last = make_strips(kept, own, late)
     rows_last = exchange(rows_last, "skyy", 1)
     rows_next = exchange(rows_next, "skyy", 0)
     inner_last = exchange(cols_last, "skyx", 1)
     inner_next = exchange(cols_next, "skyx", 0)
+    middle = make_middle(kept, late)
     cols_next, cols_last = make_edges(middle, rows_next, rows_last)
     outer_last = exchange(cols_last, "skyx", 1)
     outer_next = exchange(cols_next, "skyx", 0)

time: 97.4 us -> 96 us (0.986)
  starting transfers between devices: 32.2 us -> 28.7 us
    ppermute x6, starting transfers between devices: 16.1 us -> 13.4 us  [exchange(): return lax.ppermute(block, axis, pairs + [(j, i) for i, j in pairs])]
    pallas_call x1 -> x2, Pallas kernels: 2.1 us -> 2.93 us  [the longest x1 1.58 us: make_middle(): pl.pallas_call(middle_kernel, out_shape=jax.ShapeDtypeStruct((TILE, SIDE)...]
  transfers between devices with their start and end apart: 8 -> 8, of which waited for: 4 -> 3; matrix products, arithmetic and copies ran while one was open for 2% -> 2% of each run, Pallas kernels for 27% -> 29%
where the time goes in v5:
time: 96 us; the launch traced here: 95.3 us
  Pallas kernels  33.4 us (35%)
  starting transfers between devices  28.7 us (30%)
  waiting for transfers between devices  28.6 us (30%)
  local copies, waits for them, and re-layouts  3.34 us (3%)
    all_to_all x1, waiting for transfers between devices, per_device(): lax.all_to_all(outgoing, 'skyx', split_axis=0, concat_axis=0, tiled=True)  19.8 us
    pallas_call x1, Pallas kernels, match_first(): pl.pallas_call(first_kernel, out_shape=jax.ShapeDtypeStruct((KEPT_ROWS, S...  17.8 us
    ppermute x6, starting transfers between devices, exchange(): return lax.ppermute(block, axis, pairs + [(j, i) for i, j in pairs])  13.4 us
    all_to_all x1, starting transfers between devices, per_device(): lax.all_to_all(outgoing, 'skyx', split_axis=0, concat_axis=0, tiled=True)  8.44 us
    all_to_all x1, starting transfers between devices, per_device(): late = lax.all_to_all(late, 'skyx', split_axis=0, concat_axis=0, tiled=True)  6.87 us
    all_to_all x1, waiting for transfers between devices, per_device(): late = lax.all_to_all(late, 'skyx', split_axis=0, concat_axis=0, tiled=True)  5.95 us
    pallas_call x1, Pallas kernels, match_second(): pl.pallas_call(second_kernel, out_shape=jax.ShapeDtypeStruct((tiles, PH,...  4.25 us
    pallas_call x1, Pallas kernels, pack(): pl.pallas_call(pack_kernel, out_shape=jax.ShapeDtypeStruct((tiles, SLOT +...  3.33 us
  transfers between devices with their start and end apart: 8, of which 3 were waited for; matrix products, arithmetic and copies ran while one was open for 2% of the time, Pallas kernels for 29%

profile of v5, /device:TPU:10, one launch (start us, length us, event | category | flops | bytes accessed | tf_op | source)
XLA Modules:
  0.0 95.3 jit_solution(12735062381015385884)
XLA Ops:
  0.6 3.3 %pack.1 = f32[16,264,128]{2,1,0:T(8,128)} custom-call(s32[1,16]{1,0:T(1,128)} %bitcast.16, s32[1,16]{1,0:T(1,128)} %row_offset.1, s32[1,16]{1,0:T(1,128)} %col_offset.1, s32[1,16]{1,0:T(1,128)} %live.1, f32[1,16]{1,0:T(1,128)} %weight.1, f32[8,16]{1,0:T(8,128)} %bitcast.12, f32[16,128,256]{2,1,0:T(8,128)} %bitcast.10), custom_call_target="tpu_custom_call" | custom-call | tf_op jit(solution)/shard_map/pack/pallas_call | solution.py:164
  4.0 8.4 %all-to-all-start = ((f32[16,264,128]{2,1,0:T(8,128)}), f32[16,264,128]{2,1,0:T(8,128)}, u32[]{:S(2)}, u32[]{:S(2)}) async-start(f32[16,264,128]{2,1,0:T(8,128)} %pack.1), calls=%async_computation | async-start | bytes 4325376 | tf_op jit(solution)/shard_map/all_to_all | solution.py:580
  12.5 1.7 %list_second.1.second = s32[3,16]{1,0:T(4,128)} custom-call(s32[1,16]{1,0:T(1,128)} %bitcast.17), custom_call_target="tpu_custom_call" | custom-call | tf_op jit(solution)/shard_map/list_second/pallas_call | solution.py:216
  14.2 0.1 rev.3
  14.3 0.1 pad.10.clone
  14.4 0.1 slice_maximum_fusion
  14.5 0.1 fusion.taps
  14.6 0.7 copy-done.4
  15.3 4.2 %match_second.1 = f32[16,128,256]{2,1,0:T(8,128)S(1)} custom-call(s32[3,16]{1,0:T(4,128)S(1)} %copy-done.4, f32[8,16]{1,0:T(8,128)S(1)} %bitcast.13, s32[1,16]{1,0:T(1,128)S(1)} %copy-done.7, f32[1,16]{1,0:T(1,128)S(1)} %copy-done.8, s32[1,16]{1,0:T(1,128)S(1)} %copy-done.5, s32[1,16]{1,0:T(1,128)S(1)} %copy-done.6, f32[16,128,256]{2,1,0:T(8,128)S(1)} %bitcast.11, ...), custom_call_target="tpu_custom_call" | custom-call | flops 5000000000 | bytes 6000000 | tf_op jit(solution)/shard_map/match_second/pallas_call | solution.py:268
  19.6 1.3 %copy-done.1 = f32[16,128,256]{2,1,0:T(8,128)} copy-done((f32[16,128,256]{2,1,0:T(8,128)}, f32[16,128,256]{2,1,0:T(8,128)S(1)}, u32[]{:S(2)}) %copy-start.1) | copy-done | bytes 2097176
  20.8 19.8 %all-to-all-done.slots.group = f32[16,264,128]{2,1,0:T(8,128)} async-done(((f32[16,264,128]{2,1,0:T(8,128)}), f32[16,264,128]{2,1,0:T(8,128)}, u32[]{:S(2)}, u32[]{:S(2)}) %all-to-all-start) | async-done | bytes 2162720 | tf_op jit(solution)/shard_map/all_to_all | solution.py:580
  40.6 6.9 %all-to-all-start.1 = ((f32[16,128,256]{2,1,0:T(8,128)}), f32[16,128,256]{2,1,0:T(8,128)S(1)}, u32[]{:S(2)}, u32[]{:S(2)}) async-start(f32[16,128,256]{2,1,0:T(8,128)} %copy-done.1), calls=%async_computation.1 | async-start | bytes 4194304 | tf_op jit(solution)/shard_map/all_to_all | solution.py:584
  47.5 0.8 slice_bitcast_fusion
  48.3 0.1 slice_reduce_fusion.2
  48.4 0.1 slice.47
  48.5 0.1 slice.51
  48.6 0.1 add.16
  48.7 0.1 slice.53
  48.8 17.8 %match_first.1.kept = f32[15360,768]{1,0:T(8,128)} custom-call(f32[16,264,128]{2,1,0:T(8,128)} %all-to-all-done.slots.group, f32[16,264,128]{2,1,0:T(8,128)} %all-to-all-done.slots.group, f32[2,8,384]{2,1,0:T(8,128)} %copy-done.2), custom_call_target="tpu_custom_call" | custom-call | flops 10000000000 | bytes 8000000 | tf_op jit(solution)/shard_map/match_first/pallas_call | solution.py:368
  66.5 6.0 %all-to-all-done.1.slots = f32[16,128,256]{2,1,0:T(8,128)S(1)} async-done(((f32[16,128,256]{2,1,0:T(8,128)}), f32[16,128,256]{2,1,0:T(8,128)S(1)}, u32[]{:S(2)}, u32[]{:S(2)}) %all-to-all-start.1) | async-done | bytes 2097184 | tf_op jit(solution)/shard_map/all_to_all | solution.py:584
  72.5 1.3 %place_second.1 = (f32[136,768]{1,0:T(8,128)S(1)}, f32[136,768]{1,0:T(8,128)S(1)}, f32[256,128]{1,0:T(8,128)S(1)}, f32[256,128]{1,0:T(8,128)S(1)}) custom-call(f32[15360,768]{1,0:T(8,128)} %match_first.1.kept, f32[8,256]{1,0:T(8,128)S(1)} %select_maximum_fusion.band.own, f32[16,128,256]{2,1,0:T(8,128)S(1)} %all-to-all-done.1.slots), custom_call_target="tpu_custom_call" | custom-call | tf_op jit(solution)/shard_map/place_second/pallas_call | solution.py:454
  73.8 0.1 collective-permute-start
  73.9 2.4 %collective-permute-start.1 = (f32[136,768]{1,0:T(8,128)S(1)}, f32[136,768]{1,0:T(8,128)S(1)}, u32[]{:S(2)}, u32[]{:S(2)}) collective-permute-start(f32[136,768]{1,0:T(8,128)S(1)} %get-tuple-element.11), channel_id=1, source_target_pairs={{1,2},{3,4},{5,6},{2,1},{4,3},{6,5},{9,10},{11,12},{13,14},{10,9},... | collective-permute-start | bytes 1253384 | tf_op jit(solution)/shard_map/ppermute | solution.py:514
  76.4 0.6 collective-permute-start.2
  77.0 4.9 %collective-permute-start.3 = (f32[256,128]{1,0:T(8,128)S(1)}, f32[256,128]{1,0:T(8,128)S(1)}, u32[]{:S(2)}, u32[]{:S(2)}) collective-permute-start(f32[256,128]{1,0:T(8,128)S(1)} %get-tuple-element.13), channel_id=1, source_target_pairs={{8,16},{24,32},{40,48},{56,64},{72,80},{88,96},{104,112},{16,8},{3... | collective-permute-start | bytes 393224 | tf_op jit(solution)/shard_map/ppermute | solution.py:514
  81.9 1.6 %make_middle.1.middle = f32[512,768]{1,0:T(8,128)S(1)} custom-call(f32[15360,768]{1,0:T(8,128)} %match_first.1.kept, f32[16,128,256]{2,1,0:T(8,128)S(1)} %all-to-all-done.1.slots), custom_call_target="tpu_custom_call" | custom-call | flops 400000 | bytes 4000000 | tf_op jit(solution)/shard_map/make_middle/pallas_call | solution.py:471
  83.5 0.1 make_edges.1
  83.6 0.4 collective-permute-start.4
  84.0 5.0 %collective-permute-start.5 = (f32[256,128]{1,0:T(8,128)S(1)}, f32[256,128]{1,0:T(8,128)S(1)}, u32[]{:S(2)}, u32[]{:S(2)}) collective-permute-start(f32[256,128]{1,0:T(8,128)S(1)} %get-tuple-element.15), channel_id=1, source_target_pairs={{8,16},{24,32},{40,48},{56,64},{72,80},{88,96},{104,112},{16,8},{3... | collective-permute-start | bytes 393224 | tf_op jit(solution)/shard_map/ppermute | solution.py:514
  89.0 2.1 %make_depth.1 = (f32[512,512]{1,0:T(8,128)}, f32[512,512]{1,0:T(8,128)S(1)}) custom-call(f32[8,256]{1,0:T(8,128)S(1)} %select_maximum_fusion.band.own, f32[136,768]{1,0:T(8,128)S(1)} %collective-permute-done.rows_next, f32[136,768]{1,0:T(8,128)S(1)} %collective-permute-done.1.rows_last), custom_call_target="tpu_custom_call" | custom-call | flops 1000000000 | bytes 1000000 | tf_op jit(solution)/shard_map/make_depth/pallas_call | solution.py:501
  91.1 2.9 %collective-permute-done.5.outer_last = f32[256,128]{1,0:T(8,128)S(1)} collective-permute-done((f32[256,128]{1,0:T(8,128)S(1)}, f32[256,128]{1,0:T(8,128)S(1)}, u32[]{:S(2)}, u32[]{:S(2)}) %collective-permute-start.5) | collective-permute-done | bytes 131104 | tf_op jit(solution)/shard_map/ppermute | solution.py:514
  94.0 1.3 %make_coadd.1 = f32[512,512]{1,0:T(8,128)} custom-call(f32[512,768]{1,0:T(8,128)S(1)} %make_middle.1.middle, f32[136,768]{1,0:T(8,128)S(1)} %collective-permute-done.rows_next, f32[136,768]{1,0:T(8,128)S(1)} %collective-permute-done.1.rows_last, f32[256,128]{1,0:T(8,128)S(1)} %collective-permute-done.2.inner_next, ...), custom_call_target="tpu_custom_call" | custom-call | tf_op jit(solution)/shard_map/make_coadd/pallas_call | solution.py:564
  (26 shorter events, 0.1 us)
Async XLA Ops:
  4.0 10.3 %copy-start.9 = (f32[2,8,41]{2,1,0:T(8,128)S(1)}, f32[2,8,41]{2,1,0:T(8,128)}, u32[]{:S(2)}) copy-start(f32[2,8,41]{2,1,0:T(8,128)} %param.15) | copy-start | bytes 7876
  4.0 10.6 %copy-start = (f32[1,16,128,256]{3,2,1,0:T(8,128)S(1)}, f32[1,16,128,256]{3,2,1,0:T(8,128)}, u32[]{:S(2)}) copy-start(f32[1,16,128,256]{3,2,1,0:T(8,128)} %param.8) | copy-start | bytes 6291460
  4.0 10.6 %copy-start.3 = (f32[1,16,8]{1,2,0:T(8,128)S(1)}, f32[1,16,8]{1,2,0:T(8,128)}, u32[]{:S(2)}) copy-start(f32[1,16,8]{1,2,0:T(8,128)} %param.14) | copy-start | bytes 1540
  4.0 10.6 %copy-start.5 = (s32[1,16]{1,0:T(1,128)S(1)}, s32[1,16]{1,0:T(1,128)}, u32[]{:S(2)}) copy-start(s32[1,16]{1,0:T(1,128)} %row_offset.1) | copy-start | bytes 196
  4.0 10.5 %copy-start.6 = (s32[1,16]{1,0:T(1,128)S(1)}, s32[1,16]{1,0:T(1,128)}, u32[]{:S(2)}) copy-start(s32[1,16]{1,0:T(1,128)} %col_offset.1) | copy-start | bytes 196
  4.0 10.5 %copy-start.7 = (s32[1,16]{1,0:T(1,128)S(1)}, s32[1,16]{1,0:T(1,128)}, u32[]{:S(2)}) copy-start(s32[1,16]{1,0:T(1,128)} %live.1) | copy-start | bytes 196
  4.0 10.5 %copy-start.8 = (f32[1,16]{1,0:T(1,128)S(1)}, f32[1,16]{1,0:T(1,128)}, u32[]{:S(2)}) copy-start(f32[1,16]{1,0:T(1,128)} %weight.1) | copy-start | bytes 196
  4.0 36.5 %all-to-all-start = ((f32[16,264,128]{2,1,0:T(8,128)}), f32[16,264,128]{2,1,0:T(8,128)}, u32[]{:S(2)}, u32[]{:S(2)}) async-start(f32[16,264,128]{2,1,0:T(8,128)} %pack.1), calls=%async_computation | async-start | bytes 4325376 | tf_op jit(solution)/shard_map/all_to_all | solution.py:580
  14.6 0.7 copy-start.4
  15.3 4.3 %copy-start.2 = (f32[2,8,384]{2,1,0:T(8,128)}, f32[2,8,384]{2,1,0:T(8,128)S(1)}, u32[]{:S(2)}) copy-start(f32[2,8,384]{2,1,0:T(8,128)S(1)} %fusion.taps) | copy-start | bytes 73732
  19.5 1.3 %copy-start.1 = (f32[16,128,256]{2,1,0:T(8,128)}, f32[16,128,256]{2,1,0:T(8,128)S(1)}, u32[]{:S(2)}) copy-start(f32[16,128,256]{2,1,0:T(8,128)S(1)} %match_second.1) | copy-start | bytes 6291460
  40.6 31.9 %all-to-all-start.1 = ((f32[16,128,256]{2,1,0:T(8,128)}), f32[16,128,256]{2,1,0:T(8,128)S(1)}, u32[]{:S(2)}, u32[]{:S(2)}) async-start(f32[16,128,256]{2,1,0:T(8,128)} %copy-done.1), calls=%async_computation.1 | async-start | bytes 4194304 | tf_op jit(solution)/shard_map/all_to_all | solution.py:584
  73.8 9.7 %collective-permute-start = (f32[136,768]{1,0:T(8,128)S(1)}, f32[136,768]{1,0:T(8,128)S(1)}, u32[]{:S(2)}, u32[]{:S(2)}) collective-permute-start(f32[136,768]{1,0:T(8,128)S(1)} %get-tuple-element.10), channel_id=1, source_target_pairs={{0,1},{2,3},{4,5},{6,7},{1,0},{3,2},{5,4},{7,6},{8,9},{10,11},{12,... | collective-permute-start | bytes 1253384 | tf_op jit(solution)/shard_map/ppermute | solution.py:514
  73.9 9.6 %collective-permute-start.1 = (f32[136,768]{1,0:T(8,128)S(1)}, f32[136,768]{1,0:T(8,128)S(1)}, u32[]{:S(2)}, u32[]{:S(2)}) collective-permute-start(f32[136,768]{1,0:T(8,128)S(1)} %get-tuple-element.11), channel_id=1, source_target_pairs={{1,2},{3,4},{5,6},{2,1},{4,3},{6,5},{9,10},{11,12},{13,14},{10,9},... | collective-permute-start | bytes 1253384 | tf_op jit(solution)/shard_map/ppermute | solution.py:514
  76.4 14.7 %collective-permute-start.2 = (f32[256,128]{1,0:T(8,128)S(1)}, f32[256,128]{1,0:T(8,128)S(1)}, u32[]{:S(2)}, u32[]{:S(2)}) collective-permute-start(f32[256,128]{1,0:T(8,128)S(1)} %get-tuple-element.12), channel_id=1, source_target_pairs={{0,8},{16,24},{32,40},{48,56},{64,72},{80,88},{96,104},{112,120},{... | collective-permute-start | bytes 393224 | tf_op jit(solution)/shard_map/ppermute | solution.py:514
  77.0 14.1 %collective-permute-start.3 = (f32[256,128]{1,0:T(8,128)S(1)}, f32[256,128]{1,0:T(8,128)S(1)}, u32[]{:S(2)}, u32[]{:S(2)}) collective-permute-start(f32[256,128]{1,0:T(8,128)S(1)} %get-tuple-element.13), channel_id=1, source_target_pairs={{8,16},{24,32},{40,48},{56,64},{72,80},{88,96},{104,112},{16,8},{3... | collective-permute-start | bytes 393224 | tf_op jit(solution)/shard_map/ppermute | solution.py:514
  83.6 7.5 %collective-permute-start.4 = (f32[256,128]{1,0:T(8,128)S(1)}, f32[256,128]{1,0:T(8,128)S(1)}, u32[]{:S(2)}, u32[]{:S(2)}) collective-permute-start(f32[256,128]{1,0:T(8,128)S(1)} %get-tuple-element.14), channel_id=1, source_target_pairs={{0,8},{16,24},{32,40},{48,56},{64,72},{80,88},{96,104},{112,120},{... | collective-permute-start | bytes 393224 | tf_op jit(solution)/shard_map/ppermute | solution.py:514
  84.0 10.0 %collective-permute-start.5 = (f32[256,128]{1,0:T(8,128)S(1)}, f32[256,128]{1,0:T(8,128)S(1)}, u32[]{:S(2)}, u32[]{:S(2)}) collective-permute-start(f32[256,128]{1,0:T(8,128)S(1)} %get-tuple-element.15), channel_id=1, source_target_pairs={{8,16},{24,32},{40,48},{56,64},{72,80},{88,96},{104,112},{16,8},{3... | collective-permute-start | bytes 393224 | tf_op jit(solution)/shard_map/ppermute | solution.py:514

commit v6 on v5

--- a/solution.py
+++ b/solution.py
@@ -1,3 +1,5 @@
+import functools
+
 import jax
 import jax.numpy as jnp
 from jax import lax
@@ -392,8 +394,8 @@
 
 
 LOW, HIGH = slice(0, MARGIN), slice(MARGIN + TILE, SIDE)
-CORE, INNER, ALL = slice(MARGIN, MARGIN + TILE), slice(2 * MARGIN, TILE), slice(0, SIDE)
-STRIPS = ((LOW, ALL), (HIGH, ALL), (INNER, LOW), (INNER, HIGH))
+CORE, ALL = slice(MARGIN, MARGIN + TILE), slice(0, SIDE)
+STRIPS = ((LOW, ALL), (HIGH, ALL), (CORE, LOW), (CORE, HIGH))
 
 
 def place_slots(kept, slots, parts, told, canvas, base, told_sem, base_sems):
@@ -434,7 +436,7 @@
             @pl.when(lax.axis_index(axis) % 2 == parity)
             def _():
                 for out, strip in zip(outs, (HIGH, LOW) if parity == 0 else (LOW, HIGH)):
-                    rows, cols = (strip, ALL) if axis == "skyy" else (INNER, strip)
+                    rows, cols = (strip, ALL) if axis == "skyy" else (CORE, strip)
                     out[: rows.stop - rows.start] = base[rows, cols] + canvas[rows, cols]
 
 
@@ -450,7 +452,7 @@
 
 def make_strips(kept, band, slots):
     strip = jax.ShapeDtypeStruct((MARGIN + META, SIDE), f32)
-    side = jax.ShapeDtypeStruct((TILE - 2 * MARGIN, MARGIN), f32)
+    side = jax.ShapeDtypeStruct((TILE, MARGIN), f32)
     return pl.pallas_call(
         strips_kernel,
         out_shape=(strip, strip, side, side),
@@ -519,44 +521,61 @@
     return jnp.where(even, preceding, following), jnp.where(even, following, preceding)
 
 
-def edges_kernel(middle, rows_next, rows_last, cols_next, cols_last):
-    low = TILE - MARGIN
+NEAR = TILE - MARGIN
+
+
+def edges_kernel(near, cols_next, cols_last, rows, out_next, out_last):
     strips = slice(0, MARGIN), slice(MARGIN + TILE, SIDE)
-    for parity in range(2):
-
-        @pl.when(lax.axis_index("skyx") % 2 == parity)
-        def _():
-            for out, cols in zip((cols_next, cols_last), strips[::-1] if parity == 0 else strips):
-                above, below = by_side("skyy", rows_next[:MARGIN, cols], rows_last[:MARGIN, cols])
-                out[:MARGIN] = middle[:MARGIN, cols] + above
-                out[MARGIN:] = middle[low:, cols] + below
-
-
-def make_edges(middle, rows_next, rows_last):
-    edge = jax.ShapeDtypeStruct((2 * MARGIN, MARGIN), f32)
-    return pl.pallas_call(
-        edges_kernel,
+    for row_parity in range(2):
+        for col_parity in range(2):
+            here = (lax.axis_index("skyy") % 2 == row_parity) & (lax.axis_index("skyx") % 2 == col_parity)
+
+            @pl.when(here)
+            def _():
+                for out, side, cols in zip(
+                    (out_next, out_last), (cols_next, cols_last), strips[::-1] if col_parity == 0 else strips
+                ):
+                    came = rows[:MARGIN, cols]
+                    if not near:
+                        out[...] = (side[:MARGIN] if row_parity == 0 else side[NEAR:]) + came
+                    elif row_parity == 0:
+                        out[: NEAR - MARGIN] = side[MARGIN:NEAR]
+                        out[NEAR - MARGIN :] = side[NEAR:] + came
+                    else:
+                        out[:MARGIN] = side[:MARGIN] + came
+                        out[MARGIN:] = side[MARGIN:NEAR]
+
+
+def make_edges(near, cols_next, cols_last, rows):
+    edge = jax.ShapeDtypeStruct((NEAR if near else MARGIN, MARGIN), f32)
+    return pl.pallas_call(
+        functools.partial(edges_kernel, near),
         out_shape=(edge, edge),
         in_specs=[vmem] * 3,
         out_specs=(vmem, vmem),
         compiler_params=pltpu.CompilerParams(vmem_limit_bytes=12 * MIB),
         name="make_edges",
-    )(middle, rows_next, rows_last)
-
-
-def final_kernel(middle, rows_next, rows_last, inner_next, inner_last, outer_next, outer_last, divisor, coadd):
+    )(cols_next, cols_last, rows)
+
+
+def final_kernel(middle, rows_next, rows_last, near_next, near_last, far_next, far_last, divisor, coadd):
     core = slice(MARGIN, MARGIN + TILE)
-    low = TILE - MARGIN
     above, below = by_side("skyy", rows_next[:MARGIN, core], rows_last[:MARGIN, core])
     coadd[...] = middle[:, core]
     coadd[:MARGIN] += above
-    coadd[low:] += below
-    inner = by_side("skyx", inner_next[...], inner_last[...])
-    outer = by_side("skyx", outer_next[...], outer_last[...])
-    for cols, close, far in zip((slice(0, MARGIN), slice(low, TILE)), inner, outer):
-        coadd[:MARGIN, cols] += far[:MARGIN]
-        coadd[MARGIN:low, cols] += close
-        coadd[low:, cols] += far[MARGIN:]
+    coadd[NEAR:] += below
+    near = by_side("skyx", near_next[...], near_last[...])
+    far = by_side("skyx", far_next[...], far_last[...])
+    for parity in range(2):
+
+        @pl.when(lax.axis_index("skyy") % 2 == parity)
+        def _():
+            near_rows = slice(MARGIN, TILE) if parity == 0 else slice(0, NEAR)
+            far_rows = slice(0, MARGIN) if parity == 0 else slice(NEAR, TILE)
+            for n, cols in enumerate((slice(0, MARGIN), slice(NEAR, TILE))):
+                coadd[near_rows, cols] += near[n]
+                coadd[far_rows, cols] += far[n]
+
     coadd[...] = coadd[...] / divisor[...]
 
 
@@ -593,16 +612,13 @@
     rows_next, rows_last, cols_next, cols_last = make_strips(kept, own, late)
     rows_last = exchange(rows_last, "skyy", 1)
     rows_next = exchange(rows_next, "skyy", 0)
-    inner_last = exchange(cols_last, "skyx", 1)
-    inner_next = exchange(cols_next, "skyx", 0)
+    edges = make_edges(True, cols_next, cols_last, rows_next)
+    near_next, near_last = exchange(edges[0], "skyx", 0), exchange(edges[1], "skyx", 1)
     middle = make_middle(kept, late)
-    cols_next, cols_last = make_edges(middle, rows_next, rows_last)
-    outer_last = exchange(cols_last, "skyx", 1)
-    outer_next = exchange(cols_next, "skyx", 0)
+    edges = make_edges(False, cols_next, cols_last, rows_last)
+    far_next, far_last = exchange(edges[0], "skyx", 0), exchange(edges[1], "skyx", 1)
     depth, divisor = make_depth(own, rows_next, rows_last)
-    coadd = make_coadd(
-        middle, rows_next, rows_last, inner_next, inner_last, outer_next, outer_last, divisor
-    )
+    coadd = make_coadd(middle, rows_next, rows_last, near_next, near_last, far_next, far_last, divisor)
     return (coadd, depth)
 
 

time: 96 us -> 94.8 us (0.987)
  waiting for transfers between devices: 28.6 us -> 26.2 us
    ppermute x6, waiting for transfers between devices: 2.92 us -> 0.69 us  [exchange(): return lax.ppermute(block, axis, pairs + [(j, i) for i, j in pairs])]
where the time goes in v6:
time: 94.8 us; the launch traced here: 94 us
  Pallas kernels  33.8 us (36%)
  starting transfers between devices  29.6 us (31%)
  waiting for transfers between devices  26.2 us (28%)
  local copies, waits for them, and re-layouts  3.34 us (4%)
    all_to_all x1, waiting for transfers between devices, per_device(): lax.all_to_all(outgoing, 'skyx', split_axis=0, concat_axis=0, tiled=True)  19.7 us
    pallas_call x1, Pallas kernels, match_first(): pl.pallas_call(first_kernel, out_shape=jax.ShapeDtypeStruct((KEPT_ROWS, S...  17.8 us
    ppermute x6, starting transfers between devices, exchange(): return lax.ppermute(block, axis, pairs + [(j, i) for i, j in pairs])  14.2 us
    all_to_all x1, starting transfers between devices, per_device(): lax.all_to_all(outgoing, 'skyx', split_axis=0, concat_axis=0, tiled=True)  8.43 us
    all_to_all x1, starting transfers between devices, per_device(): late = lax.all_to_all(late, 'skyx', split_axis=0, concat_axis=0, tiled=True)  6.92 us
    all_to_all x1, waiting for transfers between devices, per_device(): late = lax.all_to_all(late, 'skyx', split_axis=0, concat_axis=0, tiled=True)  5.81 us
    pallas_call x1, Pallas kernels, match_second(): pl.pallas_call(second_kernel, out_shape=jax.ShapeDtypeStruct((tiles, PH,...  4.25 us
    pallas_call x1, Pallas kernels, pack(): pl.pallas_call(pack_kernel, out_shape=jax.ShapeDtypeStruct((tiles, SLOT +...  3.34 us
  transfers between devices with their start and end apart: 8, of which 3 were waited for; matrix products, arithmetic and copies ran while one was open for 2% of the time, Pallas kernels for 29%

profile of v6, /device:TPU:10, one launch (start us, length us, event | category | flops | bytes accessed | tf_op | source)
XLA Modules:
  0.0 94.0 jit_solution(5713701747742451181)
XLA Ops:
  0.6 3.3 %pack.1 = f32[16,264,128]{2,1,0:T(8,128)} custom-call(s32[1,16]{1,0:T(1,128)} %bitcast.16, s32[1,16]{1,0:T(1,128)} %row_offset.1, s32[1,16]{1,0:T(1,128)} %col_offset.1, s32[1,16]{1,0:T(1,128)} %live.1, f32[1,16]{1,0:T(1,128)} %weight.1, f32[8,16]{1,0:T(8,128)} %bitcast.12, f32[16,128,256]{2,1,0:T(8,128)} %bitcast.10), custom_call_target="tpu_custom_call" | custom-call | tf_op jit(solution)/shard_map/pack/pallas_call | solution.py:166
  4.1 8.4 %all-to-all-start = ((f32[16,264,128]{2,1,0:T(8,128)}), f32[16,264,128]{2,1,0:T(8,128)}, u32[]{:S(2)}, u32[]{:S(2)}) async-start(f32[16,264,128]{2,1,0:T(8,128)} %pack.1), calls=%async_computation | async-start | bytes 4325376 | tf_op jit(solution)/shard_map/all_to_all | solution.py:599
  12.5 1.7 %list_second.1.second = s32[3,16]{1,0:T(4,128)} custom-call(s32[1,16]{1,0:T(1,128)} %bitcast.17), custom_call_target="tpu_custom_call" | custom-call | tf_op jit(solution)/shard_map/list_second/pallas_call | solution.py:218
  14.2 0.1 rev.3
  14.3 0.1 pad.10.clone
  14.4 0.1 slice_maximum_fusion
  14.5 0.1 fusion.taps
  14.6 0.7 copy-done.4
  15.3 4.3 %match_second.1 = f32[16,128,256]{2,1,0:T(8,128)S(1)} custom-call(s32[3,16]{1,0:T(4,128)S(1)} %copy-done.4, f32[8,16]{1,0:T(8,128)S(1)} %bitcast.13, s32[1,16]{1,0:T(1,128)S(1)} %copy-done.7, f32[1,16]{1,0:T(1,128)S(1)} %copy-done.8, s32[1,16]{1,0:T(1,128)S(1)} %copy-done.5, s32[1,16]{1,0:T(1,128)S(1)} %copy-done.6, f32[16,128,256]{2,1,0:T(8,128)S(1)} %bitcast.11, ...), custom_call_target="tpu_custom_call" | custom-call | flops 5000000000 | bytes 6000000 | tf_op jit(solution)/shard_map/match_second/pallas_call | solution.py:270
  19.5 1.3 %copy-done.1 = f32[16,128,256]{2,1,0:T(8,128)} copy-done((f32[16,128,256]{2,1,0:T(8,128)}, f32[16,128,256]{2,1,0:T(8,128)S(1)}, u32[]{:S(2)}) %copy-start.1) | copy-done | bytes 2097176
  20.8 19.7 %all-to-all-done.slots.group = f32[16,264,128]{2,1,0:T(8,128)} async-done(((f32[16,264,128]{2,1,0:T(8,128)}), f32[16,264,128]{2,1,0:T(8,128)}, u32[]{:S(2)}, u32[]{:S(2)}) %all-to-all-start) | async-done | bytes 2162720 | tf_op jit(solution)/shard_map/all_to_all | solution.py:599
  40.5 6.9 %all-to-all-start.1 = ((f32[16,128,256]{2,1,0:T(8,128)}), f32[16,128,256]{2,1,0:T(8,128)S(1)}, u32[]{:S(2)}, u32[]{:S(2)}) async-start(f32[16,128,256]{2,1,0:T(8,128)} %copy-done.1), calls=%async_computation.1 | async-start | bytes 4194304 | tf_op jit(solution)/shard_map/all_to_all | solution.py:603
  47.4 0.8 slice_bitcast_fusion
  48.3 0.1 slice_reduce_fusion.2
  48.4 0.1 slice.47
  48.5 0.1 slice.51
  48.5 0.1 add.16
  48.6 0.1 slice.53
  48.7 17.8 %match_first.1.kept = f32[15360,768]{1,0:T(8,128)} custom-call(f32[16,264,128]{2,1,0:T(8,128)} %all-to-all-done.slots.group, f32[16,264,128]{2,1,0:T(8,128)} %all-to-all-done.slots.group, f32[2,8,384]{2,1,0:T(8,128)} %copy-done.2), custom_call_target="tpu_custom_call" | custom-call | flops 10000000000 | bytes 8000000 | tf_op jit(solution)/shard_map/match_first/pallas_call | solution.py:370
  66.5 5.8 %all-to-all-done.1.slots = f32[16,128,256]{2,1,0:T(8,128)S(1)} async-done(((f32[16,128,256]{2,1,0:T(8,128)}), f32[16,128,256]{2,1,0:T(8,128)S(1)}, u32[]{:S(2)}, u32[]{:S(2)}) %all-to-all-start.1) | async-done | bytes 2097184 | tf_op jit(solution)/shard_map/all_to_all | solution.py:603
  72.3 1.5 %place_second.1 = (f32[136,768]{1,0:T(8,128)S(1)}, f32[136,768]{1,0:T(8,128)S(1)}, f32[512,128]{1,0:T(8,128)S(1)}, f32[512,128]{1,0:T(8,128)S(1)}) custom-call(f32[15360,768]{1,0:T(8,128)} %match_first.1.kept, f32[8,256]{1,0:T(8,128)S(1)} %select_maximum_fusion.band.own, f32[16,128,256]{2,1,0:T(8,128)S(1)} %all-to-all-done.1.slots), custom_call_target="tpu_custom_call" | custom-call | tf_op jit(solution)/shard_map/place_second/pallas_call | solution.py:456
  73.8 0.1 collective-permute-start
  73.9 2.6 %collective-permute-start.1 = (f32[136,768]{1,0:T(8,128)S(1)}, f32[136,768]{1,0:T(8,128)S(1)}, u32[]{:S(2)}, u32[]{:S(2)}) collective-permute-start(f32[136,768]{1,0:T(8,128)S(1)} %get-tuple-element.13), channel_id=1, source_target_pairs={{1,2},{3,4},{5,6},{2,1},{4,3},{6,5},{9,10},{11,12},{13,14},{10,9},... | collective-permute-start | bytes 1253384 | tf_op jit(solution)/shard_map/ppermute | solution.py:516
  76.5 0.1 make_edges.2
  76.6 0.6 collective-permute-start.2
  77.2 4.9 %collective-permute-start.3 = (f32[384,128]{1,0:T(8,128)S(1)}, f32[384,128]{1,0:T(8,128)S(1)}, u32[]{:S(2)}, u32[]{:S(2)}) collective-permute-start(f32[384,128]{1,0:T(8,128)S(1)} %get-tuple-element.17), channel_id=1, source_target_pairs={{8,16},{24,32},{40,48},{56,64},{72,80},{88,96},{104,112},{16,8},{3... | collective-permute-start | bytes 589832 | tf_op jit(solution)/shard_map/ppermute | solution.py:516
  82.1 1.6 %make_middle.1.middle = f32[512,768]{1,0:T(8,128)S(1)} custom-call(f32[15360,768]{1,0:T(8,128)} %match_first.1.kept, f32[16,128,256]{2,1,0:T(8,128)S(1)} %all-to-all-done.1.slots), custom_call_target="tpu_custom_call" | custom-call | flops 400000 | bytes 4000000 | tf_op jit(solution)/shard_map/make_middle/pallas_call | solution.py:473
  83.7 0.2 collective-permute-start.4
  83.9 5.8 %collective-permute-start.5 = (f32[128,128]{1,0:T(8,128)S(1)}, f32[128,128]{1,0:T(8,128)S(1)}, u32[]{:S(2)}, u32[]{:S(2)}) collective-permute-start(f32[128,128]{1,0:T(8,128)S(1)} %get-tuple-element.19), channel_id=1, source_target_pairs={{8,16},{24,32},{40,48},{56,64},{72,80},{88,96},{104,112},{16,8},{3... | collective-permute-start | bytes 196616 | tf_op jit(solution)/shard_map/ppermute | solution.py:516
  89.8 2.1 %make_depth.1 = (f32[512,512]{1,0:T(8,128)}, f32[512,512]{1,0:T(8,128)S(1)}) custom-call(f32[8,256]{1,0:T(8,128)S(1)} %select_maximum_fusion.band.own, f32[136,768]{1,0:T(8,128)S(1)} %collective-permute-done.rows.rows_next, f32[136,768]{1,0:T(8,128)S(1)} %collective-permute-done.1.rows.rows_last), custom_call_target="tpu_custom_call" | custom-call | flops 1000000000 | bytes 1000000 | tf_op jit(solution)/shard_map/make_depth/pallas_call | solution.py:503
  91.9 0.7 collective-permute-done.5.far_last
  92.6 1.4 %make_coadd.1 = f32[512,512]{1,0:T(8,128)} custom-call(f32[512,768]{1,0:T(8,128)S(1)} %make_middle.1.middle, f32[136,768]{1,0:T(8,128)S(1)} %collective-permute-done.rows.rows_next, f32[136,768]{1,0:T(8,128)S(1)} %collective-permute-done.1.rows.rows_last, f32[384,128]{1,0:T(8,128)S(1)} %collective-permute-done.2.near_next, ...), custom_call_target="tpu_custom_call" | custom-call | tf_op jit(solution)/shard_map/make_coadd/pallas_call | solution.py:583
  (27 shorter events, 0.1 us)
Async XLA Ops:
  4.0 10.2 %copy-start.9 = (f32[2,8,41]{2,1,0:T(8,128)S(1)}, f32[2,8,41]{2,1,0:T(8,128)}, u32[]{:S(2)}) copy-start(f32[2,8,41]{2,1,0:T(8,128)} %param.15) | copy-start | bytes 7876
  4.0 10.6 %copy-start = (f32[1,16,128,256]{3,2,1,0:T(8,128)S(1)}, f32[1,16,128,256]{3,2,1,0:T(8,128)}, u32[]{:S(2)}) copy-start(f32[1,16,128,256]{3,2,1,0:T(8,128)} %param.8) | copy-start | bytes 6291460
  4.0 10.5 %copy-start.3 = (f32[1,16,8]{1,2,0:T(8,128)S(1)}, f32[1,16,8]{1,2,0:T(8,128)}, u32[]{:S(2)}) copy-start(f32[1,16,8]{1,2,0:T(8,128)} %param.14) | copy-start | bytes 1540
  4.0 10.5 %copy-start.5 = (s32[1,16]{1,0:T(1,128)S(1)}, s32[1,16]{1,0:T(1,128)}, u32[]{:S(2)}) copy-start(s32[1,16]{1,0:T(1,128)} %row_offset.1) | copy-start | bytes 196
  4.0 10.5 %copy-start.6 = (s32[1,16]{1,0:T(1,128)S(1)}, s32[1,16]{1,0:T(1,128)}, u32[]{:S(2)}) copy-start(s32[1,16]{1,0:T(1,128)} %col_offset.1) | copy-start | bytes 196
  4.0 10.5 %copy-start.7 = (s32[1,16]{1,0:T(1,128)S(1)}, s32[1,16]{1,0:T(1,128)}, u32[]{:S(2)}) copy-start(s32[1,16]{1,0:T(1,128)} %live.1) | copy-start | bytes 196
  4.0 10.5 %copy-start.8 = (f32[1,16]{1,0:T(1,128)S(1)}, f32[1,16]{1,0:T(1,128)}, u32[]{:S(2)}) copy-start(f32[1,16]{1,0:T(1,128)} %weight.1) | copy-start | bytes 196
  4.1 36.4 %all-to-all-start = ((f32[16,264,128]{2,1,0:T(8,128)}), f32[16,264,128]{2,1,0:T(8,128)}, u32[]{:S(2)}, u32[]{:S(2)}) async-start(f32[16,264,128]{2,1,0:T(8,128)} %pack.1), calls=%async_computation | async-start | bytes 4325376 | tf_op jit(solution)/shard_map/all_to_all | solution.py:599
  14.6 0.7 copy-start.4
  15.3 4.3 %copy-start.2 = (f32[2,8,384]{2,1,0:T(8,128)}, f32[2,8,384]{2,1,0:T(8,128)S(1)}, u32[]{:S(2)}) copy-start(f32[2,8,384]{2,1,0:T(8,128)S(1)} %fusion.taps) | copy-start | bytes 73732
  19.5 1.3 %copy-start.1 = (f32[16,128,256]{2,1,0:T(8,128)}, f32[16,128,256]{2,1,0:T(8,128)S(1)}, u32[]{:S(2)}) copy-start(f32[16,128,256]{2,1,0:T(8,128)S(1)} %match_second.1) | copy-start | bytes 6291460
  40.5 31.8 %all-to-all-start.1 = ((f32[16,128,256]{2,1,0:T(8,128)}), f32[16,128,256]{2,1,0:T(8,128)S(1)}, u32[]{:S(2)}, u32[]{:S(2)}) async-start(f32[16,128,256]{2,1,0:T(8,128)} %copy-done.1), calls=%async_computation.1 | async-start | bytes 4194304 | tf_op jit(solution)/shard_map/all_to_all | solution.py:603
  73.8 2.7 %collective-permute-start = (f32[136,768]{1,0:T(8,128)S(1)}, f32[136,768]{1,0:T(8,128)S(1)}, u32[]{:S(2)}, u32[]{:S(2)}) collective-permute-start(f32[136,768]{1,0:T(8,128)S(1)} %get-tuple-element.12), channel_id=1, source_target_pairs={{0,1},{2,3},{4,5},{6,7},{1,0},{3,2},{5,4},{7,6},{8,9},{10,11},{12,... | collective-permute-start | bytes 1253384 | tf_op jit(solution)/shard_map/ppermute | solution.py:516
  73.9 9.8 %collective-permute-start.1 = (f32[136,768]{1,0:T(8,128)S(1)}, f32[136,768]{1,0:T(8,128)S(1)}, u32[]{:S(2)}, u32[]{:S(2)}) collective-permute-start(f32[136,768]{1,0:T(8,128)S(1)} %get-tuple-element.13), channel_id=1, source_target_pairs={{1,2},{3,4},{5,6},{2,1},{4,3},{6,5},{9,10},{11,12},{13,14},{10,9},... | collective-permute-start | bytes 1253384 | tf_op jit(solution)/shard_map/ppermute | solution.py:516
  76.6 16.0 %collective-permute-start.2 = (f32[384,128]{1,0:T(8,128)S(1)}, f32[384,128]{1,0:T(8,128)S(1)}, u32[]{:S(2)}, u32[]{:S(2)}) collective-permute-start(f32[384,128]{1,0:T(8,128)S(1)} %get-tuple-element.16), channel_id=1, source_target_pairs={{0,8},{16,24},{32,40},{48,56},{64,72},{80,88},{96,104},{112,120},{... | collective-permute-start | bytes 589832 | tf_op jit(solution)/shard_map/ppermute | solution.py:516
  77.2 15.4 %collective-permute-start.3 = (f32[384,128]{1,0:T(8,128)S(1)}, f32[384,128]{1,0:T(8,128)S(1)}, u32[]{:S(2)}, u32[]{:S(2)}) collective-permute-start(f32[384,128]{1,0:T(8,128)S(1)} %get-tuple-element.17), channel_id=1, source_target_pairs={{8,16},{24,32},{40,48},{56,64},{72,80},{88,96},{104,112},{16,8},{3... | collective-permute-start | bytes 589832 | tf_op jit(solution)/shard_map/ppermute | solution.py:516
  83.7 8.2 %collective-permute-start.4 = (f32[128,128]{1,0:T(8,128)S(1)}, f32[128,128]{1,0:T(8,128)S(1)}, u32[]{:S(2)}, u32[]{:S(2)}) collective-permute-start(f32[128,128]{1,0:T(8,128)S(1)} %get-tuple-element.18), channel_id=1, source_target_pairs={{0,8},{16,24},{32,40},{48,56},{64,72},{80,88},{96,104},{112,120},{... | collective-permute-start | bytes 196616 | tf_op jit(solution)/shard_map/ppermute | solution.py:516
  83.9 8.6 %collective-permute-start.5 = (f32[128,128]{1,0:T(8,128)S(1)}, f32[128,128]{1,0:T(8,128)S(1)}, u32[]{:S(2)}, u32[]{:S(2)}) collective-permute-start(f32[128,128]{1,0:T(8,128)S(1)} %get-tuple-element.19), channel_id=1, source_target_pairs={{8,16},{24,32},{40,48},{56,64},{72,80},{88,96},{104,112},{16,8},{3... | collective-permute-start | bytes 196616 | tf_op jit(solution)/shard_map/ppermute | solution.py:516

commit v7 on v6

--- a/solution.py
+++ b/solution.py
@@ -22,6 +22,7 @@
 HALF_COLS = PW // 2
 SLOT = 2 * PH
 GROUP = 4
+CHUNK = 4
 KEPT_ROWS = 20 * SIDE
 MIB = 1024 * 1024
 
@@ -89,7 +90,7 @@
 def pack_kernel(*refs):
     given, patches, out = refs[:6], refs[6], refs[7]
     scalars, vectors = refs[8:14], refs[14:19]
-    slots, held, meta, small_sems, in_sem, out_sems, meta_sem = refs[19:]
+    slots, held, meta, small_sems, in_sems, out_sems, meta_sem = refs[19:]
     dest, row_offset, col_offset, live, weight, coefs = scalars
     count = patches.shape[0]
     tiles = out.shape[0]
@@ -104,13 +105,26 @@
     ]
     for copy in small:
         copy.start()
-    bring = pltpu.make_async_copy(patches, held, in_sem)
-    bring.start()
+    brings = []
+    for n in range(count // CHUNK):
+        part = pl.ds(n * CHUNK, CHUNK)
+        brings.append(pltpu.make_async_copy(patches.at[part], held.at[part], in_sems.at[n]))
+        brings[-1].start()
     meta[...] = jnp.zeros_like(meta)
     for copy in small:
         copy.wait()
 
     assign_slots(dest, slots)
+    for k in range(count):
+        if k % CHUNK == 0:
+            brings[k // CHUNK].wait()
+        t = dest[0, k]
+
+        @pl.when(slots[0, t] == k)
+        def _():
+            give(k, t, 0).start()
+            give(k, t, 1).start()
+
     for row, values in enumerate(vectors):
         line = values[...].astype(f32)
         for t in range(tiles):
@@ -141,15 +155,6 @@
     about = pltpu.make_async_copy(meta, out.at[:, pl.ds(SLOT, META)], meta_sem)
     about.start()
 
-    bring.wait()
-    for k in range(count):
-        t = dest[0, k]
-
-        @pl.when(slots[0, t] == k)
-        def _():
-            give(k, t, 0).start()
-            give(k, t, 1).start()
-
     for k in range(count):
         t = dest[0, k]
 
@@ -175,7 +180,7 @@
             pltpu.VMEM(patches.shape, f32),
             pltpu.VMEM((tiles, META, HALF_COLS), f32),
             pltpu.SemaphoreType.DMA((11,)),
-            pltpu.SemaphoreType.DMA,
+            pltpu.SemaphoreType.DMA((patches.shape[0] // CHUNK,)),
             pltpu.SemaphoreType.DMA((patches.shape[0], 2)),
             pltpu.SemaphoreType.DMA,
         ],
@@ -558,33 +563,72 @@
     )(cols_next, cols_last, rows)
 
 
-def final_kernel(middle, rows_next, rows_last, near_next, near_last, far_next, far_last, divisor, coadd):
-    core = slice(MARGIN, MARGIN + TILE)
-    above, below = by_side("skyy", rows_next[:MARGIN, core], rows_last[:MARGIN, core])
-    coadd[...] = middle[:, core]
-    coadd[:MARGIN] += above
-    coadd[NEAR:] += below
+SIDES = slice(0, MARGIN), slice(NEAR, TILE)
+
+
+def with_rows(total, middle, rows_next, rows_last, cols):
+    at = slice(MARGIN + cols.start, MARGIN + cols.stop)
+    above, below = by_side("skyy", rows_next[:MARGIN, at], rows_last[:MARGIN, at])
+    total[:, cols] = middle[:, at]
+    total[:MARGIN, cols] += above
+    total[NEAR:, cols] += below
+
+
+def inside_kernel(middle, rows_next, rows_last, divisor, out, total, sem):
+    cols = slice(MARGIN, NEAR)
+    with_rows(total, middle, rows_next, rows_last, cols)
+    total[:, cols] = total[:, cols] / divisor[:, cols]
+    at = pl.ds(MARGIN, NEAR - MARGIN)
+    copy = pltpu.make_async_copy(total.at[:, at], out.at[:, at], sem)
+    copy.start()
+    copy.wait()
+
+
+def make_inside(*parts):
+    return pl.pallas_call(
+        inside_kernel,
+        out_shape=jax.ShapeDtypeStruct((TILE, TILE), f32),
+        in_specs=[vmem] * 4,
+        out_specs=anywhere,
+        scratch_shapes=[pltpu.VMEM((TILE, TILE), f32), pltpu.SemaphoreType.DMA],
+        compiler_params=pltpu.CompilerParams(vmem_limit_bytes=16 * MIB),
+        name="make_inside",
+    )(*parts)
+
+
+def final_kernel(
+    inside, middle, rows_next, rows_last, near_next, near_last, far_next, far_last, divisor, out, total, sems
+):
     near = by_side("skyx", near_next[...], near_last[...])
     far = by_side("skyx", far_next[...], far_last[...])
-    for parity in range(2):
-
-        @pl.when(lax.axis_index("skyy") % 2 == parity)
-        def _():
-            near_rows = slice(MARGIN, TILE) if parity == 0 else slice(0, NEAR)
-            far_rows = slice(0, MARGIN) if parity == 0 else slice(NEAR, TILE)
-            for n, cols in enumerate((slice(0, MARGIN), slice(NEAR, TILE))):
-                coadd[near_rows, cols] += near[n]
-                coadd[far_rows, cols] += far[n]
-
-    coadd[...] = coadd[...] / divisor[...]
+    copies = []
+    for n, cols in enumerate(SIDES):
+        with_rows(total, middle, rows_next, rows_last, cols)
+        for parity in range(2):
+
+            @pl.when(lax.axis_index("skyy") % 2 == parity)
+            def _():
+                near_rows = slice(MARGIN, TILE) if parity == 0 else slice(0, NEAR)
+                far_rows = slice(0, MARGIN) if parity == 0 else slice(NEAR, TILE)
+                total[near_rows, cols] += near[n]
+                total[far_rows, cols] += far[n]
+
+        total[:, cols] = total[:, cols] / divisor[:, cols]
+        at = pl.ds(cols.start, MARGIN)
+        copies.append(pltpu.make_async_copy(total.at[:, at], out.at[:, at], sems.at[n]))
+        copies[-1].start()
+    for copy in copies:
+        copy.wait()
 
 
 def make_coadd(*parts):
     return pl.pallas_call(
         final_kernel,
         out_shape=jax.ShapeDtypeStruct((TILE, TILE), f32),
-        in_specs=[vmem] * 8,
-        out_specs=vmem,
+        in_specs=[anywhere] + [vmem] * 8,
+        out_specs=anywhere,
+        scratch_shapes=[pltpu.VMEM((TILE, TILE), f32), pltpu.SemaphoreType.DMA((2,))],
+        input_output_aliases={0: 0},
         compiler_params=pltpu.CompilerParams(vmem_limit_bytes=16 * MIB),
         name="make_coadd",
     )(*parts)
@@ -618,7 +662,8 @@
     edges = make_edges(False, cols_next, cols_last, rows_last)
     far_next, far_last = exchange(edges[0], "skyx", 0), exchange(edges[1], "skyx", 1)
     depth, divisor = make_depth(own, rows_next, rows_last)
-    coadd = make_coadd(middle, rows_next, rows_last, near_next, near_last, far_next, far_last, divisor)
+    inside = make_inside(middle, rows_next, rows_last, divisor)
+    coadd = make_coadd(inside, middle, rows_next, rows_last, near_next, near_last, far_next, far_last, divisor)
     return (coadd, depth)
 
 

time: 94.8 us -> 94.1 us (level)
  transfers between devices with their start and end apart: 8 -> 8, of which waited for: 3 -> 3; matrix products, arithmetic and copies ran while one was open for 2% -> 2% of each run, Pallas kernels for 29% -> 31%
where the time goes in v7:
time: 94.1 us; the launch traced here: 93.2 us
  Pallas kernels  34 us (36%)
  starting transfers between devices  28.9 us (31%)
  waiting for transfers between devices  25.8 us (27%)
  local copies, waits for them, and re-layouts  3.34 us (4%)
    all_to_all x1, waiting for transfers between devices, per_device(): lax.all_to_all(outgoing, 'skyx', split_axis=0, concat_axis=0, tiled=True)  19.7 us
    pallas_call x1, Pallas kernels, match_first(): pl.pallas_call(first_kernel, out_shape=jax.ShapeDtypeStruct((KEPT_ROWS, S...  17.8 us
    ppermute x6, starting transfers between devices, exchange(): return lax.ppermute(block, axis, pairs + [(j, i) for i, j in pairs])  13.5 us
    all_to_all x1, starting transfers between devices, per_device(): lax.all_to_all(outgoing, 'skyx', split_axis=0, concat_axis=0, tiled=True)  8.47 us
    all_to_all x1, starting transfers between devices, per_device(): late = lax.all_to_all(late, 'skyx', split_axis=0, concat_axis=0, tiled=True)  6.92 us
    all_to_all x1, waiting for transfers between devices, per_device(): late = lax.all_to_all(late, 'skyx', split_axis=0, concat_axis=0, tiled=True)  5.85 us
    pallas_call x1, Pallas kernels, match_second(): pl.pallas_call(second_kernel, out_shape=jax.ShapeDtypeStruct((tiles, PH,...  4.25 us
    pallas_call x1, Pallas kernels, pack(): pl.pallas_call(pack_kernel, out_shape=jax.ShapeDtypeStruct((tiles, SLOT +...  2.94 us
  transfers between devices with their start and end apart: 8, of which 3 were waited for; matrix products, arithmetic and copies ran while one was open for 2% of the time, Pallas kernels for 31%

profile of v7, /device:TPU:10, one launch (start us, length us, event | category | flops | bytes accessed | tf_op | source)
XLA Modules:
  0.0 93.2 jit_solution(14893610544298428476)
XLA Ops:
  0.6 2.9 %pack.1 = f32[16,264,128]{2,1,0:T(8,128)} custom-call(s32[1,16]{1,0:T(1,128)} %bitcast.16, s32[1,16]{1,0:T(1,128)} %row_offset.1, s32[1,16]{1,0:T(1,128)} %col_offset.1, s32[1,16]{1,0:T(1,128)} %live.1, f32[1,16]{1,0:T(1,128)} %weight.1, f32[8,16]{1,0:T(8,128)} %bitcast.12, f32[16,128,256]{2,1,0:T(8,128)} %bitcast.10), custom_call_target="tpu_custom_call" | custom-call | tf_op jit(solution)/shard_map/pack/pallas_call | solution.py:171
  3.7 8.5 %all-to-all-start = ((f32[16,264,128]{2,1,0:T(8,128)}), f32[16,264,128]{2,1,0:T(8,128)}, u32[]{:S(2)}, u32[]{:S(2)}) async-start(f32[16,264,128]{2,1,0:T(8,128)} %pack.1), calls=%async_computation | async-start | bytes 4325376 | tf_op jit(solution)/shard_map/all_to_all | solution.py:643
  12.1 1.7 %list_second.1.second = s32[3,16]{1,0:T(4,128)} custom-call(s32[1,16]{1,0:T(1,128)} %bitcast.17), custom_call_target="tpu_custom_call" | custom-call | tf_op jit(solution)/shard_map/list_second/pallas_call | solution.py:223
  13.9 0.1 rev.3
  13.9 0.1 pad.10.clone
  14.0 0.1 slice_maximum_fusion
  14.1 0.1 fusion.taps
  14.2 0.7 copy-done.4
  14.9 4.3 %match_second.1 = f32[16,128,256]{2,1,0:T(8,128)S(1)} custom-call(s32[3,16]{1,0:T(4,128)S(1)} %copy-done.4, f32[8,16]{1,0:T(8,128)S(1)} %bitcast.13, s32[1,16]{1,0:T(1,128)S(1)} %copy-done.7, f32[1,16]{1,0:T(1,128)S(1)} %copy-done.8, s32[1,16]{1,0:T(1,128)S(1)} %copy-done.5, s32[1,16]{1,0:T(1,128)S(1)} %copy-done.6, f32[16,128,256]{2,1,0:T(8,128)S(1)} %bitcast.11, ...), custom_call_target="tpu_custom_call" | custom-call | flops 5000000000 | bytes 6000000 | tf_op jit(solution)/shard_map/match_second/pallas_call | solution.py:275
  19.2 1.3 %copy-done.1 = f32[16,128,256]{2,1,0:T(8,128)} copy-done((f32[16,128,256]{2,1,0:T(8,128)}, f32[16,128,256]{2,1,0:T(8,128)S(1)}, u32[]{:S(2)}) %copy-start.1) | copy-done | bytes 2097176
  20.5 19.7 %all-to-all-done.slots.group = f32[16,264,128]{2,1,0:T(8,128)} async-done(((f32[16,264,128]{2,1,0:T(8,128)}), f32[16,264,128]{2,1,0:T(8,128)}, u32[]{:S(2)}, u32[]{:S(2)}) %all-to-all-start) | async-done | bytes 2162720 | tf_op jit(solution)/shard_map/all_to_all | solution.py:643
  40.1 6.9 %all-to-all-start.1 = ((f32[16,128,256]{2,1,0:T(8,128)}), f32[16,128,256]{2,1,0:T(8,128)S(1)}, u32[]{:S(2)}, u32[]{:S(2)}) async-start(f32[16,128,256]{2,1,0:T(8,128)} %copy-done.1), calls=%async_computation.1 | async-start | bytes 4194304 | tf_op jit(solution)/shard_map/all_to_all | solution.py:647
  47.1 0.8 slice_bitcast_fusion
  47.9 0.1 slice_reduce_fusion.2
  48.0 0.1 slice.47
  48.1 0.1 slice.51
  48.2 0.1 add.16
  48.2 0.1 slice.53
  48.3 17.8 %match_first.1.kept = f32[15360,768]{1,0:T(8,128)} custom-call(f32[16,264,128]{2,1,0:T(8,128)} %all-to-all-done.slots.group, f32[16,264,128]{2,1,0:T(8,128)} %all-to-all-done.slots.group, f32[2,8,384]{2,1,0:T(8,128)} %copy-done.2), custom_call_target="tpu_custom_call" | custom-call | flops 10000000000 | bytes 8000000 | tf_op jit(solution)/shard_map/match_first/pallas_call | solution.py:375
  66.1 5.8 %all-to-all-done.1.slots = f32[16,128,256]{2,1,0:T(8,128)S(1)} async-done(((f32[16,128,256]{2,1,0:T(8,128)}), f32[16,128,256]{2,1,0:T(8,128)S(1)}, u32[]{:S(2)}, u32[]{:S(2)}) %all-to-all-start.1) | async-done | bytes 2097184 | tf_op jit(solution)/shard_map/all_to_all | solution.py:647
  72.0 1.5 %place_second.1 = (f32[136,768]{1,0:T(8,128)S(1)}, f32[136,768]{1,0:T(8,128)S(1)}, f32[512,128]{1,0:T(8,128)S(1)}, f32[512,128]{1,0:T(8,128)S(1)}) custom-call(f32[15360,768]{1,0:T(8,128)} %match_first.1.kept, f32[8,256]{1,0:T(8,128)S(1)} %select_maximum_fusion.band.own, f32[16,128,256]{2,1,0:T(8,128)S(1)} %all-to-all-done.1.slots), custom_call_target="tpu_custom_call" | custom-call | tf_op jit(solution)/shard_map/place_second/pallas_call | solution.py:461
  73.4 0.1 collective-permute-start
  73.5 2.4 %collective-permute-start.1 = (f32[136,768]{1,0:T(8,128)S(1)}, f32[136,768]{1,0:T(8,128)S(1)}, u32[]{:S(2)}, u32[]{:S(2)}) collective-permute-start(f32[136,768]{1,0:T(8,128)S(1)} %get-tuple-element.13), channel_id=1, source_target_pairs={{1,2},{3,4},{5,6},{2,1},{4,3},{6,5},{9,10},{11,12},{13,14},{10,9},... | collective-permute-start | bytes 1253384 | tf_op jit(solution)/shard_map/ppermute | solution.py:521
  76.1 0.6 collective-permute-start.2
  76.7 4.9 %collective-permute-start.3 = (f32[384,128]{1,0:T(8,128)S(1)}, f32[384,128]{1,0:T(8,128)S(1)}, u32[]{:S(2)}, u32[]{:S(2)}) collective-permute-start(f32[384,128]{1,0:T(8,128)S(1)} %get-tuple-element.18), channel_id=1, source_target_pairs={{8,16},{24,32},{40,48},{56,64},{72,80},{88,96},{104,112},{16,8},{3... | collective-permute-start | bytes 589832 | tf_op jit(solution)/shard_map/ppermute | solution.py:521
  81.7 1.6 %make_middle.1.middle = f32[512,768]{1,0:T(8,128)S(1)} custom-call(f32[15360,768]{1,0:T(8,128)} %match_first.1.kept, f32[16,128,256]{2,1,0:T(8,128)S(1)} %all-to-all-done.1.slots), custom_call_target="tpu_custom_call" | custom-call | flops 400000 | bytes 4000000 | tf_op jit(solution)/shard_map/make_middle/pallas_call | solution.py:478
  83.3 0.2 collective-permute-start.4
  83.6 5.2 %collective-permute-start.5 = (f32[128,128]{1,0:T(8,128)S(1)}, f32[128,128]{1,0:T(8,128)S(1)}, u32[]{:S(2)}, u32[]{:S(2)}) collective-permute-start(f32[128,128]{1,0:T(8,128)S(1)} %get-tuple-element.20), channel_id=1, source_target_pairs={{8,16},{24,32},{40,48},{56,64},{72,80},{88,96},{104,112},{16,8},{3... | collective-permute-start | bytes 196616 | tf_op jit(solution)/shard_map/ppermute | solution.py:521
  88.7 2.1 %make_depth.1 = (f32[512,512]{1,0:T(8,128)}, f32[512,512]{1,0:T(8,128)S(1)}) custom-call(f32[8,256]{1,0:T(8,128)S(1)} %select_maximum_fusion.band.own, f32[136,768]{1,0:T(8,128)S(1)} %collective-permute-done.rows_next.rows, f32[136,768]{1,0:T(8,128)S(1)} %collective-permute-done.1.rows_last.rows), custom_call_target="tpu_custom_call" | custom-call | flops 1000000000 | bytes 1000000 | tf_op jit(solution)/shard_map/make_depth/pallas_call | solution.py:508
  90.8 0.9 make_inside.1.inside
  91.8 0.3 collective-permute-done.5.far_last
  92.1 1.1 %make_coadd.1 = f32[512,512]{1,0:T(8,128)} custom-call(f32[512,512]{1,0:T(8,128)} %make_inside.1.inside, f32[512,768]{1,0:T(8,128)S(1)} %make_middle.1.middle, f32[136,768]{1,0:T(8,128)S(1)} %collective-permute-done.rows_next.rows, f32[136,768]{1,0:T(8,128)S(1)} %collective-permute-done.1.rows_last.rows, ...), custom_call_target="tpu_custom_call", output_to_operand_aliasing={{}: (0, {})} | custom-call | tf_op jit(solution)/shard_map/make_coadd/pallas_call | solution.py:625
  (28 shorter events, 0.2 us)
Async XLA Ops:
  3.6 10.3 %copy-start.9 = (f32[2,8,41]{2,1,0:T(8,128)S(1)}, f32[2,8,41]{2,1,0:T(8,128)}, u32[]{:S(2)}) copy-start(f32[2,8,41]{2,1,0:T(8,128)} %param.15) | copy-start | bytes 7876
  3.6 10.6 %copy-start = (f32[1,16,128,256]{3,2,1,0:T(8,128)S(1)}, f32[1,16,128,256]{3,2,1,0:T(8,128)}, u32[]{:S(2)}) copy-start(f32[1,16,128,256]{3,2,1,0:T(8,128)} %param.8) | copy-start | bytes 6291460
  3.6 10.6 %copy-start.3 = (f32[1,16,8]{1,2,0:T(8,128)S(1)}, f32[1,16,8]{1,2,0:T(8,128)}, u32[]{:S(2)}) copy-start(f32[1,16,8]{1,2,0:T(8,128)} %param.14) | copy-start | bytes 1540
  3.6 10.6 %copy-start.5 = (s32[1,16]{1,0:T(1,128)S(1)}, s32[1,16]{1,0:T(1,128)}, u32[]{:S(2)}) copy-start(s32[1,16]{1,0:T(1,128)} %row_offset.1) | copy-start | bytes 196
  3.6 10.6 %copy-start.6 = (s32[1,16]{1,0:T(1,128)S(1)}, s32[1,16]{1,0:T(1,128)}, u32[]{:S(2)}) copy-start(s32[1,16]{1,0:T(1,128)} %col_offset.1) | copy-start | bytes 196
  3.6 10.6 %copy-start.7 = (s32[1,16]{1,0:T(1,128)S(1)}, s32[1,16]{1,0:T(1,128)}, u32[]{:S(2)}) copy-start(s32[1,16]{1,0:T(1,128)} %live.1) | copy-start | bytes 196
  3.6 10.6 %copy-start.8 = (f32[1,16]{1,0:T(1,128)S(1)}, f32[1,16]{1,0:T(1,128)}, u32[]{:S(2)}) copy-start(f32[1,16]{1,0:T(1,128)} %weight.1) | copy-start | bytes 196
  3.7 36.5 %all-to-all-start = ((f32[16,264,128]{2,1,0:T(8,128)}), f32[16,264,128]{2,1,0:T(8,128)}, u32[]{:S(2)}, u32[]{:S(2)}) async-start(f32[16,264,128]{2,1,0:T(8,128)} %pack.1), calls=%async_computation | async-start | bytes 4325376 | tf_op jit(solution)/shard_map/all_to_all | solution.py:643
  14.2 0.7 copy-start.4
  14.9 4.3 %copy-start.2 = (f32[2,8,384]{2,1,0:T(8,128)}, f32[2,8,384]{2,1,0:T(8,128)S(1)}, u32[]{:S(2)}) copy-start(f32[2,8,384]{2,1,0:T(8,128)S(1)} %fusion.taps) | copy-start | bytes 73732
  19.2 1.3 %copy-start.1 = (f32[16,128,256]{2,1,0:T(8,128)}, f32[16,128,256]{2,1,0:T(8,128)S(1)}, u32[]{:S(2)}) copy-start(f32[16,128,256]{2,1,0:T(8,128)S(1)} %match_second.1) | copy-start | bytes 6291460
  40.1 31.8 %all-to-all-start.1 = ((f32[16,128,256]{2,1,0:T(8,128)}), f32[16,128,256]{2,1,0:T(8,128)S(1)}, u32[]{:S(2)}, u32[]{:S(2)}) async-start(f32[16,128,256]{2,1,0:T(8,128)} %copy-done.1), calls=%async_computation.1 | async-start | bytes 4194304 | tf_op jit(solution)/shard_map/all_to_all | solution.py:647
  73.4 2.6 %collective-permute-start = (f32[136,768]{1,0:T(8,128)S(1)}, f32[136,768]{1,0:T(8,128)S(1)}, u32[]{:S(2)}, u32[]{:S(2)}) collective-permute-start(f32[136,768]{1,0:T(8,128)S(1)} %get-tuple-element.12), channel_id=1, source_target_pairs={{0,1},{2,3},{4,5},{6,7},{1,0},{3,2},{5,4},{7,6},{8,9},{10,11},{12,... | collective-permute-start | bytes 1253384 | tf_op jit(solution)/shard_map/ppermute | solution.py:521
  73.5 9.7 %collective-permute-start.1 = (f32[136,768]{1,0:T(8,128)S(1)}, f32[136,768]{1,0:T(8,128)S(1)}, u32[]{:S(2)}, u32[]{:S(2)}) collective-permute-start(f32[136,768]{1,0:T(8,128)S(1)} %get-tuple-element.13), channel_id=1, source_target_pairs={{1,2},{3,4},{5,6},{2,1},{4,3},{6,5},{9,10},{11,12},{13,14},{10,9},... | collective-permute-start | bytes 1253384 | tf_op jit(solution)/shard_map/ppermute | solution.py:521
  76.1 16.0 %collective-permute-start.2 = (f32[384,128]{1,0:T(8,128)S(1)}, f32[384,128]{1,0:T(8,128)S(1)}, u32[]{:S(2)}, u32[]{:S(2)}) collective-permute-start(f32[384,128]{1,0:T(8,128)S(1)} %get-tuple-element.17), channel_id=1, source_target_pairs={{0,8},{16,24},{32,40},{48,56},{64,72},{80,88},{96,104},{112,120},{... | collective-permute-start | bytes 589832 | tf_op jit(solution)/shard_map/ppermute | solution.py:521
  76.7 15.3 %collective-permute-start.3 = (f32[384,128]{1,0:T(8,128)S(1)}, f32[384,128]{1,0:T(8,128)S(1)}, u32[]{:S(2)}, u32[]{:S(2)}) collective-permute-start(f32[384,128]{1,0:T(8,128)S(1)} %get-tuple-element.18), channel_id=1, source_target_pairs={{8,16},{24,32},{40,48},{56,64},{72,80},{88,96},{104,112},{16,8},{3... | collective-permute-start | bytes 589832 | tf_op jit(solution)/shard_map/ppermute | solution.py:521
  83.3 8.4 %collective-permute-start.4 = (f32[128,128]{1,0:T(8,128)S(1)}, f32[128,128]{1,0:T(8,128)S(1)}, u32[]{:S(2)}, u32[]{:S(2)}) collective-permute-start(f32[128,128]{1,0:T(8,128)S(1)} %get-tuple-element.19), channel_id=1, source_target_pairs={{0,8},{16,24},{32,40},{48,56},{64,72},{80,88},{96,104},{112,120},{... | collective-permute-start | bytes 196616 | tf_op jit(solution)/shard_map/ppermute | solution.py:521
  83.6 8.5 %collective-permute-start.5 = (f32[128,128]{1,0:T(8,128)S(1)}, f32[128,128]{1,0:T(8,128)S(1)}, u32[]{:S(2)}, u32[]{:S(2)}) collective-permute-start(f32[128,128]{1,0:T(8,128)S(1)} %get-tuple-element.20), channel_id=1, source_target_pairs={{8,16},{24,32},{40,48},{56,64},{72,80},{88,96},{104,112},{16,8},{3... | collective-permute-start | bytes 196616 | tf_op jit(solution)/shard_map/ppermute | solution.py:521

commit v8 on v7

--- a/solution.py
+++ b/solution.py
@@ -403,7 +403,7 @@
 STRIPS = ((LOW, ALL), (HIGH, ALL), (CORE, LOW), (CORE, HIGH))
 
 
-def place_slots(kept, slots, parts, told, canvas, base, told_sem, base_sems):
+def place_slots(kept, slots, parts, told, canvas, base, told_sem, base_sems, core_too):
     tiles = slots.shape[0]
     tell = pltpu.make_async_copy(kept.at[pl.ds(SIDE, tiles), pl.ds(0, 128)], told, told_sem)
     tell.start()
@@ -416,10 +416,15 @@
     tell.wait()
 
     def add(t, carry):
-        @pl.when(told[t, 4] > 0)
+        top, left = told[t, 5].astype(i32) + MARGIN, told[t, 6].astype(i32) + MARGIN
+        needed = told[t, 4] > 0
+        if not core_too:
+            inside = (top >= MARGIN) & (top <= MARGIN + TILE - PH) & (left >= MARGIN) & (left <= MARGIN + TILE - PW)
+            needed = needed & jnp.logical_not(inside)
+
+        @pl.when(needed)
         def _():
-            corner = told[t, 5].astype(i32) + MARGIN, told[t, 6].astype(i32) + MARGIN
-            add_turned(canvas, slots[t], *corner)
+            add_turned(canvas, slots[t], top, left)
 
         return carry
 
@@ -431,7 +436,7 @@
 def strips_kernel(
     kept, band, slots, rows_next, rows_last, cols_next, cols_last, told, canvas, base, told_sem, base_sems
 ):
-    place_slots(kept, slots, STRIPS, told, canvas, base, told_sem, base_sems)
+    place_slots(kept, slots, STRIPS, told, canvas, base, told_sem, base_sems, False)
     for out in (rows_next, rows_last):
         out[MARGIN:] = jnp.zeros((META, SIDE), f32)
         out[MARGIN:, : band.shape[1]] = band[...]
@@ -470,7 +475,7 @@
 
 
 def middle_kernel(kept, slots, middle, told, canvas, base, told_sem, base_sems):
-    place_slots(kept, slots, ((CORE, ALL),), told, canvas, base, told_sem, base_sems)
+    place_slots(kept, slots, ((CORE, ALL),), told, canvas, base, told_sem, base_sems, True)
     middle[...] = base[CORE] + canvas[CORE, :SIDE]
 
 

time: 94.1 us -> 94 us (level)
  transfers between devices with their start and end apart: 8 -> 8, of which waited for: 3 -> 2; matrix products, arithmetic and copies ran while one was open for 2% -> 2% of each run, Pallas kernels for 31% -> 30%
where the time goes in v8:
time: 94 us; the launch traced here: 93.4 us
  Pallas kernels  34 us (36%)
  starting transfers between devices  29.3 us (31%)
  waiting for transfers between devices  25.5 us (27%)
  local copies, waits for them, and re-layouts  3.34 us (4%)
    all_to_all x1, waiting for transfers between devices, per_device(): lax.all_to_all(outgoing, 'skyx', split_axis=0, concat_axis=0, tiled=True)  19.7 us
    pallas_call x1, Pallas kernels, match_first(): pl.pallas_call(first_kernel, out_shape=jax.ShapeDtypeStruct((KEPT_ROWS, S...  17.8 us
    ppermute x6, starting transfers between devices, exchange(): return lax.ppermute(block, axis, pairs + [(j, i) for i, j in pairs])  13.9 us
    all_to_all x1, starting transfers between devices, per_device(): lax.all_to_all(outgoing, 'skyx', split_axis=0, concat_axis=0, tiled=True)  8.47 us
    all_to_all x1, starting transfers between devices, per_device(): late = lax.all_to_all(late, 'skyx', split_axis=0, concat_axis=0, tiled=True)  6.92 us
    all_to_all x1, waiting for transfers between devices, per_device(): late = lax.all_to_all(late, 'skyx', split_axis=0, concat_axis=0, tiled=True)  5.85 us
    pallas_call x1, Pallas kernels, match_second(): pl.pallas_call(second_kernel, out_shape=jax.ShapeDtypeStruct((tiles, PH,...  4.25 us
    pallas_call x1, Pallas kernels, pack(): pl.pallas_call(pack_kernel, out_shape=jax.ShapeDtypeStruct((tiles, SLOT +...  2.94 us
  transfers between devices with their start and end apart: 8, of which 2 were waited for; matrix products, arithmetic and copies ran while one was open for 2% of the time, Pallas kernels for 30%

profile of v8, /device:TPU:10, one launch (start us, length us, event | category | flops | bytes accessed | tf_op | source)
XLA Modules:
  0.0 93.4 jit_solution(9907741158152005705)
XLA Ops:
  0.6 2.9 %pack.1 = f32[16,264,128]{2,1,0:T(8,128)} custom-call(s32[1,16]{1,0:T(1,128)} %bitcast.16, s32[1,16]{1,0:T(1,128)} %row_offset.1, s32[1,16]{1,0:T(1,128)} %col_offset.1, s32[1,16]{1,0:T(1,128)} %live.1, f32[1,16]{1,0:T(1,128)} %weight.1, f32[8,16]{1,0:T(8,128)} %bitcast.12, f32[16,128,256]{2,1,0:T(8,128)} %bitcast.10), custom_call_target="tpu_custom_call" | custom-call | tf_op jit(solution)/shard_map/pack/pallas_call | solution.py:171
  3.7 8.5 %all-to-all-start = ((f32[16,264,128]{2,1,0:T(8,128)}), f32[16,264,128]{2,1,0:T(8,128)}, u32[]{:S(2)}, u32[]{:S(2)}) async-start(f32[16,264,128]{2,1,0:T(8,128)} %pack.1), calls=%async_computation | async-start | bytes 4325376 | tf_op jit(solution)/shard_map/all_to_all | solution.py:648
  12.1 1.7 %list_second.1.second = s32[3,16]{1,0:T(4,128)} custom-call(s32[1,16]{1,0:T(1,128)} %bitcast.17), custom_call_target="tpu_custom_call" | custom-call | tf_op jit(solution)/shard_map/list_second/pallas_call | solution.py:223
  13.9 0.1 rev.3
  13.9 0.1 pad.10.clone
  14.0 0.1 slice_maximum_fusion
  14.1 0.1 fusion.taps
  14.2 0.7 copy-done.4
  14.9 4.3 %match_second.1 = f32[16,128,256]{2,1,0:T(8,128)S(1)} custom-call(s32[3,16]{1,0:T(4,128)S(1)} %copy-done.4, f32[8,16]{1,0:T(8,128)S(1)} %bitcast.13, s32[1,16]{1,0:T(1,128)S(1)} %copy-done.7, f32[1,16]{1,0:T(1,128)S(1)} %copy-done.8, s32[1,16]{1,0:T(1,128)S(1)} %copy-done.5, s32[1,16]{1,0:T(1,128)S(1)} %copy-done.6, f32[16,128,256]{2,1,0:T(8,128)S(1)} %bitcast.11, ...), custom_call_target="tpu_custom_call" | custom-call | flops 5000000000 | bytes 6000000 | tf_op jit(solution)/shard_map/match_second/pallas_call | solution.py:275
  19.2 1.3 %copy-done.1 = f32[16,128,256]{2,1,0:T(8,128)} copy-done((f32[16,128,256]{2,1,0:T(8,128)}, f32[16,128,256]{2,1,0:T(8,128)S(1)}, u32[]{:S(2)}) %copy-start.1) | copy-done | bytes 2097176
  20.5 19.7 %all-to-all-done.slots.group = f32[16,264,128]{2,1,0:T(8,128)} async-done(((f32[16,264,128]{2,1,0:T(8,128)}), f32[16,264,128]{2,1,0:T(8,128)}, u32[]{:S(2)}, u32[]{:S(2)}) %all-to-all-start) | async-done | bytes 2162720 | tf_op jit(solution)/shard_map/all_to_all | solution.py:648
  40.1 6.9 %all-to-all-start.1 = ((f32[16,128,256]{2,1,0:T(8,128)}), f32[16,128,256]{2,1,0:T(8,128)S(1)}, u32[]{:S(2)}, u32[]{:S(2)}) async-start(f32[16,128,256]{2,1,0:T(8,128)} %copy-done.1), calls=%async_computation.1 | async-start | bytes 4194304 | tf_op jit(solution)/shard_map/all_to_all | solution.py:652
  47.1 0.8 slice_bitcast_fusion
  47.9 0.1 slice_reduce_fusion.2
  48.0 0.1 slice.47
  48.1 0.1 slice.51
  48.2 0.1 add.16
  48.2 0.1 slice.53
  48.3 17.8 %match_first.1.kept = f32[15360,768]{1,0:T(8,128)} custom-call(f32[16,264,128]{2,1,0:T(8,128)} %all-to-all-done.slots.group, f32[16,264,128]{2,1,0:T(8,128)} %all-to-all-done.slots.group, f32[2,8,384]{2,1,0:T(8,128)} %copy-done.2), custom_call_target="tpu_custom_call" | custom-call | flops 10000000000 | bytes 8000000 | tf_op jit(solution)/shard_map/match_first/pallas_call | solution.py:375
  66.1 5.8 %all-to-all-done.1.slots = f32[16,128,256]{2,1,0:T(8,128)S(1)} async-done(((f32[16,128,256]{2,1,0:T(8,128)}), f32[16,128,256]{2,1,0:T(8,128)S(1)}, u32[]{:S(2)}, u32[]{:S(2)}) %all-to-all-start.1) | async-done | bytes 2097184 | tf_op jit(solution)/shard_map/all_to_all | solution.py:652
  72.0 1.5 %place_second.1 = (f32[136,768]{1,0:T(8,128)S(1)}, f32[136,768]{1,0:T(8,128)S(1)}, f32[512,128]{1,0:T(8,128)S(1)}, f32[512,128]{1,0:T(8,128)S(1)}) custom-call(f32[15360,768]{1,0:T(8,128)} %match_first.1.kept, f32[8,256]{1,0:T(8,128)S(1)} %select_maximum_fusion.band.own, f32[16,128,256]{2,1,0:T(8,128)S(1)} %all-to-all-done.1.slots), custom_call_target="tpu_custom_call" | custom-call | tf_op jit(solution)/shard_map/place_second/pallas_call | solution.py:466
  73.5 0.1 collective-permute-start
  73.6 2.5 %collective-permute-start.1 = (f32[136,768]{1,0:T(8,128)S(1)}, f32[136,768]{1,0:T(8,128)S(1)}, u32[]{:S(2)}, u32[]{:S(2)}) collective-permute-start(f32[136,768]{1,0:T(8,128)S(1)} %get-tuple-element.13), channel_id=1, source_target_pairs={{1,2},{3,4},{5,6},{2,1},{4,3},{6,5},{9,10},{11,12},{13,14},{10,9},... | collective-permute-start | bytes 1253384 | tf_op jit(solution)/shard_map/ppermute | solution.py:526
  76.0 0.1 make_edges.2
  76.1 0.6 collective-permute-start.2
  76.8 4.9 %collective-permute-start.3 = (f32[384,128]{1,0:T(8,128)S(1)}, f32[384,128]{1,0:T(8,128)S(1)}, u32[]{:S(2)}, u32[]{:S(2)}) collective-permute-start(f32[384,128]{1,0:T(8,128)S(1)} %get-tuple-element.18), channel_id=1, source_target_pairs={{8,16},{24,32},{40,48},{56,64},{72,80},{88,96},{104,112},{16,8},{3... | collective-permute-start | bytes 589832 | tf_op jit(solution)/shard_map/ppermute | solution.py:526
  81.7 1.6 %make_middle.1.middle = f32[512,768]{1,0:T(8,128)S(1)} custom-call(f32[15360,768]{1,0:T(8,128)} %match_first.1.kept, f32[16,128,256]{2,1,0:T(8,128)S(1)} %all-to-all-done.1.slots), custom_call_target="tpu_custom_call" | custom-call | flops 400000 | bytes 4000000 | tf_op jit(solution)/shard_map/make_middle/pallas_call | solution.py:483
  83.3 0.3 collective-permute-start.4
  83.6 5.6 %collective-permute-start.5 = (f32[128,128]{1,0:T(8,128)S(1)}, f32[128,128]{1,0:T(8,128)S(1)}, u32[]{:S(2)}, u32[]{:S(2)}) collective-permute-start(f32[128,128]{1,0:T(8,128)S(1)} %get-tuple-element.20), channel_id=1, source_target_pairs={{8,16},{24,32},{40,48},{56,64},{72,80},{88,96},{104,112},{16,8},{3... | collective-permute-start | bytes 196616 | tf_op jit(solution)/shard_map/ppermute | solution.py:526
  89.2 2.1 %make_depth.1 = (f32[512,512]{1,0:T(8,128)}, f32[512,512]{1,0:T(8,128)S(1)}) custom-call(f32[8,256]{1,0:T(8,128)S(1)} %select_maximum_fusion.band.own, f32[136,768]{1,0:T(8,128)S(1)} %collective-permute-done.rows_next.rows, f32[136,768]{1,0:T(8,128)S(1)} %collective-permute-done.1.rows_last.rows), custom_call_target="tpu_custom_call" | custom-call | flops 1000000000 | bytes 1000000 | tf_op jit(solution)/shard_map/make_depth/pallas_call | solution.py:513
  91.3 0.9 make_inside.1.inside
  92.3 1.1 %make_coadd.1 = f32[512,512]{1,0:T(8,128)} custom-call(f32[512,512]{1,0:T(8,128)} %make_inside.1.inside, f32[512,768]{1,0:T(8,128)S(1)} %make_middle.1.middle, f32[136,768]{1,0:T(8,128)S(1)} %collective-permute-done.rows_next.rows, f32[136,768]{1,0:T(8,128)S(1)} %collective-permute-done.1.rows_last.rows, ...), custom_call_target="tpu_custom_call", output_to_operand_aliasing={{}: (0, {})} | custom-call | tf_op jit(solution)/shard_map/make_coadd/pallas_call | solution.py:630
  (28 shorter events, 0.1 us)
Async XLA Ops:
  3.6 10.3 %copy-start.9 = (f32[2,8,41]{2,1,0:T(8,128)S(1)}, f32[2,8,41]{2,1,0:T(8,128)}, u32[]{:S(2)}) copy-start(f32[2,8,41]{2,1,0:T(8,128)} %param.15) | copy-start | bytes 7876
  3.6 10.6 %copy-start = (f32[1,16,128,256]{3,2,1,0:T(8,128)S(1)}, f32[1,16,128,256]{3,2,1,0:T(8,128)}, u32[]{:S(2)}) copy-start(f32[1,16,128,256]{3,2,1,0:T(8,128)} %param.8) | copy-start | bytes 6291460
  3.6 10.6 %copy-start.3 = (f32[1,16,8]{1,2,0:T(8,128)S(1)}, f32[1,16,8]{1,2,0:T(8,128)}, u32[]{:S(2)}) copy-start(f32[1,16,8]{1,2,0:T(8,128)} %param.14) | copy-start | bytes 1540
  3.6 10.6 %copy-start.5 = (s32[1,16]{1,0:T(1,128)S(1)}, s32[1,16]{1,0:T(1,128)}, u32[]{:S(2)}) copy-start(s32[1,16]{1,0:T(1,128)} %row_offset.1) | copy-start | bytes 196
  3.6 10.6 %copy-start.6 = (s32[1,16]{1,0:T(1,128)S(1)}, s32[1,16]{1,0:T(1,128)}, u32[]{:S(2)}) copy-start(s32[1,16]{1,0:T(1,128)} %col_offset.1) | copy-start | bytes 196
  3.6 10.6 %copy-start.7 = (s32[1,16]{1,0:T(1,128)S(1)}, s32[1,16]{1,0:T(1,128)}, u32[]{:S(2)}) copy-start(s32[1,16]{1,0:T(1,128)} %live.1) | copy-start | bytes 196
  3.6 10.6 %copy-start.8 = (f32[1,16]{1,0:T(1,128)S(1)}, f32[1,16]{1,0:T(1,128)}, u32[]{:S(2)}) copy-start(f32[1,16]{1,0:T(1,128)} %weight.1) | copy-start | bytes 196
  3.7 36.5 %all-to-all-start = ((f32[16,264,128]{2,1,0:T(8,128)}), f32[16,264,128]{2,1,0:T(8,128)}, u32[]{:S(2)}, u32[]{:S(2)}) async-start(f32[16,264,128]{2,1,0:T(8,128)} %pack.1), calls=%async_computation | async-start | bytes 4325376 | tf_op jit(solution)/shard_map/all_to_all | solution.py:648
  14.2 0.7 copy-start.4
  14.9 4.3 %copy-start.2 = (f32[2,8,384]{2,1,0:T(8,128)}, f32[2,8,384]{2,1,0:T(8,128)S(1)}, u32[]{:S(2)}) copy-start(f32[2,8,384]{2,1,0:T(8,128)S(1)} %fusion.taps) | copy-start | bytes 73732
  19.2 1.3 %copy-start.1 = (f32[16,128,256]{2,1,0:T(8,128)}, f32[16,128,256]{2,1,0:T(8,128)S(1)}, u32[]{:S(2)}) copy-start(f32[16,128,256]{2,1,0:T(8,128)S(1)} %match_second.1) | copy-start | bytes 6291460
  40.1 31.8 %all-to-all-start.1 = ((f32[16,128,256]{2,1,0:T(8,128)}), f32[16,128,256]{2,1,0:T(8,128)S(1)}, u32[]{:S(2)}, u32[]{:S(2)}) async-start(f32[16,128,256]{2,1,0:T(8,128)} %copy-done.1), calls=%async_computation.1 | async-start | bytes 4194304 | tf_op jit(solution)/shard_map/all_to_all | solution.py:652
  73.5 2.6 %collective-permute-start = (f32[136,768]{1,0:T(8,128)S(1)}, f32[136,768]{1,0:T(8,128)S(1)}, u32[]{:S(2)}, u32[]{:S(2)}) collective-permute-start(f32[136,768]{1,0:T(8,128)S(1)} %get-tuple-element.12), channel_id=1, source_target_pairs={{0,1},{2,3},{4,5},{6,7},{1,0},{3,2},{5,4},{7,6},{8,9},{10,11},{12,... | collective-permute-start | bytes 1253384 | tf_op jit(solution)/shard_map/ppermute | solution.py:526
  73.6 9.7 %collective-permute-start.1 = (f32[136,768]{1,0:T(8,128)S(1)}, f32[136,768]{1,0:T(8,128)S(1)}, u32[]{:S(2)}, u32[]{:S(2)}) collective-permute-start(f32[136,768]{1,0:T(8,128)S(1)} %get-tuple-element.13), channel_id=1, source_target_pairs={{1,2},{3,4},{5,6},{2,1},{4,3},{6,5},{9,10},{11,12},{13,14},{10,9},... | collective-permute-start | bytes 1253384 | tf_op jit(solution)/shard_map/ppermute | solution.py:526
  76.1 16.1 %collective-permute-start.2 = (f32[384,128]{1,0:T(8,128)S(1)}, f32[384,128]{1,0:T(8,128)S(1)}, u32[]{:S(2)}, u32[]{:S(2)}) collective-permute-start(f32[384,128]{1,0:T(8,128)S(1)} %get-tuple-element.17), channel_id=1, source_target_pairs={{0,8},{16,24},{32,40},{48,56},{64,72},{80,88},{96,104},{112,120},{... | collective-permute-start | bytes 589832 | tf_op jit(solution)/shard_map/ppermute | solution.py:526
  76.8 15.5 %collective-permute-start.3 = (f32[384,128]{1,0:T(8,128)S(1)}, f32[384,128]{1,0:T(8,128)S(1)}, u32[]{:S(2)}, u32[]{:S(2)}) collective-permute-start(f32[384,128]{1,0:T(8,128)S(1)} %get-tuple-element.18), channel_id=1, source_target_pairs={{8,16},{24,32},{40,48},{56,64},{72,80},{88,96},{104,112},{16,8},{3... | collective-permute-start | bytes 589832 | tf_op jit(solution)/shard_map/ppermute | solution.py:526
  83.3 8.9 %collective-permute-start.4 = (f32[128,128]{1,0:T(8,128)S(1)}, f32[128,128]{1,0:T(8,128)S(1)}, u32[]{:S(2)}, u32[]{:S(2)}) collective-permute-start(f32[128,128]{1,0:T(8,128)S(1)} %get-tuple-element.19), channel_id=1, source_target_pairs={{0,8},{16,24},{32,40},{48,56},{64,72},{80,88},{96,104},{112,120},{... | collective-permute-start | bytes 196616 | tf_op jit(solution)/shard_map/ppermute | solution.py:526
  83.6 8.6 %collective-permute-start.5 = (f32[128,128]{1,0:T(8,128)S(1)}, f32[128,128]{1,0:T(8,128)S(1)}, u32[]{:S(2)}, u32[]{:S(2)}) collective-permute-start(f32[128,128]{1,0:T(8,128)S(1)} %get-tuple-element.20), channel_id=1, source_target_pairs={{8,16},{24,32},{40,48},{56,64},{72,80},{88,96},{104,112},{16,8},{3... | collective-permute-start | bytes 196616 | tf_op jit(solution)/shard_map/ppermute | solution.py:526

commit v9 on v7

--- a/solution.py
+++ b/solution.py
@@ -111,8 +111,7 @@
         brings.append(pltpu.make_async_copy(patches.at[part], held.at[part], in_sems.at[n]))
         brings[-1].start()
     meta[...] = jnp.zeros_like(meta)
-    for copy in small:
-        copy.wait()
+    small[0].wait()
 
     assign_slots(dest, slots)
     for k in range(count):
@@ -125,6 +124,8 @@
             give(k, t, 0).start()
             give(k, t, 1).start()
 
+    for copy in small[1:]:
+        copy.wait()
     for row, values in enumerate(vectors):
         line = values[...].astype(f32)
         for t in range(tiles):

time: 94.1 us -> 94 us (level)
  transfers between devices with their start and end apart: 8 -> 8, of which waited for: 3 -> 3; matrix products, arithmetic and copies ran while one was open for 2% -> 2% of each run, Pallas kernels for 31% -> 30%
where the time goes in v9:
time: 94 us; the launch traced here: 93.8 us
  Pallas kernels  34 us (36%)
  starting transfers between devices  29.4 us (31%)
  waiting for transfers between devices  25.9 us (28%)
  local copies, waits for them, and re-layouts  3.34 us (4%)
    all_to_all x1, waiting for transfers between devices, per_device(): lax.all_to_all(outgoing, 'skyx', split_axis=0, concat_axis=0, tiled=True)  19.7 us
    pallas_call x1, Pallas kernels, match_first(): pl.pallas_call(first_kernel, out_shape=jax.ShapeDtypeStruct((KEPT_ROWS, S...  17.8 us
    ppermute x6, starting transfers between devices, exchange(): return lax.ppermute(block, axis, pairs + [(j, i) for i, j in pairs])  14 us
    all_to_all x1, starting transfers between devices, per_device(): lax.all_to_all(outgoing, 'skyx', split_axis=0, concat_axis=0, tiled=True)  8.46 us
    all_to_all x1, starting transfers between devices, per_device(): late = lax.all_to_all(late, 'skyx', split_axis=0, concat_axis=0, tiled=True)  6.92 us
    all_to_all x1, waiting for transfers between devices, per_device(): late = lax.all_to_all(late, 'skyx', split_axis=0, concat_axis=0, tiled=True)  5.8 us
    pallas_call x1, Pallas kernels, match_second(): pl.pallas_call(second_kernel, out_shape=jax.ShapeDtypeStruct((tiles, PH,...  4.25 us
    pallas_call x1, Pallas kernels, pack(): pl.pallas_call(pack_kernel, out_shape=jax.ShapeDtypeStruct((tiles, SLOT +...  2.99 us
  transfers between devices with their start and end apart: 8, of which 3 were waited for; matrix products, arithmetic and copies ran while one was open for 2% of the time, Pallas kernels for 30%

profile of v9, /device:TPU:10, one launch (start us, length us, event | category | flops | bytes accessed | tf_op | source)
XLA Modules:
  0.0 93.8 jit_solution(18329121104798007325)
XLA Ops:
  0.6 3.0 %pack.1 = f32[16,264,128]{2,1,0:T(8,128)} custom-call(s32[1,16]{1,0:T(1,128)} %bitcast.16, s32[1,16]{1,0:T(1,128)} %row_offset.1, s32[1,16]{1,0:T(1,128)} %col_offset.1, s32[1,16]{1,0:T(1,128)} %live.1, f32[1,16]{1,0:T(1,128)} %weight.1, f32[8,16]{1,0:T(8,128)} %bitcast.12, f32[16,128,256]{2,1,0:T(8,128)} %bitcast.10), custom_call_target="tpu_custom_call" | custom-call | tf_op jit(solution)/shard_map/pack/pallas_call | solution.py:172
  3.7 8.5 %all-to-all-start = ((f32[16,264,128]{2,1,0:T(8,128)}), f32[16,264,128]{2,1,0:T(8,128)}, u32[]{:S(2)}, u32[]{:S(2)}) async-start(f32[16,264,128]{2,1,0:T(8,128)} %pack.1), calls=%async_computation | async-start | bytes 4325376 | tf_op jit(solution)/shard_map/all_to_all | solution.py:644
  12.2 1.7 %list_second.1.second = s32[3,16]{1,0:T(4,128)} custom-call(s32[1,16]{1,0:T(1,128)} %bitcast.17), custom_call_target="tpu_custom_call" | custom-call | tf_op jit(solution)/shard_map/list_second/pallas_call | solution.py:224
  13.9 0.1 rev.3
  14.0 0.1 pad.10.clone
  14.1 0.1 slice_maximum_fusion
  14.1 0.1 fusion.taps
  14.3 0.7 copy-done.4
  15.0 4.3 %match_second.1 = f32[16,128,256]{2,1,0:T(8,128)S(1)} custom-call(s32[3,16]{1,0:T(4,128)S(1)} %copy-done.4, f32[8,16]{1,0:T(8,128)S(1)} %bitcast.13, s32[1,16]{1,0:T(1,128)S(1)} %copy-done.7, f32[1,16]{1,0:T(1,128)S(1)} %copy-done.8, s32[1,16]{1,0:T(1,128)S(1)} %copy-done.5, s32[1,16]{1,0:T(1,128)S(1)} %copy-done.6, f32[16,128,256]{2,1,0:T(8,128)S(1)} %bitcast.11, ...), custom_call_target="tpu_custom_call" | custom-call | flops 5000000000 | bytes 6000000 | tf_op jit(solution)/shard_map/match_second/pallas_call | solution.py:276
  19.2 1.3 %copy-done.1 = f32[16,128,256]{2,1,0:T(8,128)} copy-done((f32[16,128,256]{2,1,0:T(8,128)}, f32[16,128,256]{2,1,0:T(8,128)S(1)}, u32[]{:S(2)}) %copy-start.1) | copy-done | bytes 2097176
  20.5 19.7 %all-to-all-done.slots.group = f32[16,264,128]{2,1,0:T(8,128)} async-done(((f32[16,264,128]{2,1,0:T(8,128)}), f32[16,264,128]{2,1,0:T(8,128)}, u32[]{:S(2)}, u32[]{:S(2)}) %all-to-all-start) | async-done | bytes 2162720 | tf_op jit(solution)/shard_map/all_to_all | solution.py:644
  40.2 6.9 %all-to-all-start.1 = ((f32[16,128,256]{2,1,0:T(8,128)}), f32[16,128,256]{2,1,0:T(8,128)S(1)}, u32[]{:S(2)}, u32[]{:S(2)}) async-start(f32[16,128,256]{2,1,0:T(8,128)} %copy-done.1), calls=%async_computation.1 | async-start | bytes 4194304 | tf_op jit(solution)/shard_map/all_to_all | solution.py:648
  47.1 0.8 slice_bitcast_fusion
  48.0 0.1 slice_reduce_fusion.2
  48.1 0.1 slice.47
  48.1 0.1 slice.51
  48.2 0.1 add.16
  48.3 0.1 slice.53
  48.4 17.8 %match_first.1.kept = f32[15360,768]{1,0:T(8,128)} custom-call(f32[16,264,128]{2,1,0:T(8,128)} %all-to-all-done.slots.group, f32[16,264,128]{2,1,0:T(8,128)} %all-to-all-done.slots.group, f32[2,8,384]{2,1,0:T(8,128)} %copy-done.2), custom_call_target="tpu_custom_call" | custom-call | flops 10000000000 | bytes 8000000 | tf_op jit(solution)/shard_map/match_first/pallas_call | solution.py:376
  66.2 5.8 %all-to-all-done.1.slots = f32[16,128,256]{2,1,0:T(8,128)S(1)} async-done(((f32[16,128,256]{2,1,0:T(8,128)}), f32[16,128,256]{2,1,0:T(8,128)S(1)}, u32[]{:S(2)}, u32[]{:S(2)}) %all-to-all-start.1) | async-done | bytes 2097184 | tf_op jit(solution)/shard_map/all_to_all | solution.py:648
  72.0 1.5 %place_second.1 = (f32[136,768]{1,0:T(8,128)S(1)}, f32[136,768]{1,0:T(8,128)S(1)}, f32[512,128]{1,0:T(8,128)S(1)}, f32[512,128]{1,0:T(8,128)S(1)}) custom-call(f32[15360,768]{1,0:T(8,128)} %match_first.1.kept, f32[8,256]{1,0:T(8,128)S(1)} %select_maximum_fusion.band.own, f32[16,128,256]{2,1,0:T(8,128)S(1)} %all-to-all-done.1.slots), custom_call_target="tpu_custom_call" | custom-call | tf_op jit(solution)/shard_map/place_second/pallas_call | solution.py:462
  73.5 0.1 collective-permute-start
  73.5 2.5 %collective-permute-start.1 = (f32[136,768]{1,0:T(8,128)S(1)}, f32[136,768]{1,0:T(8,128)S(1)}, u32[]{:S(2)}, u32[]{:S(2)}) collective-permute-start(f32[136,768]{1,0:T(8,128)S(1)} %get-tuple-element.13), channel_id=1, source_target_pairs={{1,2},{3,4},{5,6},{2,1},{4,3},{6,5},{9,10},{11,12},{13,14},{10,9},... | collective-permute-start | bytes 1253384 | tf_op jit(solution)/shard_map/ppermute | solution.py:522
  76.1 0.6 collective-permute-start.2
  76.8 5.6 %collective-permute-start.3 = (f32[384,128]{1,0:T(8,128)S(1)}, f32[384,128]{1,0:T(8,128)S(1)}, u32[]{:S(2)}, u32[]{:S(2)}) collective-permute-start(f32[384,128]{1,0:T(8,128)S(1)} %get-tuple-element.18), channel_id=1, source_target_pairs={{8,16},{24,32},{40,48},{56,64},{72,80},{88,96},{104,112},{16,8},{3... | collective-permute-start | bytes 589832 | tf_op jit(solution)/shard_map/ppermute | solution.py:522
  82.4 1.6 %make_middle.1.middle = f32[512,768]{1,0:T(8,128)S(1)} custom-call(f32[15360,768]{1,0:T(8,128)} %match_first.1.kept, f32[16,128,256]{2,1,0:T(8,128)S(1)} %all-to-all-done.1.slots), custom_call_target="tpu_custom_call" | custom-call | flops 400000 | bytes 4000000 | tf_op jit(solution)/shard_map/make_middle/pallas_call | solution.py:479
  84.0 0.1 collective-permute-start.4
  84.1 5.1 %collective-permute-start.5 = (f32[128,128]{1,0:T(8,128)S(1)}, f32[128,128]{1,0:T(8,128)S(1)}, u32[]{:S(2)}, u32[]{:S(2)}) collective-permute-start(f32[128,128]{1,0:T(8,128)S(1)} %get-tuple-element.20), channel_id=1, source_target_pairs={{8,16},{24,32},{40,48},{56,64},{72,80},{88,96},{104,112},{16,8},{3... | collective-permute-start | bytes 196616 | tf_op jit(solution)/shard_map/ppermute | solution.py:522
  89.2 2.1 %make_depth.1 = (f32[512,512]{1,0:T(8,128)}, f32[512,512]{1,0:T(8,128)S(1)}) custom-call(f32[8,256]{1,0:T(8,128)S(1)} %select_maximum_fusion.band.own, f32[136,768]{1,0:T(8,128)S(1)} %collective-permute-done.rows_next.rows, f32[136,768]{1,0:T(8,128)S(1)} %collective-permute-done.1.rows_last.rows), custom_call_target="tpu_custom_call" | custom-call | flops 1000000000 | bytes 1000000 | tf_op jit(solution)/shard_map/make_depth/pallas_call | solution.py:509
  91.3 0.9 make_inside.1.inside
  92.3 0.4 collective-permute-done.5.far_last
  92.7 1.1 %make_coadd.1 = f32[512,512]{1,0:T(8,128)} custom-call(f32[512,512]{1,0:T(8,128)} %make_inside.1.inside, f32[512,768]{1,0:T(8,128)S(1)} %make_middle.1.middle, f32[136,768]{1,0:T(8,128)S(1)} %collective-permute-done.rows_next.rows, f32[136,768]{1,0:T(8,128)S(1)} %collective-permute-done.1.rows_last.rows, ...), custom_call_target="tpu_custom_call", output_to_operand_aliasing={{}: (0, {})} | custom-call | tf_op jit(solution)/shard_map/make_coadd/pallas_call | solution.py:626
  (28 shorter events, 0.2 us)
Async XLA Ops:
  3.6 10.3 %copy-start.9 = (f32[2,8,41]{2,1,0:T(8,128)S(1)}, f32[2,8,41]{2,1,0:T(8,128)}, u32[]{:S(2)}) copy-start(f32[2,8,41]{2,1,0:T(8,128)} %param.15) | copy-start | bytes 7876
  3.6 10.6 %copy-start = (f32[1,16,128,256]{3,2,1,0:T(8,128)S(1)}, f32[1,16,128,256]{3,2,1,0:T(8,128)}, u32[]{:S(2)}) copy-start(f32[1,16,128,256]{3,2,1,0:T(8,128)} %param.8) | copy-start | bytes 6291460
  3.7 10.6 %copy-start.3 = (f32[1,16,8]{1,2,0:T(8,128)S(1)}, f32[1,16,8]{1,2,0:T(8,128)}, u32[]{:S(2)}) copy-start(f32[1,16,8]{1,2,0:T(8,128)} %param.14) | copy-start | bytes 1540
  3.7 10.6 %copy-start.5 = (s32[1,16]{1,0:T(1,128)S(1)}, s32[1,16]{1,0:T(1,128)}, u32[]{:S(2)}) copy-start(s32[1,16]{1,0:T(1,128)} %row_offset.1) | copy-start | bytes 196
  3.7 10.6 %copy-start.6 = (s32[1,16]{1,0:T(1,128)S(1)}, s32[1,16]{1,0:T(1,128)}, u32[]{:S(2)}) copy-start(s32[1,16]{1,0:T(1,128)} %col_offset.1) | copy-start | bytes 196
  3.7 10.6 %copy-start.7 = (s32[1,16]{1,0:T(1,128)S(1)}, s32[1,16]{1,0:T(1,128)}, u32[]{:S(2)}) copy-start(s32[1,16]{1,0:T(1,128)} %live.1) | copy-start | bytes 196
  3.7 10.6 %copy-start.8 = (f32[1,16]{1,0:T(1,128)S(1)}, f32[1,16]{1,0:T(1,128)}, u32[]{:S(2)}) copy-start(f32[1,16]{1,0:T(1,128)} %weight.1) | copy-start | bytes 196
  3.7 36.5 %all-to-all-start = ((f32[16,264,128]{2,1,0:T(8,128)}), f32[16,264,128]{2,1,0:T(8,128)}, u32[]{:S(2)}, u32[]{:S(2)}) async-start(f32[16,264,128]{2,1,0:T(8,128)} %pack.1), calls=%async_computation | async-start | bytes 4325376 | tf_op jit(solution)/shard_map/all_to_all | solution.py:644
  14.3 0.7 copy-start.4
  15.0 4.3 %copy-start.2 = (f32[2,8,384]{2,1,0:T(8,128)}, f32[2,8,384]{2,1,0:T(8,128)S(1)}, u32[]{:S(2)}) copy-start(f32[2,8,384]{2,1,0:T(8,128)S(1)} %fusion.taps) | copy-start | bytes 73732
  19.2 1.3 %copy-start.1 = (f32[16,128,256]{2,1,0:T(8,128)}, f32[16,128,256]{2,1,0:T(8,128)S(1)}, u32[]{:S(2)}) copy-start(f32[16,128,256]{2,1,0:T(8,128)S(1)} %match_second.1) | copy-start | bytes 6291460
  40.2 31.8 %all-to-all-start.1 = ((f32[16,128,256]{2,1,0:T(8,128)}), f32[16,128,256]{2,1,0:T(8,128)S(1)}, u32[]{:S(2)}, u32[]{:S(2)}) async-start(f32[16,128,256]{2,1,0:T(8,128)} %copy-done.1), calls=%async_computation.1 | async-start | bytes 4194304 | tf_op jit(solution)/shard_map/all_to_all | solution.py:648
  73.5 2.6 %collective-permute-start = (f32[136,768]{1,0:T(8,128)S(1)}, f32[136,768]{1,0:T(8,128)S(1)}, u32[]{:S(2)}, u32[]{:S(2)}) collective-permute-start(f32[136,768]{1,0:T(8,128)S(1)} %get-tuple-element.12), channel_id=1, source_target_pairs={{0,1},{2,3},{4,5},{6,7},{1,0},{3,2},{5,4},{7,6},{8,9},{10,11},{12,... | collective-permute-start | bytes 1253384 | tf_op jit(solution)/shard_map/ppermute | solution.py:522
  73.5 10.4 %collective-permute-start.1 = (f32[136,768]{1,0:T(8,128)S(1)}, f32[136,768]{1,0:T(8,128)S(1)}, u32[]{:S(2)}, u32[]{:S(2)}) collective-permute-start(f32[136,768]{1,0:T(8,128)S(1)} %get-tuple-element.13), channel_id=1, source_target_pairs={{1,2},{3,4},{5,6},{2,1},{4,3},{6,5},{9,10},{11,12},{13,14},{10,9},... | collective-permute-start | bytes 1253384 | tf_op jit(solution)/shard_map/ppermute | solution.py:522
  76.1 16.6 %collective-permute-start.2 = (f32[384,128]{1,0:T(8,128)S(1)}, f32[384,128]{1,0:T(8,128)S(1)}, u32[]{:S(2)}, u32[]{:S(2)}) collective-permute-start(f32[384,128]{1,0:T(8,128)S(1)} %get-tuple-element.17), channel_id=1, source_target_pairs={{0,8},{16,24},{32,40},{48,56},{64,72},{80,88},{96,104},{112,120},{... | collective-permute-start | bytes 589832 | tf_op jit(solution)/shard_map/ppermute | solution.py:522
  76.8 15.9 %collective-permute-start.3 = (f32[384,128]{1,0:T(8,128)S(1)}, f32[384,128]{1,0:T(8,128)S(1)}, u32[]{:S(2)}, u32[]{:S(2)}) collective-permute-start(f32[384,128]{1,0:T(8,128)S(1)} %get-tuple-element.18), channel_id=1, source_target_pairs={{8,16},{24,32},{40,48},{56,64},{72,80},{88,96},{104,112},{16,8},{3... | collective-permute-start | bytes 589832 | tf_op jit(solution)/shard_map/ppermute | solution.py:522
  84.0 8.2 %collective-permute-start.4 = (f32[128,128]{1,0:T(8,128)S(1)}, f32[128,128]{1,0:T(8,128)S(1)}, u32[]{:S(2)}, u32[]{:S(2)}) collective-permute-start(f32[128,128]{1,0:T(8,128)S(1)} %get-tuple-element.19), channel_id=1, source_target_pairs={{0,8},{16,24},{32,40},{48,56},{64,72},{80,88},{96,104},{112,120},{... | collective-permute-start | bytes 196616 | tf_op jit(solution)/shard_map/ppermute | solution.py:522
  84.1 8.6 %collective-permute-start.5 = (f32[128,128]{1,0:T(8,128)S(1)}, f32[128,128]{1,0:T(8,128)S(1)}, u32[]{:S(2)}, u32[]{:S(2)}) collective-permute-start(f32[128,128]{1,0:T(8,128)S(1)} %get-tuple-element.20), channel_id=1, source_target_pairs={{8,16},{24,32},{40,48},{56,64},{72,80},{88,96},{104,112},{16,8},{3... | collective-permute-start | bytes 196616 | tf_op jit(solution)/shard_map/ppermute | solution.py:522
